TPU v7x, 32 devices: a whole 2x2x4 slice. The times are simulated.
32 devices in a mesh: grp: 2 (over y), wa: 4 (over z), col: 2 (over x), row: 2 (over core).
Axes of the slice: x: 2, y: 2, z: 4, core: 2. Of those that a mesh axis runs over, the one named last changes fastest.
Arguments:
- walkers: bfloat16 [64, 1024, 384], P(('grp', 'wa', 'col', 'row')), parts along dimension 0, may hold values from -2 to 2
- intersection_inverse: bfloat16 [64, 384, 384], P(('grp', 'wa', 'col', 'row')), parts along dimension 0, may hold values from -0.3125 to 0.3125
- noise_index: int32 [64, 64], P(('grp', 'wa', 'col', 'row')), parts along dimension 0, may hold values from 0 to 65535
- cholesky: bfloat16 [64, 1024, 1024], P(None, ('wa', 'col')), may hold values from -0.21875 to 0.21875
Outputs:
- walkers_new: bfloat16 [64, 1024, 384], P(('grp', 'wa', 'col', 'row')), parts along dimension 0
- log_weight: float32 [64], P(('grp', 'wa', 'col', 'row')), parts along dimension 0
There are 2 independent parts, one for each index of `grp`. A program takes and returns all parts, laid end to end along the dimension named above; an argument that names none is the same for every part. Nothing has to cross between parts.
All inputs are finite; a program needn't handle non-finite values.
Results may differ from a plain program's by a relative error of at most 0.006.
Values may be sent and summed in bfloat16 or wider, within the bound.
No kernel may reach another device: no remote copies, remote signals or barrier semaphores. Data moves between devices by JAX's collectives and lax.ppermute only.
A program may use at most 128 MiB of HBM per device.

v0:
```python
import jax
import jax.numpy as jnp
from jax import lax
from jax.sharding import PartitionSpec as P

NOISE_LEVELS = 65536


STEP_ROOT = 0.1
BIAS_CAP = 1.0
ROOT_TWO = 1.4142135623730951


def force_terms(green_tiles, half_tile):
    return jnp.einsum("ksf,gf->ksg", green_tiles, half_tile, preferred_element_type=jnp.float32)


def shift_field(bias_sum, code_block):
    force_bias = jnp.clip(STEP_ROOT * bias_sum, -BIAS_CAP, BIAS_CAP)
    level = (code_block.astype(jnp.float32) + 0.5) / NOISE_LEVELS
    noise = ROOT_TWO * lax.erf_inv(2.0 * level - 1.0)
    shifted = noise - force_bias
    log_step = jnp.sum(shifted * force_bias - 0.5 * force_bias * force_bias, axis=-1)
    return (shifted.astype(jnp.bfloat16), log_step)


def per_device(walkers, intersection_inverse, noise_index, cholesky):
    walker_count = walkers.shape[0]
    orbitals = walkers.shape[1]
    electrons = walkers.shape[2]
    vectors = cholesky.shape[0]
    tile_rows = cholesky.shape[1]
    along_wa = lax.axis_size("wa")
    along_col = lax.axis_size("col")
    planes = along_wa * along_col
    green_half = jnp.einsum(
        "kpe,kef->kpf", walkers, intersection_inverse, preferred_element_type=jnp.float32
    ).astype(jnp.bfloat16)
    packed = green_half.reshape(walker_count, planes, tile_rows * electrons)
    half_tile = cholesky[:, :, :electrons].reshape(vectors, tile_rows * electrons)
    partial_sums = force_terms(
        lax.all_to_all(packed, ("wa", "col"), split_axis=1, concat_axis=1, tiled=True), half_tile
    )
    bias_sum = lax.psum(partial_sums, ("wa", "col"))
    gathered = lax.all_gather(noise_index, ("wa", "col"), axis=0, tiled=True)
    gathered = jnp.transpose(gathered.reshape(planes, walker_count, vectors), (1, 0, 2))
    field, log_all = shift_field(bias_sum, gathered)
    log_weight = lax.dynamic_slice_in_dim(log_all, lax.axis_index(("wa", "col")), 1, 1)[:, 0]
    full_tile = cholesky.reshape(vectors, tile_rows * orbitals)
    tiles_out = jnp.einsum(
        "ksg,gf->ksf", field, full_tile, preferred_element_type=jnp.float32
    ).astype(jnp.bfloat16)
    returned = lax.all_to_all(tiles_out, ("wa", "col"), split_axis=1, concat_axis=1, tiled=True)
    potential = returned.reshape(walker_count, orbitals, orbitals)
    running = walkers.astype(jnp.float32)
    factor_term = walkers
    for degree in range(1, 5):
        product = (
            -STEP_ROOT
            / degree
            * jnp.einsum("kpq,kqe->kpe", potential, factor_term, preferred_element_type=jnp.float32)
        )
        running = running + product
        factor_term = product.astype(jnp.bfloat16)
    return (running.astype(jnp.bfloat16), log_weight)


def solution(mesh):
    placed = (
        P(("grp", "wa", "col", "row"), None, None),
        P(("grp", "wa", "col", "row"), None, None),
        P(("grp", "wa", "col", "row"), None),
        P(None, ("wa", "col"), None),
    )
    return jax.shard_map(
        per_device,
        mesh=mesh,
        in_specs=placed,
        out_specs=(P(("grp", "wa", "col", "row"), None, None), P(("grp", "wa", "col", "row"))),
        check_vma=False,
    )
```

profile of v0, /device:TPU:8, one launch (start us, length us, event | category | flops | bytes accessed | tf_op | source)
XLA Modules:
  0.0 218.8 jit_solution(10613116380865848635)
XLA Ops:
  0.6 0.0 copy-start
  0.6 1.1 copy-done
  1.7 3.7 %convolution_convert_fusion.1 = bf16[2,1024,384]{2,1,0:T(8,128)(2,1)} fusion(bf16[2,1024,384]{2,1,0:T(8,128)(2,1)} %param.4, bf16[2,384,384]{2,1,0:T(8,128)(2,1)S(1)} %copy-done), kind=kOutput, calls=%fused_computation.5 | convolution fusion | flops 604766208 | bytes 3735552 | tf_op jit(solution)/shard_map/kpe,kef->kpf/dot_general | solution.py:36
  5.4 1.9 reshape.22
  7.3 2.8 %copy.13 = bf16[2,8,49152]{2,0,1:T(2,128)(2,1)} copy(bf16[2,8,49152]{2,1,0:T(8,128)(2,1)S(1)} %reshape.22) | data formatting | bytes 3145728 | tf_op jit(solution)/shard_map/reshape | solution.py:39
  10.0 6.3 %all-to-all-start = ((bf16[2,8,49152]{2,0,1:T(2,128)(2,1)}), bf16[2,8,49152]{2,0,1:T(2,128)(2,1)S(1)}, u32[]{:S(2)}, u32[]{:S(2)}) async-start(bf16[2,8,49152]{2,0,1:T(2,128)(2,1)} %copy.13), calls=%async_computation | async-start | bytes 3145728 | tf_op jit(solution)/shard_map/all_to_all | solution.py:42
  16.3 6.6 %slice.3 = bf16[64,128,384]{2,1,0:T(8,128)(2,1)} slice(bf16[64,128,1024]{2,1,0:T(8,128)(2,1)} %param.7), slice={[0:64], [0:128], [0:384]} | slice | bytes 12582912 | tf_op jit(solution)/shard_map/slice | solution.py:40
  22.9 17.0 %reshape.39 = bf16[64,131072,1]{1,0,2:T(8,128)(2,1)} reshape(bf16[64,128,1024]{2,1,0:T(8,128)(2,1)} %param.7) | data formatting | bytes 33554432 | tf_op jit(solution)/shard_map/reshape | solution.py:49
  39.9 0.0 copy-start.4
  39.9 9.0 %reshape.38 = bf16[64,49152,1]{1,0,2:T(8,128)(2,1)} reshape(bf16[64,128,384]{2,1,0:T(8,128)(2,1)} %slice.3) | data formatting | bytes 12582912 | tf_op jit(solution)/shard_map/reshape | solution.py:40
  48.9 0.0 copy-done.4
  48.9 17.7 %all-gather = s32[8,2,64]{2,1,0:T(2,128)S(1)} all-gather(s32[1,2,64]{2,1,0:T(2,128)S(1)} %bitcast.38), channel_id=1, replica_groups=mesh['grp'=2,'wa'=4,'col'=2,'row'=2] {'wa','col'}, dimensions={0}, use_global_device_ids=true | all-gather | bytes 4608 | tf_op jit(solution)/shard_map/all_gather | solution.py:45
  66.6 0.0 all-to-all-done
  66.6 4.5 %fusion.2 = f32[2,8,64]{2,1,0:T(8,128)S(1)} fusion(bf16[64,49152,1]{1,0,2:T(8,128)(2,1)} %reshape.38, bf16[2,8,49152]{2,0,1:T(2,128)(2,1)S(1)} %all-to-all-done), kind=kOutput, calls=%fused_computation.8 | convolution fusion | flops 100663296 | bytes 7868416 | tf_op jit(solution)/shard_map/ksf,gf->ksg/dot_general | solution.py:15
  71.1 17.6 %psum.7 = f32[2,8,64]{2,1,0:T(8,128)S(1)} all-reduce(f32[2,8,64]{2,1,0:T(8,128)S(1)} %fusion.2), channel_id=1, replica_groups=mesh['grp'=2,'wa'=4,'col'=2,'row'=2] {'wa','col'}, use_global_device_ids=true, to_apply=%region_0.0 | all-reduce | flops 1024 | bytes 8192 | tf_op jit(solution)/shard_map/psum | solution.py:44
  88.8 8.1 %convolution_convert_fusion = bf16[2,8,131072]{2,1,0:T(8,128)(2,1)S(1)} fusion(bf16[64,131072,1]{1,0,2:T(8,128)(2,1)} %reshape.39, s32[8,2,64]{2,1,0:T(2,128)S(1)} %all-gather, f32[2,8,64]{2,1,0:T(8,128)S(1)} %psum.7), kind=kOutput, calls=%fused_computation | convolution fusion | flops 270579712 | bytes 20979712 | tf_op jit(solution)/shard_map/ksg,gf->ksf/dot_general | solution.py:50
  96.9 6.3 %copy.15 = bf16[2,8,131072]{2,0,1:T(2,128)(2,1)} copy(bf16[2,8,131072]{2,1,0:T(8,128)(2,1)S(1)} %convolution_convert_fusion) | data formatting | bytes 8388608 | tf_op jit(solution)/shard_map/convert_element_type | solution.py:52
  103.1 7.7 %all-to-all-start.1 = ((bf16[2,8,131072]{2,0,1:T(2,128)(2,1)}), bf16[2,8,131072]{2,0,1:T(2,128)(2,1)}, u32[]{:S(2)}, u32[]{:S(2)}) async-start(bf16[2,8,131072]{2,0,1:T(2,128)(2,1)} %copy.15), calls=%async_computation.1 | async-start | bytes 8388608 | tf_op jit(solution)/shard_map/all_to_all | solution.py:53
  110.8 0.1 fusion.10
  111.0 0.7 dynamic-slice_reduce_fusion
  111.7 82.5 %all-to-all-done.1 = bf16[2,8,131072]{2,0,1:T(2,128)(2,1)} async-done(((bf16[2,8,131072]{2,0,1:T(2,128)(2,1)}), bf16[2,8,131072]{2,0,1:T(2,128)(2,1)}, u32[]{:S(2)}, u32[]{:S(2)}) %all-to-all-start.1) | async-done | bytes 4194336 | tf_op jit(solution)/shard_map/all_to_all | solution.py:53
  194.2 6.4 %copy.16 = bf16[2,8,131072]{2,1,0:T(8,128)(2,1)} copy(bf16[2,8,131072]{2,0,1:T(2,128)(2,1)} %all-to-all-done.1) | data formatting | bytes 8388608 | tf_op jit(solution)/shard_map/all_to_all | solution.py:53
  200.6 0.0 copy-start.3
  200.6 4.9 %reshape.25 = bf16[2,1024,1024]{2,1,0:T(8,128)(2,1)} reshape(bf16[2,8,131072]{2,1,0:T(8,128)(2,1)} %copy.16) | data formatting | bytes 8388608 | tf_op jit(solution)/shard_map/reshape | solution.py:54
  205.5 0.0 copy-done.3
  205.5 4.7 %fusion.24 = f32[2,1024,384]{2,1,0:T(8,128)S(1)} fusion(bf16[2,1024,1024]{2,1,0:T(8,128)(2,1)} %reshape.25, bf16[2,1024,384]{2,1,0:T(8,128)(2,1)S(1)} %copy-done.3), kind=kOutput, calls=%fused_computation.37 | convolution fusion | flops 1610612736 | bytes 8912896 | tf_op jit(solution)/shard_map/kpq,kqe->kpe/dot_general | solution.py:61
  210.2 0.0 copy-done.2
  210.2 2.3 %fusion = f32[2,1024,384]{2,1,0:T(8,128)S(1)} fusion(bf16[2,1024,1024]{2,1,0:T(8,128)(2,1)S(1)} %copy-done.2, f32[2,1024,384]{2,1,0:T(8,128)S(1)} %fusion.24), kind=kOutput, calls=%fused_computation.6 | convolution fusion | flops 1612185600 | bytes 10485760 | tf_op jit(solution)/shard_map/kpq,kqe->kpe/dot_general | solution.py:61
  212.6 2.3 %fusion.1 = f32[2,1024,384]{2,1,0:T(8,128)S(1)} fusion(bf16[2,1024,1024]{2,1,0:T(8,128)(2,1)S(1)} %copy-done.2, f32[2,1024,384]{2,1,0:T(8,128)S(1)} %fusion), kind=kOutput, calls=%fused_computation.7 | convolution fusion | flops 1612185600 | bytes 10485760 | tf_op jit(solution)/shard_map/kpq,kqe->kpe/dot_general | solution.py:61
  214.9 0.0 copy-start.1
  214.9 3.9 %add_convert_fusion = bf16[2,1024,384]{2,1,0:T(8,128)(2,1)} fusion(bf16[2,1024,384]{2,1,0:T(8,128)(2,1)S(1)} %copy-done.3, f32[2,1024,384]{2,1,0:T(8,128)S(1)} %fusion.1, f32[2,1024,384]{2,1,0:T(8,128)S(1)} %fusion, f32[2,1024,384]{2,1,0:T(8,128)S(1)} %fusion.24, bf16[2,1024,1024]{2,1,0:T(8,128)(2,1)S(1)} %copy-done.2), kind=kOutput, calls=%fused_computation.1 | convolution fusion | flops 1620049920 | bytes 16777216 | tf_op jit(solution)/shard_map/kpq,kqe->kpe/dot_general | solution.py:61
  218.8 0.0 copy-done.1
  (1 shorter events, 0.0 us)
Async XLA Ops:
  0.6 1.1 copy-start
  10.0 56.6 %all-to-all-start = ((bf16[2,8,49152]{2,0,1:T(2,128)(2,1)}), bf16[2,8,49152]{2,0,1:T(2,128)(2,1)S(1)}, u32[]{:S(2)}, u32[]{:S(2)}) async-start(bf16[2,8,49152]{2,0,1:T(2,128)(2,1)} %copy.13), calls=%async_computation | async-start | bytes 3145728 | tf_op jit(solution)/shard_map/all_to_all | solution.py:42
  39.9 9.0 %copy-start.4 = (s32[2,64]{1,0:T(2,128)S(1)}, s32[2,64]{1,0:T(2,128)}, u32[]{:S(2)}) copy-start(s32[2,64]{1,0:T(2,128)} %param.6) | copy-start | bytes 1540
  103.1 91.0 %all-to-all-start.1 = ((bf16[2,8,131072]{2,0,1:T(2,128)(2,1)}), bf16[2,8,131072]{2,0,1:T(2,128)(2,1)}, u32[]{:S(2)}, u32[]{:S(2)}) async-start(bf16[2,8,131072]{2,0,1:T(2,128)(2,1)} %copy.15), calls=%async_computation.1 | async-start | bytes 8388608 | tf_op jit(solution)/shard_map/all_to_all | solution.py:53
  200.6 4.9 %copy-start.3 = (bf16[2,1024,384]{2,1,0:T(8,128)(2,1)S(1)}, bf16[2,1024,384]{2,1,0:T(8,128)(2,1)}, u32[]{:S(2)}) copy-start(bf16[2,1024,384]{2,1,0:T(8,128)(2,1)} %param.4) | copy-start | bytes 4718596
  205.5 4.7 %copy-start.2 = (bf16[2,1024,1024]{2,1,0:T(8,128)(2,1)S(1)}, bf16[2,1024,1024]{2,1,0:T(8,128)(2,1)}, u32[]{:S(2)}) copy-start(bf16[2,1024,1024]{2,1,0:T(8,128)(2,1)} %reshape.25) | copy-start | bytes 12582916
  214.9 3.9 %copy-start.1 = (bf16[2,384,384]{2,1,0:T(8,128)(2,1)S(1)}, bf16[2,384,384]{2,1,0:T(8,128)(2,1)}, u32[]{:S(2)}) copy-start(bf16[2,384,384]{2,1,0:T(8,128)(2,1)} %param.5) | copy-start | bytes 1769476
where the time goes:
time: 223 us; the launch traced here: 219 us
  waiting for transfers between devices  82.5 us (37%)
  local copies, waits for them, and re-layouts  56.7 us (25%)
  blocking collectives  35.3 us (16%)
  matrix products  29.5 us (13%)
  starting transfers between devices  13.9 us (6%)
    all_to_all x1, waiting for transfers between devices, per_device(): lax.all_to_all(tiles_out, ('wa', 'col'), split_axis=1, concat_axis=1, til...  82.5 us
    all_gather x1, blocking collectives, per_device(): gathered = lax.all_gather(noise_index, ('wa', 'col'), axis=0, tiled=True)  17.7 us
    psum x1, blocking collectives, per_device(): bias_sum = lax.psum(partial_sums, ('wa', 'col'))  17.6 us
    reshape x1, local copies, waits for them, and re-layouts, per_device(): full_tile = cholesky.reshape(vectors, tile_rows * orbitals)  17 us
    dot_general x4, matrix products, per_device(): jnp.einsum('kpq,kqe->kpe', potential, factor_term, preferred_element_type...  13.2 us
    reshape x1, local copies, waits for them, and re-layouts, per_device(): cholesky[:, :, :electrons].reshape(vectors, tile_rows * electrons)  8.98 us
    dot_general x1, matrix products, per_device(): jnp.einsum('ksg,gf->ksf', field, full_tile, preferred_element_type=jnp.fl...  8.09 us
    all_to_all x1, starting transfers between devices, per_device(): lax.all_to_all(tiles_out, ('wa', 'col'), split_axis=1, concat_axis=1, til...  7.68 us
  transfers between devices with their start and end apart: 2, of which 1 were waited for; matrix products, arithmetic and copies ran while one was open for 15% of the time, Pallas kernels for 0%

commit v1 on v0

v1 whole, which is shorter than its diff:
```python
import functools

import jax
import jax.numpy as jnp
from jax import lax
from jax.experimental import pallas as pl
from jax.experimental.pallas import tpu as pltpu
from jax.sharding import PartitionSpec as P

NOISE_LEVELS = 65536


STEP_ROOT = 0.1
BIAS_CAP = 1.0
ROOT_TWO = 1.4142135623730951
DEGREES = 4
PLANE = ("wa", "col")
ROWS = 16
VMEM = 48 * 1024 * 1024


def bias_kernel(chol_ref, green_ref, out_ref, acc_ref):
    step = pl.program_id(0)
    vectors, rows, electrons = chol_ref.shape
    count = green_ref.shape[0]
    pairs = lax.dot_general(
        chol_ref[...].reshape(vectors * rows, electrons),
        green_ref[...].reshape(count * rows, electrons),
        (((1,), (1,)), ((), ())),
        preferred_element_type=jnp.float32,
    )

    @pl.when(step == 0)
    def _():
        acc_ref[...] = pairs

    @pl.when(step > 0)
    def _():
        acc_ref[...] += pairs

    @pl.when(step == pl.num_programs(0) - 1)
    def _():
        total = acc_ref[...].reshape(vectors, rows, count * rows)
        own = lax.broadcasted_iota(jnp.int32, total.shape, 1)
        other = lax.broadcasted_iota(jnp.int32, total.shape, 2) % rows
        summed = jnp.sum(jnp.where(own == other, total, 0.0), axis=1)
        fold_at = lax.broadcasted_iota(jnp.int32, (count, count * rows), 1) // rows
        fold = (fold_at == lax.broadcasted_iota(jnp.int32, (count, count * rows), 0)).astype(jnp.float32)
        out_ref[...] = lax.dot_general(
            fold,
            summed,
            (((1,), (1,)), ((), ())),
            preferred_element_type=jnp.float32,
            precision=lax.Precision.HIGHEST,
        )


def partial_bias(cholesky, green):
    vectors, tile_rows, _ = cholesky.shape
    count, _, electrons = green.shape
    if tile_rows % ROWS:
        return jnp.einsum("gpe,kpe->kg", cholesky[:, :, :electrons], green, preferred_element_type=jnp.float32)
    return pl.pallas_call(
        bias_kernel,
        grid=(tile_rows // ROWS,),
        in_specs=[
            pl.BlockSpec((vectors, ROWS, electrons), lambda t: (0, t, 0)),
            pl.BlockSpec((count, ROWS, electrons), lambda t: (0, t, 0)),
        ],
        out_specs=pl.BlockSpec((count, vectors), lambda t: (0, 0)),
        out_shape=jax.ShapeDtypeStruct((count, vectors), jnp.float32),
        scratch_shapes=[pltpu.VMEM((vectors * ROWS, count * ROWS), jnp.float32)],
        compiler_params=pltpu.CompilerParams(vmem_limit_bytes=VMEM),
        cost_estimate=pl.CostEstimate(
            flops=2 * vectors * ROWS * count * tile_rows * electrons,
            bytes_accessed=2 * (vectors + count) * tile_rows * electrons,
            transcendentals=0,
        ),
        name="bias_sum",
    )(cholesky, green)


def shifted_field(sums, noise):
    force_bias = jnp.clip(STEP_ROOT * jnp.sum(sums, axis=0), -BIAS_CAP, BIAS_CAP)
    return noise - force_bias, force_bias


def potential_kernel(sums_ref, noise_ref, chol_ref, out_ref, spread_ref):
    vectors, rows, orbitals = chol_ref.shape
    count = noise_ref.shape[0]

    @pl.when(pl.program_id(0) == 0)
    def _():
        shifted, _ = shifted_field(sums_ref[...], noise_ref[...])
        field = shifted.astype(jnp.bfloat16)
        widen_at = lax.broadcasted_iota(jnp.int32, (vectors, vectors * rows), 1) // rows
        widen = (widen_at == lax.broadcasted_iota(jnp.int32, (vectors, vectors * rows), 0)).astype(jnp.bfloat16)
        wide = jnp.dot(field, widen, preferred_element_type=jnp.float32)
        shape = (count, rows, vectors * rows)
        own = lax.broadcasted_iota(jnp.int32, shape, 1)
        other = lax.broadcasted_iota(jnp.int32, shape, 2) % rows
        spread = jnp.where(own == other, wide[:, None, :], 0.0)
        spread_ref[...] = spread.reshape(count * rows, vectors * rows).astype(jnp.bfloat16)

    out_ref[...] = (
        jnp.dot(
            spread_ref[...],
            chol_ref[...].reshape(vectors * rows, orbitals),
            preferred_element_type=jnp.float32,
        )
        .astype(jnp.bfloat16)
        .reshape(count, rows, orbitals)
    )


def potential_rows(sums, noise, cholesky):
    vectors, tile_rows, orbitals = cholesky.shape
    count = noise.shape[0]
    if tile_rows % ROWS:
        shifted, _ = shifted_field(sums, noise)
        return jnp.einsum(
            "kg,gpq->kpq", shifted.astype(jnp.bfloat16), cholesky, preferred_element_type=jnp.float32
        ).astype(jnp.bfloat16)
    return pl.pallas_call(
        potential_kernel,
        grid=(tile_rows // ROWS,),
        in_specs=[
            pl.BlockSpec(sums.shape, lambda t: (0, 0, 0)),
            pl.BlockSpec(noise.shape, lambda t: (0, 0)),
            pl.BlockSpec((vectors, ROWS, orbitals), lambda t: (0, t, 0)),
        ],
        out_specs=pl.BlockSpec((count, ROWS, orbitals), lambda t: (0, t, 0)),
        out_shape=jax.ShapeDtypeStruct((count, tile_rows, orbitals), jnp.bfloat16),
        scratch_shapes=[pltpu.VMEM((count * ROWS, vectors * ROWS), jnp.bfloat16)],
        compiler_params=pltpu.CompilerParams(vmem_limit_bytes=VMEM),
        cost_estimate=pl.CostEstimate(
            flops=2 * count * ROWS * vectors * tile_rows * orbitals,
            bytes_accessed=2 * (vectors + count) * tile_rows * orbitals,
            transcendentals=0,
        ),
        name="potential_rows",
    )(sums, noise, cholesky)


def taylor_kernel(potential_ref, walker_ref, out_ref):
    potential = potential_ref[...]
    term = walker_ref[...]
    running = term.astype(jnp.float32)
    for degree in range(1, DEGREES + 1):
        product = (-STEP_ROOT / degree) * jnp.dot(potential, term, preferred_element_type=jnp.float32)
        running = running + product
        term = product.astype(jnp.bfloat16)
    out_ref[...] = running.astype(jnp.bfloat16)


def taylor(potential, walker):
    orbitals, electrons = walker.shape
    return pl.pallas_call(
        taylor_kernel,
        out_shape=jax.ShapeDtypeStruct(walker.shape, jnp.bfloat16),
        compiler_params=pltpu.CompilerParams(vmem_limit_bytes=VMEM),
        cost_estimate=pl.CostEstimate(
            flops=2 * DEGREES * orbitals * orbitals * electrons,
            bytes_accessed=2 * orbitals * (orbitals + 2 * electrons),
            transcendentals=0,
        ),
        name="taylor",
    )(potential, walker)


def exchange(blocks):
    return lax.all_to_all(blocks, PLANE, 0, 0, tiled=True)


def gather(block):
    planes = lax.axis_size(PLANE)
    return exchange(jnp.broadcast_to(block[None], (planes,) + block.shape))


def per_device(walkers, intersection_inverse, noise_index, cholesky):
    walker_count, orbitals, electrons = walkers.shape
    vectors, tile_rows, _ = cholesky.shape
    planes = lax.axis_size(PLANE)
    me = lax.axis_index(PLANE)

    level = (noise_index.astype(jnp.float32) + 0.5) / NOISE_LEVELS
    noise = ROOT_TWO * lax.erf_inv(2.0 * level - 1.0)

    greens = []
    for k in range(walker_count):
        green = jnp.dot(walkers[k], intersection_inverse[k], preferred_element_type=jnp.float32)
        greens.append(exchange(green.astype(jnp.bfloat16).reshape(planes, tile_rows, electrons)))
    gathered = []
    for k in range(walker_count):
        sums = partial_bias(cholesky, greens[k])
        gathered.append(gather(jnp.concatenate([sums, noise[k : k + 1]], axis=0)))
    returned = []
    log_steps = []
    for k in range(walker_count):
        sums, noise_all = gathered[k][:, :planes], gathered[k][:, planes]
        returned.append(exchange(potential_rows(sums, noise_all, cholesky)))
        own_sums = lax.dynamic_index_in_dim(sums, me, 1, keepdims=False)
        shifted, force_bias = shifted_field(own_sums, noise[k])
        log_steps.append(jnp.sum(shifted * force_bias - 0.5 * force_bias * force_bias))
    new = [taylor(returned[k].reshape(orbitals, orbitals), walkers[k]) for k in range(walker_count)]
    return jnp.stack(new), jnp.stack(log_steps)


def solution(mesh):
    placed = (
        P(("grp", "wa", "col", "row"), None, None),
        P(("grp", "wa", "col", "row"), None, None),
        P(("grp", "wa", "col", "row"), None),
        P(None, ("wa", "col"), None),
    )
    return jax.shard_map(
        per_device,
        mesh=mesh,
        in_specs=placed,
        out_specs=(P(("grp", "wa", "col", "row"), None, None), P(("grp", "wa", "col", "row"))),
        check_vma=False,
    )
```

time: 223 us -> 198 us (0.89)
  the two profiles are of different devices: /device:TPU:8 before, /device:TPU:0 now
where the time goes in v1:
time: 198 us; the launch traced here: 197 us
  waiting for transfers between devices  105 us (53%)
  Pallas kernels  46.3 us (23%)
  starting transfers between devices  30.7 us (16%)
  other arithmetic  5.23 us (3%)
  local copies, waits for them, and re-layouts  4.56 us (2%)
  matrix products  4.38 us (2%)
    all_to_all x6, waiting for transfers between devices, exchange(): return lax.all_to_all(blocks, PLANE, 0, 0, tiled=True)  105 us
    all_to_all x6, starting transfers between devices, exchange(): return lax.all_to_all(blocks, PLANE, 0, 0, tiled=True)  30.7 us
    pallas_call x2, Pallas kernels, potential_rows(): pl.pallas_call(potential_kernel, grid=(tile_rows // ROWS,), in_specs=[pl....  21.3 us
    pallas_call x2, Pallas kernels, partial_bias(): pl.pallas_call(bias_kernel, grid=(tile_rows // ROWS,), in_specs=[pl.Block...  14.3 us
    pallas_call x2, Pallas kernels, taylor(): pl.pallas_call(taylor_kernel, out_shape=jax.ShapeDtypeStruct(walker.shape...  10.6 us
    dot_general x2, matrix products, per_device(): jnp.dot(walkers[k], intersection_inverse[k], preferred_element_type=jnp.f...  4.38 us
  transfers between devices with their start and end apart: 6, of which 4 were waited for; matrix products, arithmetic and copies ran while one was open for 5% of the time, Pallas kernels for 20%

profile of v1, /device:TPU:0, one launch (start us, length us, event | category | flops | bytes accessed | tf_op | source)
XLA Modules:
  0.0 197.2 jit_solution(15794890461092584136)
XLA Ops:
  0.6 0.0 copy-start.2
  0.7 2.9 %convolution_convert_fusion.1 = bf16[1024,384]{1,0:T(8,128)(2,1)} fusion(bf16[2,384,384]{2,1,0:T(8,128)(2,1)} %param.5, bf16[2,1024,384]{2,1,0:T(8,128)(2,1)} %param.4), kind=kOutput, calls=%fused_computation.2 | convolution fusion | flops 302383104 | bytes 1867776 | tf_op jit(solution)/shard_map/dot_general | solution.py:191
  3.5 7.2 %all-to-all-start = ((bf16[8,128,384]{2,1,0:T(8,128)(2,1)}), bf16[8,128,384]{2,1,0:T(8,128)(2,1)S(1)}, u32[]{:S(2)}, u32[]{:S(2)}) async-start(bf16[8,128,384]{2,1,0:T(8,128)(2,1)} %bitcast.2), calls=%async_computation | async-start | bytes 1572864 | tf_op jit(solution)/shard_map/all_to_all | solution.py:172
  10.8 0.0 copy-start.3
  10.8 1.5 convolution_convert_fusion
  12.3 18.6 %all-to-all-done.green_ref = bf16[8,128,384]{2,1,0:T(8,128)(2,1)S(1)} async-done(((bf16[8,128,384]{2,1,0:T(8,128)(2,1)}), bf16[8,128,384]{2,1,0:T(8,128)(2,1)S(1)}, u32[]{:S(2)}, u32[]{:S(2)}) %all-to-all-start) | async-done | bytes 786464 | tf_op jit(solution)/shard_map/all_to_all | solution.py:172
  31.0 3.6 %all-to-all-start.3 = ((bf16[8,128,384]{2,1,0:T(8,128)(2,1)}), bf16[8,128,384]{2,1,0:T(8,128)(2,1)S(1)}, u32[]{:S(2)}, u32[]{:S(2)}) async-start(bf16[8,128,384]{2,1,0:T(8,128)(2,1)} %bitcast.39), calls=%async_computation.3 | async-start | bytes 1572864 | tf_op jit(solution)/shard_map/all_to_all | solution.py:172
  34.6 7.2 %bias_sum.2 = f32[8,64]{1,0:T(8,128)S(1)} custom-call(bf16[64,128,1024]{2,1,0:T(8,128)(2,1)} %chol_ref.7, bf16[8,128,384]{2,1,0:T(8,128)(2,1)S(1)} %all-to-all-done.green_ref), custom_call_target="tpu_custom_call" | custom-call | flops 805306368 | bytes 7077888 | tf_op jit(solution)/shard_map/bias_sum/pallas_call | solution.py:63
  41.8 0.7 reshape.24
  42.5 12.4 %all-to-all-done.3.green_ref = bf16[8,128,384]{2,1,0:T(8,128)(2,1)S(1)} async-done(((bf16[8,128,384]{2,1,0:T(8,128)(2,1)}), bf16[8,128,384]{2,1,0:T(8,128)(2,1)S(1)}, u32[]{:S(2)}, u32[]{:S(2)}) %all-to-all-start.3) | async-done | bytes 786464 | tf_op jit(solution)/shard_map/all_to_all | solution.py:172
  54.9 3.5 %all-to-all-start.1 = ((f32[8,1,576]{2,1,0:T(1,128)}), f32[8,1,576]{2,1,0:T(1,128)S(1)}, u32[]{:S(2)}, u32[]{:S(2)}) async-start(f32[8,1,576]{2,1,0:T(1,128)} %reshape.24), calls=%async_computation.1 | async-start | bytes 40960 | tf_op jit(solution)/shard_map/all_to_all | solution.py:172
  58.4 7.2 %bias_sum.3 = f32[8,64]{1,0:T(8,128)S(1)} custom-call(bf16[64,128,1024]{2,1,0:T(8,128)(2,1)} %chol_ref.7, bf16[8,128,384]{2,1,0:T(8,128)(2,1)S(1)} %all-to-all-done.3.green_ref), custom_call_target="tpu_custom_call" | custom-call | flops 805306368 | bytes 7077888 | tf_op jit(solution)/shard_map/bias_sum/pallas_call | solution.py:63
  65.6 0.7 reshape.22
  66.3 6.0 %all-to-all-start.4 = ((f32[8,1,576]{2,1,0:T(1,128)}), f32[8,1,576]{2,1,0:T(1,128)S(1)}, u32[]{:S(2)}, u32[]{:S(2)}) async-start(f32[8,1,576]{2,1,0:T(1,128)} %reshape.22), calls=%async_computation.4 | async-start | bytes 40960 | tf_op jit(solution)/shard_map/all_to_all | solution.py:172
  72.3 0.5 broadcast.36
  72.8 0.7 reduce.3
  73.5 0.1 reshape.25
  73.6 10.7 %potential_rows.2 = bf16[8,128,1024]{2,1,0:T(8,128)(2,1)} custom-call(f32[8,8,64]{2,1,0:T(8,128)S(1)} %slice.44.sums_ref, f32[8,64]{1,0:T(8,128)S(1)} %bitcast.37, bf16[64,128,1024]{2,1,0:T(8,128)(2,1)} %chol_ref.7), custom_call_target="tpu_custom_call" | custom-call | flops 2147483648 | bytes 18874368 | tf_op jit(solution)/shard_map/potential_rows/pallas_call | solution.py:124
  84.3 6.0 %all-to-all-start.2 = ((bf16[8,128,1024]{2,1,0:T(8,128)(2,1)}), bf16[8,128,1024]{2,1,0:T(8,128)(2,1)S(1)}, u32[]{:S(2)}, u32[]{:S(2)}) async-start(bf16[8,128,1024]{2,1,0:T(8,128)(2,1)} %potential_rows.2), calls=%async_computation.2 | async-start | bytes 4194304 | tf_op jit(solution)/shard_map/all_to_all | solution.py:172
  90.3 0.7 reduce.2
  91.0 0.1 reshape.23
  91.1 10.6 %potential_rows.3 = bf16[8,128,1024]{2,1,0:T(8,128)(2,1)} custom-call(f32[8,8,64]{2,1,0:T(8,128)S(1)} %slice.46.sums_ref, f32[8,64]{1,0:T(8,128)S(1)} %bitcast.38, bf16[64,128,1024]{2,1,0:T(8,128)(2,1)} %chol_ref.7), custom_call_target="tpu_custom_call" | custom-call | flops 2147483648 | bytes 18874368 | tf_op jit(solution)/shard_map/potential_rows/pallas_call | solution.py:124
  101.7 35.9 %all-to-all-done.2 = bf16[8,128,1024]{2,1,0:T(8,128)(2,1)S(1)} async-done(((bf16[8,128,1024]{2,1,0:T(8,128)(2,1)}), bf16[8,128,1024]{2,1,0:T(8,128)(2,1)S(1)}, u32[]{:S(2)}, u32[]{:S(2)}) %all-to-all-start.2) | async-done | bytes 2097184 | tf_op jit(solution)/shard_map/all_to_all | solution.py:172
  137.6 4.4 %all-to-all-start.5 = ((bf16[8,128,1024]{2,1,0:T(8,128)(2,1)}), bf16[8,128,1024]{2,1,0:T(8,128)(2,1)}, u32[]{:S(2)}, u32[]{:S(2)}) async-start(bf16[8,128,1024]{2,1,0:T(8,128)(2,1)} %potential_rows.3), calls=%async_computation.5 | async-start | bytes 4194304 | tf_op jit(solution)/shard_map/all_to_all | solution.py:172
  142.0 1.5 slice_bitcast_fusion.1
  143.5 0.6 fusion.10
  144.2 1.8 pad_maximum_fusion.3
  146.0 4.5 %taylor.2 = bf16[1024,384]{1,0:T(8,128)(2,1)S(1)} custom-call(bf16[1024,1024]{1,0:T(8,128)(2,1)S(1)} %bitcast.34, bf16[1024,384]{1,0:T(8,128)(2,1)S(1)} %get-tuple-element.4.walker_ref), custom_call_target="tpu_custom_call" | custom-call | flops 3221225472 | bytes 3670016 | tf_op jit(solution)/shard_map/taylor/pallas_call | solution.py:158
  150.5 0.9 copy-done
  151.3 38.4 %all-to-all-done.5 = bf16[8,128,1024]{2,1,0:T(8,128)(2,1)} async-done(((bf16[8,128,1024]{2,1,0:T(8,128)(2,1)}), bf16[8,128,1024]{2,1,0:T(8,128)(2,1)}, u32[]{:S(2)}, u32[]{:S(2)}) %all-to-all-start.5) | async-done | bytes 2097184 | tf_op jit(solution)/shard_map/all_to_all | solution.py:172
  189.7 6.2 %taylor.3 = bf16[1024,384]{1,0:T(8,128)(2,1)S(1)} custom-call(bf16[1024,1024]{1,0:T(8,128)(2,1)} %bitcast.10.potential_ref, bf16[1024,384]{1,0:T(8,128)(2,1)S(1)} %get-tuple-element.5.walker_ref), custom_call_target="tpu_custom_call" | custom-call | flops 3221225472 | bytes 3670016 | tf_op jit(solution)/shard_map/taylor/pallas_call | solution.py:158
  195.9 1.3 pad_maximum_fusion
  (21 shorter events, 0.2 us)
Async XLA Ops:
  0.6 10.1 %copy-start.2 = (bf16[2,1024,384]{2,1,0:T(8,128)(2,1)S(1)}, bf16[2,1024,384]{2,1,0:T(8,128)(2,1)}, u32[]{:S(2)}) copy-start(bf16[2,1024,384]{2,1,0:T(8,128)(2,1)} %param.4) | copy-start | bytes 4718596
  0.6 10.1 %copy-start.4 = (bf16[2,384,384]{2,1,0:T(8,128)(2,1)S(1)}, bf16[2,384,384]{2,1,0:T(8,128)(2,1)}, u32[]{:S(2)}) copy-start(bf16[2,384,384]{2,1,0:T(8,128)(2,1)} %param.5) | copy-start | bytes 1769476
  3.5 27.4 %all-to-all-start = ((bf16[8,128,384]{2,1,0:T(8,128)(2,1)}), bf16[8,128,384]{2,1,0:T(8,128)(2,1)S(1)}, u32[]{:S(2)}, u32[]{:S(2)}) async-start(bf16[8,128,384]{2,1,0:T(8,128)(2,1)} %bitcast.2), calls=%async_computation | async-start | bytes 1572864 | tf_op jit(solution)/shard_map/all_to_all | solution.py:172
  10.8 23.7 %copy-start.3 = (s32[2,64]{1,0:T(2,128)S(1)}, s32[2,64]{1,0:T(2,128)}, u32[]{:S(2)}) copy-start(s32[2,64]{1,0:T(2,128)} %param.6) | copy-start | bytes 1540
  31.0 23.9 %all-to-all-start.3 = ((bf16[8,128,384]{2,1,0:T(8,128)(2,1)}), bf16[8,128,384]{2,1,0:T(8,128)(2,1)S(1)}, u32[]{:S(2)}, u32[]{:S(2)}) async-start(bf16[8,128,384]{2,1,0:T(8,128)(2,1)} %bitcast.39), calls=%async_computation.3 | async-start | bytes 1572864 | tf_op jit(solution)/shard_map/all_to_all | solution.py:172
  54.9 11.4 %all-to-all-start.1 = ((f32[8,1,576]{2,1,0:T(1,128)}), f32[8,1,576]{2,1,0:T(1,128)S(1)}, u32[]{:S(2)}, u32[]{:S(2)}) async-start(f32[8,1,576]{2,1,0:T(1,128)} %reshape.24), calls=%async_computation.1 | async-start | bytes 40960 | tf_op jit(solution)/shard_map/all_to_all | solution.py:172
  66.3 17.9 %all-to-all-start.4 = ((f32[8,1,576]{2,1,0:T(1,128)}), f32[8,1,576]{2,1,0:T(1,128)S(1)}, u32[]{:S(2)}, u32[]{:S(2)}) async-start(f32[8,1,576]{2,1,0:T(1,128)} %reshape.22), calls=%async_computation.4 | async-start | bytes 40960 | tf_op jit(solution)/shard_map/all_to_all | solution.py:172
  84.3 53.3 %all-to-all-start.2 = ((bf16[8,128,1024]{2,1,0:T(8,128)(2,1)}), bf16[8,128,1024]{2,1,0:T(8,128)(2,1)S(1)}, u32[]{:S(2)}, u32[]{:S(2)}) async-start(bf16[8,128,1024]{2,1,0:T(8,128)(2,1)} %potential_rows.2), calls=%async_computation.2 | async-start | bytes 4194304 | tf_op jit(solution)/shard_map/all_to_all | solution.py:172
  137.6 52.2 %all-to-all-start.5 = ((bf16[8,128,1024]{2,1,0:T(8,128)(2,1)}), bf16[8,128,1024]{2,1,0:T(8,128)(2,1)}, u32[]{:S(2)}, u32[]{:S(2)}) async-start(bf16[8,128,1024]{2,1,0:T(8,128)(2,1)} %potential_rows.3), calls=%async_computation.5 | async-start | bytes 4194304 | tf_op jit(solution)/shard_map/all_to_all | solution.py:172
  150.5 0.9 copy-start
  189.7 6.2 %copy-start.1 = (bf16[1024,384]{1,0:T(8,128)(2,1)S(1)}, bf16[1024,384]{1,0:T(8,128)(2,1)}, u32[]{:S(2)}) copy-start(bf16[1024,384]{1,0:T(8,128)(2,1)} %copy-done) | copy-start | bytes 2359300

commit v2 on v0

v2 whole, which is shorter than its diff:
```python
import functools

import jax
import jax.numpy as jnp
from jax import lax
from jax.experimental import pallas as pl
from jax.experimental.pallas import tpu as pltpu
from jax.sharding import PartitionSpec as P

NOISE_LEVELS = 65536


STEP_ROOT = 0.1
BIAS_CAP = 1.0
ROOT_TWO = 1.4142135623730951
DEGREES = 4
PLANE = ("wa", "col")
ROWS = 16
MOST_PERMUTES = 8
VMEM = 24 * 1024 * 1024
IN_VMEM = pl.BlockSpec(memory_space=pltpu.VMEM)
IN_HBM = pl.BlockSpec(memory_space=pl.ANY)


def kernel_params():
    return pltpu.CompilerParams(vmem_limit_bytes=VMEM)


def quantile(codes):
    level = (codes.astype(jnp.float32) + 0.5) / NOISE_LEVELS
    return ROOT_TWO * lax.erf_inv(2.0 * level - 1.0)


def shifted_field(bias_sum, noise):
    force_bias = jnp.clip(STEP_ROOT * bias_sum, -BIAS_CAP, BIAS_CAP)
    shifted = noise - force_bias
    return shifted, shifted * force_bias - 0.5 * force_bias * force_bias


def iota(shape, dimension):
    return lax.broadcasted_iota(jnp.int32, shape, dimension)


def own_place():
    return lax.axis_index("wa") * lax.axis_size("col") + lax.axis_index("col")


def green_kernel(places, walker_ref, inverse_ref, *out_refs):
    me = own_place()
    inverse = inverse_ref[0]
    for place, out_ref in zip(places, out_refs):
        tile_rows = out_ref.shape[0]
        start = pl.multiple_of(jnp.bitwise_xor(me, place) * tile_rows, tile_rows)
        rows = walker_ref[0, pl.ds(start, tile_rows), :]
        out_ref[...] = jnp.dot(rows, inverse, preferred_element_type=jnp.float32).astype(jnp.bfloat16)


def green_rows(walkers, inverses, k, places, tile_rows):
    _, orbitals, electrons = walkers.shape
    return pl.pallas_call(
        functools.partial(green_kernel, places),
        grid=(1,),
        in_specs=[
            pl.BlockSpec((1, orbitals, electrons), lambda t: (k, 0, 0)),
            pl.BlockSpec((1, electrons, electrons), lambda t: (k, 0, 0)),
        ],
        out_specs=[pl.BlockSpec((tile_rows, electrons), lambda t: (0, 0))] * len(places),
        out_shape=[jax.ShapeDtypeStruct((tile_rows, electrons), jnp.bfloat16)] * len(places),
        compiler_params=kernel_params(),
        cost_estimate=pl.CostEstimate(
            flops=2 * len(places) * tile_rows * electrons * electrons,
            bytes_accessed=2 * electrons * (orbitals + electrons + len(places) * tile_rows),
            transcendentals=0,
        ),
        name="green_rows",
    )(walkers, inverses)


def bias_kernel(count, chol_ref, noise_ref, *refs):
    greens, out_ref = refs[:count], refs[count]
    vectors, tile_rows, _ = chol_ref.shape
    electrons = greens[0].shape[1]
    me = own_place()
    total = jnp.zeros((vectors * ROWS, count * ROWS), jnp.float32)
    for start in range(0, tile_rows, ROWS):
        green = jnp.concatenate([ref[start : start + ROWS, :] for ref in greens], axis=0)
        tile = chol_ref[:, start : start + ROWS, :electrons].reshape(vectors * ROWS, electrons)
        total += lax.dot_general(tile, green, (((1,), (1,)), ((), ())), preferred_element_type=jnp.float32)
    total = total.reshape(vectors, ROWS, count * ROWS)
    same = iota(total.shape, 1) == iota(total.shape, 2) % ROWS
    summed = jnp.sum(jnp.where(same, total, 0.0), axis=1)
    shape = (count, count * ROWS)
    fold = jnp.bitwise_xor(iota(shape, 1) // ROWS, me) == iota(shape, 0)
    out_ref[:count, :] = lax.dot_general(
        fold.astype(jnp.float32),
        summed,
        (((1,), (1,)), ((), ())),
        preferred_element_type=jnp.float32,
        precision=lax.Precision.HIGHEST,
    )
    out_ref[count:, :] = jnp.where(iota((count, vectors), 0) == me, noise_ref[...], 0.0)


def bias_rows(cholesky, noise, greens):
    vectors, tile_rows, _ = cholesky.shape
    count, electrons = len(greens), greens[0].shape[1]
    return pl.pallas_call(
        functools.partial(bias_kernel, count),
        in_specs=[IN_VMEM] * (2 + count),
        out_specs=IN_VMEM,
        out_shape=jax.ShapeDtypeStruct((2 * count, vectors), jnp.float32),
        compiler_params=kernel_params(),
        cost_estimate=pl.CostEstimate(
            flops=2 * vectors * ROWS * count * tile_rows * electrons,
            bytes_accessed=2 * (vectors + count) * tile_rows * electrons,
            transcendentals=0,
        ),
        name="bias_rows",
    )(pltpu.with_memory_space_constraint(cholesky, pltpu.VMEM), noise, *greens)


def potential_kernel(count, sums_ref, chol_ref, *refs):
    outs, log_ref = refs[:count], refs[count]
    vectors, tile_rows, orbitals = chol_ref.shape
    me = own_place()
    shifted, log_terms = shifted_field(sums_ref[:count, :], sums_ref[count:, :])
    log_ref[...] = jnp.sum(log_terms, axis=1, keepdims=True)
    field = shifted.astype(jnp.bfloat16)
    order = (jnp.bitwise_xor(iota((count, count), 0), me) == iota((count, count), 1)).astype(jnp.bfloat16)
    field = jnp.dot(order, field, preferred_element_type=jnp.float32).astype(jnp.bfloat16)
    widen = (iota((vectors, vectors * ROWS), 1) // ROWS == iota((vectors, vectors * ROWS), 0)).astype(jnp.bfloat16)
    wide = jnp.dot(field, widen, preferred_element_type=jnp.float32)
    shape = (count, ROWS, vectors * ROWS)
    spread = jnp.where(iota(shape, 1) == iota(shape, 2) % ROWS, wide[:, None, :], 0.0)
    spread = spread.reshape(count * ROWS, vectors * ROWS).astype(jnp.bfloat16)
    for start in range(0, tile_rows, ROWS):
        tile = chol_ref[:, start : start + ROWS, :].reshape(vectors * ROWS, orbitals)
        rows = jnp.dot(spread, tile, preferred_element_type=jnp.float32).astype(jnp.bfloat16)
        for place in range(count):
            outs[place][start : start + ROWS, :] = rows[place * ROWS : (place + 1) * ROWS, :]


def potential_rows(sums, cholesky):
    vectors, tile_rows, orbitals = cholesky.shape
    count = sums.shape[0] // 2
    rows = jax.ShapeDtypeStruct((tile_rows, orbitals), jnp.bfloat16)
    *blocks, log_steps = pl.pallas_call(
        functools.partial(potential_kernel, count),
        in_specs=[IN_VMEM, IN_VMEM],
        out_specs=[IN_VMEM] * (count + 1),
        out_shape=[rows] * count + [jax.ShapeDtypeStruct((count, 1), jnp.float32)],
        compiler_params=kernel_params(),
        cost_estimate=pl.CostEstimate(
            flops=2 * count * ROWS * vectors * tile_rows * orbitals,
            bytes_accessed=2 * (vectors + count) * tile_rows * orbitals,
            transcendentals=0,
        ),
        name="potential_rows",
    )(sums, pltpu.with_memory_space_constraint(cholesky, pltpu.VMEM))
    return blocks, log_steps


def taylor_steps(potential, term, product_of):
    running = term.astype(jnp.float32)
    for degree in range(1, DEGREES + 1):
        product = (-STEP_ROOT / degree) * product_of(potential, term)
        running = running + product
        term = product.astype(jnp.bfloat16)
    return running.astype(jnp.bfloat16)


def taylor_kernel(count, *refs):
    blocks, walker_ref, out_ref, held, arrived = refs[:count], *refs[count:]
    me = own_place()
    copies = [
        pltpu.make_async_copy(block, held.at[jnp.bitwise_xor(me, place)], arrived.at[place])
        for place, block in enumerate(blocks)
    ]
    for copy in copies:
        copy.start()
    for copy in copies:
        copy.wait()
    orbitals = held.shape[2]
    out_ref[0] = taylor_steps(
        held[...].reshape(orbitals, orbitals),
        walker_ref[0],
        lambda a, b: jnp.dot(a, b, preferred_element_type=jnp.float32),
    )


def taylor(blocks, walkers, k):
    _, orbitals, electrons = walkers.shape
    count, tile_rows = len(blocks), blocks[0].shape[0]
    return pl.pallas_call(
        functools.partial(taylor_kernel, count),
        grid=(1,),
        in_specs=[IN_HBM] * count + [pl.BlockSpec((1, orbitals, electrons), lambda t: (k, 0, 0))],
        out_specs=pl.BlockSpec((1, orbitals, electrons), lambda t: (0, 0, 0)),
        out_shape=jax.ShapeDtypeStruct((1, orbitals, electrons), jnp.bfloat16),
        scratch_shapes=[
            pltpu.VMEM((count, tile_rows, orbitals), jnp.bfloat16),
            pltpu.SemaphoreType.DMA((count,)),
        ],
        compiler_params=kernel_params(),
        cost_estimate=pl.CostEstimate(
            flops=2 * DEGREES * orbitals * orbitals * electrons,
            bytes_accessed=2 * orbitals * (orbitals + 2 * electrons),
            transcendentals=0,
        ),
        name="taylor",
    )(*blocks, walkers)


def swap(block, place):
    if place == 0:
        return block
    planes = lax.axis_size(PLANE)
    return lax.ppermute(block, PLANE, [(i, i ^ place) for i in range(planes)])


def by_permutes(walkers, intersection_inverse, noise_index, cholesky):
    walker_count = walkers.shape[0]
    tile_rows = cholesky.shape[1]
    planes = lax.axis_size(PLANE)
    far = tuple(range(planes // 2, planes))
    near = tuple(range(planes // 2))
    noise = quantile(noise_index)

    greens = []
    for k in range(walker_count):
        far_rows = green_rows(walkers, intersection_inverse, k, far, tile_rows)
        near_rows = green_rows(walkers, intersection_inverse, k, near, tile_rows)
        greens.append([swap(rows, place) for place, rows in enumerate((*near_rows, *far_rows))])
    sums = []
    for k in range(walker_count):
        total = bias_rows(cholesky, noise[k : k + 1], greens[k])
        distance = 1
        while distance < planes:
            total = total + swap(total, distance)
            distance *= 2
        sums.append(total)
    new, log_steps = [], []
    for k in range(walker_count):
        blocks, log_all = potential_rows(sums[k], cholesky)
        new.append(taylor([swap(rows, place) for place, rows in enumerate(blocks)], walkers, k))
        log_steps.append(lax.dynamic_index_in_dim(log_all[:, 0], lax.axis_index(PLANE), 0, keepdims=True))
    return jnp.concatenate(new, axis=0), jnp.concatenate(log_steps)


def by_all_to_all(walkers, intersection_inverse, noise_index, cholesky):
    walker_count, orbitals, electrons = walkers.shape
    vectors, tile_rows, _ = cholesky.shape
    planes = lax.axis_size(PLANE)
    green = jnp.einsum(
        "kpe,kef->kpf", walkers, intersection_inverse, preferred_element_type=jnp.float32
    ).astype(jnp.bfloat16)
    green = lax.all_to_all(
        green.reshape(walker_count, planes, tile_rows, electrons), PLANE, split_axis=1, concat_axis=1, tiled=True
    )
    partial_sums = jnp.einsum(
        "kspe,gpe->ksg", green, cholesky[:, :, :electrons], preferred_element_type=jnp.float32
    )
    bias_sum = lax.psum(partial_sums, PLANE)
    noise = lax.all_gather(quantile(noise_index), PLANE, axis=1, tiled=False)
    shifted, log_terms = shifted_field(bias_sum, noise)
    log_weight = lax.dynamic_index_in_dim(jnp.sum(log_terms, axis=-1), lax.axis_index(PLANE), 1, keepdims=False)
    rows = jnp.einsum(
        "ksg,gpq->kspq", shifted.astype(jnp.bfloat16), cholesky, preferred_element_type=jnp.float32
    ).astype(jnp.bfloat16)
    potential = lax.all_to_all(rows, PLANE, split_axis=1, concat_axis=1, tiled=True)
    new = taylor_steps(
        potential.reshape(walker_count, orbitals, orbitals),
        walkers,
        lambda a, b: jnp.einsum("kpq,kqe->kpe", a, b, preferred_element_type=jnp.float32),
    )
    return new, log_weight


def per_device(walkers, intersection_inverse, noise_index, cholesky):
    planes = lax.axis_size(PLANE)
    tile_rows = cholesky.shape[1]
    permutes = planes <= MOST_PERMUTES and planes & (planes - 1) == 0 and tile_rows % ROWS == 0
    step = by_permutes if permutes else by_all_to_all
    return step(walkers, intersection_inverse, noise_index, cholesky)


def solution(mesh):
    placed = (
        P(("grp", "wa", "col", "row"), None, None),
        P(("grp", "wa", "col", "row"), None, None),
        P(("grp", "wa", "col", "row"), None),
        P(None, ("wa", "col"), None),
    )
    return jax.shard_map(
        per_device,
        mesh=mesh,
        in_specs=placed,
        out_specs=(P(("grp", "wa", "col", "row"), None, None), P(("grp", "wa", "col", "row"))),
        check_vma=False,
    )
```

time: 223 us -> 167 us (0.75); the launches traced: 219 us -> 167 us
  local copies, waits for them, and re-layouts: 56.7 us -> 13.5 us
  blocking collectives: 35.3 us -> 0 us
  starting transfers between devices: 13.9 us -> 48.3 us
  matrix products: 29.5 us -> 0 us
  Pallas kernels: 0 us -> 23.9 us
  waiting for transfers between devices: 82.5 us -> 77 us
  other arithmetic: 0.13 us -> 3.18 us
    all_to_all x2 -> x0, waiting for transfers between devices: 82.5 us -> none  [the longest x1 82.5 us: per_device(): lax.all_to_all(tiles_out, ('wa', 'col'), split_axis=1, concat_axis=1, til...]
    ppermute x0 -> x34, waiting for transfers between devices: none -> 77 us  [swap(): return lax.ppermute(block, PLANE, [(i, i ^ place) for i in range(planes)])]
    ppermute x0 -> x34, starting transfers between devices: none -> 48.3 us  [swap(): return lax.ppermute(block, PLANE, [(i, i ^ place) for i in range(planes)])]
    reshape x5 -> x0, local copies, waits for them, and re-layouts: 35.5 us -> none  [the longest x1 17 us: per_device(): full_tile = cholesky.reshape(vectors, tile_rows * orbitals)]
    dot_general x7 -> x0, matrix products: 29.5 us -> none  [the longest x4 13.2 us: per_device(): jnp.einsum('kpq,kqe->kpe', potential, factor_term, preferred_element_type...]
    pallas_call x0 -> x10, Pallas kernels: none -> 23.9 us  [the longest x2 11.4 us: taylor(): pl.pallas_call(functools.partial(taylor_kernel, count), grid=(1,), in_spe...]
    all_gather x1 -> x0, blocking collectives: 17.7 us -> none  [per_device(): gathered = lax.all_gather(noise_index, ('wa', 'col'), axis=0, tiled=True)]
    psum x1 -> x0, blocking collectives: 17.6 us -> none  [per_device(): bias_sum = lax.psum(partial_sums, ('wa', 'col'))]
  transfers between devices with their start and end apart: 2 -> 34, of which waited for: 1 -> 12; matrix products, arithmetic and copies ran while one was open for 15% -> 2% of each run, Pallas kernels for 0% -> 11%
where the time goes in v2:
time: 167 us
  waiting for transfers between devices  77 us (46%)
  starting transfers between devices  48.3 us (29%)
  Pallas kernels  23.9 us (14%)
  local copies, waits for them, and re-layouts  13.5 us (8%)
  other arithmetic  3.18 us (2%)
    ppermute x34, waiting for transfers between devices, swap(): return lax.ppermute(block, PLANE, [(i, i ^ place) for i in range(planes)])  77 us
    ppermute x34, starting transfers between devices, swap(): return lax.ppermute(block, PLANE, [(i, i ^ place) for i in range(planes)])  48.3 us
    unnamed x28, local copies, waits for them, and re-layouts  12.4 us
    pallas_call x2, Pallas kernels, taylor(): pl.pallas_call(functools.partial(taylor_kernel, count), grid=(1,), in_spe...  11.4 us
    pallas_call x2, Pallas kernels, potential_rows(): pl.pallas_call(functools.partial(potential_kernel, count), in_specs=[IN_V...  6.69 us
    pallas_call x2, Pallas kernels, bias_rows(): pl.pallas_call(functools.partial(bias_kernel, count), in_specs=[IN_VMEM]...  4.14 us
  transfers between devices with their start and end apart: 34, of which 12 were waited for; matrix products, arithmetic and copies ran while one was open for 2% of the time, Pallas kernels for 11%

profile of v2, /device:TPU:8, one launch (start us, length us, event | category | flops | bytes accessed | tf_op | source)
XLA Modules:
  0.0 166.7 jit_solution(12642373799027872265)
XLA Ops:
  3.5 2.7 %collective-permute-start.20 = (bf16[128,384]{1,0:T(8,128)(2,1)S(1)}, bf16[128,384]{1,0:T(8,128)(2,1)S(1)}, u32[]{:S(2)}, u32[]{:S(2)}) collective-permute-start(bf16[128,384]{1,0:T(8,128)(2,1)S(1)} %get-tuple-element.56), channel_id=1, source_target_pairs={{0,8},{2,10},{4,12},{6,14},{8,0},{10,2},{12,4},{14,6},{1,9},{3,11}... | collective-permute-start | bytes 294920 | tf_op jit(solution)/shard_map/ppermute | solution.py:218
  7.5 1.6 collective-permute-start.22
  11.5 5.2 %collective-permute-done.20.refs_4_ = bf16[128,384]{1,0:T(8,128)(2,1)S(1)} collective-permute-done((bf16[128,384]{1,0:T(8,128)(2,1)S(1)}, bf16[128,384]{1,0:T(8,128)(2,1)S(1)}, u32[]{:S(2)}, u32[]{:S(2)}) %collective-permute-start.20) | collective-permute-done | bytes 98336 | tf_op jit(solution)/shard_map/ppermute | solution.py:218
  16.6 2.1 %collective-permute-start.18 = (bf16[128,384]{1,0:T(8,128)(2,1)S(1)}, bf16[128,384]{1,0:T(8,128)(2,1)S(1)}, u32[]{:S(2)}, u32[]{:S(2)}) collective-permute-start(bf16[128,384]{1,0:T(8,128)(2,1)S(1)} %get-tuple-element.54), channel_id=1, source_target_pairs={{0,4},{2,6},{4,0},{6,2},{8,12},{10,14},{12,8},{14,10},{1,5},{3,7},... | collective-permute-start | bytes 294920 | tf_op jit(solution)/shard_map/ppermute | solution.py:218
  18.8 2.9 %collective-permute-start.19 = (bf16[128,384]{1,0:T(8,128)(2,1)S(1)}, bf16[128,384]{1,0:T(8,128)(2,1)S(1)}, u32[]{:S(2)}, u32[]{:S(2)}) collective-permute-start(bf16[128,384]{1,0:T(8,128)(2,1)S(1)} %get-tuple-element.55), channel_id=1, source_target_pairs={{0,6},{2,4},{4,2},{6,0},{8,14},{10,12},{12,10},{14,8},{1,7},{3,5},... | collective-permute-start | bytes 294920 | tf_op jit(solution)/shard_map/ppermute | solution.py:218
  26.3 5.8 %copy-done = bf16[64,128,1024]{2,1,0:T(8,128)(2,1)S(1)} copy-done((bf16[64,128,1024]{2,1,0:T(8,128)(2,1)S(1)}, bf16[64,128,1024]{2,1,0:T(8,128)(2,1)}, u32[]{:S(2)}) %copy-start) | copy-done | bytes 16777240
  32.1 2.1 %bias_rows.3 = f32[16,64]{1,0:T(8,128)S(1)} custom-call(bf16[64,128,1024]{2,1,0:T(8,128)(2,1)S(1)} %copy-done, f32[1,64]{1,0:T(1,128)S(1)} %get-tuple-element.71.noise_ref, bf16[128,384]{1,0:T(8,128)(2,1)S(1)} %get-tuple-element.52.refs_0_, bf16[128,384]{1,0:T(8,128)(2,1)S(1)} %collective-permute-done.17.refs_1_, ...), custom_call_target="tpu_custom_call" | custom-call | flops 805306368 | bytes 7077888 | tf_op jit(solution)/shard_map/bias_rows/pallas_call | solution.py:107
  34.5 3.3 %collective-permute-done.24 = f32[16,64]{1,0:T(8,128)S(1)} collective-permute-done((f32[16,64]{1,0:T(8,128)S(1)}, f32[16,64]{1,0:T(8,128)S(1)}, u32[]{:S(2)}, u32[]{:S(2)}) %collective-permute-start.24) | collective-permute-done | bytes 4128 | tf_op jit(solution)/shard_map/ppermute | solution.py:218
  37.8 2.8 %collective-permute-start.25 = (f32[16,64]{1,0:T(8,128)S(1)}, f32[16,64]{1,0:T(8,128)S(1)}, u32[]{:S(2)}, u32[]{:S(2)}) collective-permute-start(f32[16,64]{1,0:T(8,128)S(1)} %add.41), channel_id=1, source_target_pairs={{0,4},{2,6},{4,0},{6,2},{8,12},{10,14},{12,8},{14,10},{1,5},{3,7},... | collective-permute-start | bytes 12296 | tf_op jit(solution)/shard_map/ppermute | solution.py:218
  41.8 2.3 %collective-permute-start.6 = (bf16[128,384]{1,0:T(8,128)(2,1)S(1)}, bf16[128,384]{1,0:T(8,128)(2,1)S(1)}, u32[]{:S(2)}, u32[]{:S(2)}) collective-permute-start(bf16[128,384]{1,0:T(8,128)(2,1)S(1)} %get-tuple-element.43), channel_id=1, source_target_pairs={{0,14},{2,12},{4,10},{6,8},{8,6},{10,4},{12,2},{14,0},{1,15},{3,13... | collective-permute-start | bytes 294920 | tf_op jit(solution)/shard_map/ppermute | solution.py:218
  45.8 3.0 %collective-permute-done.26 = f32[16,64]{1,0:T(8,128)S(1)} collective-permute-done((f32[16,64]{1,0:T(8,128)S(1)}, f32[16,64]{1,0:T(8,128)S(1)}, u32[]{:S(2)}, u32[]{:S(2)}) %collective-permute-start.26) | collective-permute-done | bytes 4128 | tf_op jit(solution)/shard_map/ppermute | solution.py:218
  49.5 3.9 %collective-permute-start.1 = (bf16[128,384]{1,0:T(8,128)(2,1)S(1)}, bf16[128,384]{1,0:T(8,128)(2,1)S(1)}, u32[]{:S(2)}, u32[]{:S(2)}) collective-permute-start(bf16[128,384]{1,0:T(8,128)(2,1)S(1)} %get-tuple-element.38), channel_id=1, source_target_pairs={{0,4},{2,6},{4,0},{6,2},{8,12},{10,14},{12,8},{14,10},{1,5},{3,7},... | collective-permute-start | bytes 294920 | tf_op jit(solution)/shard_map/ppermute | solution.py:218
  53.4 3.3 %potential_rows.3 = (bf16[128,1024]{1,0:T(8,128)(2,1)S(1)}, bf16[128,1024]{1,0:T(8,128)(2,1)S(1)}, bf16[128,1024]{1,0:T(8,128)(2,1)S(1)}, bf16[128,1024]{1,0:T(8...) custom-call(f32[16,64]{1,0:T(8,128)S(1)} %add.43.sums_ref, ...), custom_call_target="tpu_custom_call" | custom-call | flops 2147483648 | bytes 18874368 | tf_op jit(solution)/shard_map/potential_rows/pallas_call | solution.py:147
  58.3 1.9 %collective-permute-start.28 = (bf16[128,1024]{1,0:T(8,128)(2,1)S(1)}, bf16[128,1024]{1,0:T(8,128)(2,1)S(1)}, u32[]{:S(2)}, u32[]{:S(2)}) collective-permute-start(bf16[128,1024]{1,0:T(8,128)(2,1)S(1)} %get-tuple-element.62), channel_id=1, source_target_pairs={{0,4},{2,6},{4,0},{6,2},{8,12},{10,14},{12,8},{14,10},{1,5},{3,7},... | collective-permute-start | bytes 786440 | tf_op jit(solution)/shard_map/ppermute | solution.py:218
  60.2 2.0 %collective-permute-start.30 = (bf16[128,1024]{1,0:T(8,128)(2,1)S(1)}, bf16[128,1024]{1,0:T(8,128)(2,1)S(1)}, u32[]{:S(2)}, u32[]{:S(2)}) collective-permute-start(bf16[128,1024]{1,0:T(8,128)(2,1)S(1)} %get-tuple-element.64), channel_id=1, source_target_pairs={{0,8},{2,10},{4,12},{6,14},{8,0},{10,2},{12,4},{14,6},{1,9},{3,11}... | collective-permute-start | bytes 786440 | tf_op jit(solution)/shard_map/ppermute | solution.py:218
  62.2 2.1 %bias_rows.2 = f32[16,64]{1,0:T(8,128)S(1)} custom-call(bf16[64,128,1024]{2,1,0:T(8,128)(2,1)S(1)} %copy-done.1, f32[1,64]{1,0:T(1,128)S(1)} %get-tuple-element.70.noise_ref, bf16[128,384]{1,0:T(8,128)(2,1)S(1)} %get-tuple-element.36.refs_0_, bf16[128,384]{1,0:T(8,128)(2,1)S(1)} %collective-permute-done.refs_1_, ...), custom_call_target="tpu_custom_call" | custom-call | flops 805306368 | bytes 7077888 | tf_op jit(solution)/shard_map/bias_rows/pallas_call | solution.py:107
  65.3 2.7 %collective-permute-done.7 = f32[16,64]{1,0:T(8,128)S(1)} collective-permute-done((f32[16,64]{1,0:T(8,128)S(1)}, f32[16,64]{1,0:T(8,128)S(1)}, u32[]{:S(2)}, u32[]{:S(2)}) %collective-permute-start.7) | collective-permute-done | bytes 4128 | tf_op jit(solution)/shard_map/ppermute | solution.py:218
  68.1 7.8 %collective-permute-done.8 = f32[16,64]{1,0:T(8,128)S(1)} collective-permute-done((f32[16,64]{1,0:T(8,128)S(1)}, f32[16,64]{1,0:T(8,128)S(1)}, u32[]{:S(2)}, u32[]{:S(2)}) %collective-permute-start.8) | collective-permute-done | bytes 4128 | tf_op jit(solution)/shard_map/ppermute | solution.py:218
  75.9 4.7 %collective-permute-done.9 = f32[16,64]{1,0:T(8,128)S(1)} collective-permute-done((f32[16,64]{1,0:T(8,128)S(1)}, f32[16,64]{1,0:T(8,128)S(1)}, u32[]{:S(2)}, u32[]{:S(2)}) %collective-permute-start.9) | collective-permute-done | bytes 4128 | tf_op jit(solution)/shard_map/ppermute | solution.py:218
  80.7 3.4 %potential_rows.2 = (bf16[128,1024]{1,0:T(8,128)(2,1)S(1)}, bf16[128,1024]{1,0:T(8,128)(2,1)}, bf16[128,1024]{1,0:T(8,128)(2,1)}, bf16[128,1024]{1,0:T(8,128)(2,...) custom-call(f32[16,64]{1,0:T(8,128)S(1)} %add.40.sums_ref, ...), custom_call_target="tpu_custom_call" | custom-call | flops 2147483648 | bytes 18874368 | tf_op jit(solution)/shard_map/potential_rows/pallas_call | solution.py:147
  88.3 2.7 %collective-permute-start.32 = (bf16[128,1024]{1,0:T(8,128)(2,1)S(1)}, bf16[128,1024]{1,0:T(8,128)(2,1)}, u32[]{:S(2)}, u32[]{:S(2)}) collective-permute-start(bf16[128,1024]{1,0:T(8,128)(2,1)S(1)} %get-tuple-element.66), channel_id=1, source_target_pairs={{0,12},{2,14},{4,8},{6,10},{8,4},{10,6},{12,0},{14,2},{1,13},{3,15... | collective-permute-start | bytes 786440 | tf_op jit(solution)/shard_map/ppermute | solution.py:218
  91.0 4.0 %collective-permute-start.33 = (bf16[128,1024]{1,0:T(8,128)(2,1)S(1)}, bf16[128,1024]{1,0:T(8,128)(2,1)}, u32[]{:S(2)}, u32[]{:S(2)}) collective-permute-start(bf16[128,1024]{1,0:T(8,128)(2,1)S(1)} %get-tuple-element.67), channel_id=1, source_target_pairs={{0,14},{2,12},{4,10},{6,8},{8,6},{10,4},{12,2},{14,0},{1,15},{3,13... | collective-permute-start | bytes 786440 | tf_op jit(solution)/shard_map/ppermute | solution.py:218
  95.5 2.3 %collective-permute-start.11 = (bf16[128,1024]{1,0:T(8,128)(2,1)}, bf16[128,1024]{1,0:T(8,128)(2,1)}, u32[]{:S(2)}, u32[]{:S(2)}) collective-permute-start(bf16[128,1024]{1,0:T(8,128)(2,1)} %get-tuple-element.46), channel_id=1, source_target_pairs={{0,4},{2,6},{4,0},{6,2},{8,12},{10,14},{12,8},{14,10},{1,5},{3,7},... | collective-permute-start | bytes 786440 | tf_op jit(solution)/shard_map/ppermute | solution.py:218
  98.9 1.8 %pad_maximum_fusion.1 = f32[2]{0:T(128)} fusion(f32[1]{0:T(128)} %bitcast.1, f32[1]{0:T(128)} %bitcast), kind=kLoop, calls=%fused_computation.7 | loop fusion | flops 2 | bytes 16 | tf_op jit(solution)/shard_map/concatenate | solution.py:247
  100.7 4.2 %collective-permute-start.12 = (bf16[128,1024]{1,0:T(8,128)(2,1)}, bf16[128,1024]{1,0:T(8,128)(2,1)S(1)}, u32[]{:S(2)}, u32[]{:S(2)}) collective-permute-start(bf16[128,1024]{1,0:T(8,128)(2,1)} %copy-done.12), channel_id=1, source_target_pairs={{0,6},{2,4},{4,2},{6,0},{8,14},{10,12},{12,10},{14,8},{1,7},{3,5},... | collective-permute-start | bytes 786440 | tf_op jit(solution)/shard_map/ppermute | solution.py:218
  104.9 5.7 %collective-permute-done.32.refs_6_ = bf16[128,1024]{1,0:T(8,128)(2,1)} collective-permute-done((bf16[128,1024]{1,0:T(8,128)(2,1)S(1)}, bf16[128,1024]{1,0:T(8,128)(2,1)}, u32[]{:S(2)}, u32[]{:S(2)}) %collective-permute-start.32) | collective-permute-done | bytes 262176 | tf_op jit(solution)/shard_map/ppermute | solution.py:218
  110.6 20.8 %collective-permute-done.33.refs_7_ = bf16[128,1024]{1,0:T(8,128)(2,1)} collective-permute-done((bf16[128,1024]{1,0:T(8,128)(2,1)S(1)}, bf16[128,1024]{1,0:T(8,128)(2,1)}, u32[]{:S(2)}, u32[]{:S(2)}) %collective-permute-start.33) | collective-permute-done | bytes 262176 | tf_op jit(solution)/shard_map/ppermute | solution.py:218
  131.6 5.8 %taylor.3 = bf16[1,1024,384]{2,1,0:T(8,128)(2,1)S(1)} custom-call(bf16[128,1024]{1,0:T(8,128)(2,1)S(1)} %get-tuple-element.60.refs_0_, bf16[128,1024]{1,0:T(8,128)(2,1)S(1)} %collective-permute-done.27.refs_1_, bf16[128,1024]{1,0:T(8,128)(2,1)S(1)} %collective-permute-done.28.refs_2_, bf16[128,1024]{1,0:T(8,128)(2,1)S(1)} %collective-permute-done.29.refs_3_, ...), custom_call_target="tpu_custom_call" | custom-call | flops 3221225472 | bytes 3670016 | tf_op jit(solution)/shard_map/taylor/pallas_call | solution.py:194
  137.4 9.6 %collective-permute-done.14.refs_5_ = bf16[128,1024]{1,0:T(8,128)(2,1)S(1)} collective-permute-done((bf16[128,1024]{1,0:T(8,128)(2,1)}, bf16[128,1024]{1,0:T(8,128)(2,1)S(1)}, u32[]{:S(2)}, u32[]{:S(2)}) %collective-permute-start.14) | collective-permute-done | bytes 262176 | tf_op jit(solution)/shard_map/ppermute | solution.py:218
  147.0 8.4 %collective-permute-done.15.refs_6_ = bf16[128,1024]{1,0:T(8,128)(2,1)S(1)} collective-permute-done((bf16[128,1024]{1,0:T(8,128)(2,1)}, bf16[128,1024]{1,0:T(8,128)(2,1)S(1)}, u32[]{:S(2)}, u32[]{:S(2)}) %collective-permute-start.15) | collective-permute-done | bytes 262176 | tf_op jit(solution)/shard_map/ppermute | solution.py:218
  155.5 4.3 %collective-permute-done.16.refs_7_ = bf16[128,1024]{1,0:T(8,128)(2,1)S(1)} collective-permute-done((bf16[128,1024]{1,0:T(8,128)(2,1)}, bf16[128,1024]{1,0:T(8,128)(2,1)S(1)}, u32[]{:S(2)}, u32[]{:S(2)}) %collective-permute-start.16) | collective-permute-done | bytes 262176 | tf_op jit(solution)/shard_map/ppermute | solution.py:218
  159.7 5.6 %taylor.2 = bf16[1,1024,384]{2,1,0:T(8,128)(2,1)S(1)} custom-call(bf16[128,1024]{1,0:T(8,128)(2,1)S(1)} %copy-done.7, bf16[128,1024]{1,0:T(8,128)(2,1)} %collective-permute-done.10.refs_1_, bf16[128,1024]{1,0:T(8,128)(2,1)} %collective-permute-done.11.refs_2_, bf16[128,1024]{1,0:T(8,128)(2,1)S(1)} %collective-permute-done.12.refs_3_, ...), custom_call_target="tpu_custom_call" | custom-call | flops 3221225472 | bytes 3670016 | tf_op jit(solution)/shard_map/taylor/pallas_call | solution.py:194
  (86 shorter events, 25.0 us)
Async XLA Ops:
  3.5 13.1 %collective-permute-start.20 = (bf16[128,384]{1,0:T(8,128)(2,1)S(1)}, bf16[128,384]{1,0:T(8,128)(2,1)S(1)}, u32[]{:S(2)}, u32[]{:S(2)}) collective-permute-start(bf16[128,384]{1,0:T(8,128)(2,1)S(1)} %get-tuple-element.56), channel_id=1, source_target_pairs={{0,8},{2,10},{4,12},{6,14},{8,0},{10,2},{12,4},{14,6},{1,9},{3,11}... | collective-permute-start | bytes 294920 | tf_op jit(solution)/shard_map/ppermute | solution.py:218
  6.2 12.6 %collective-permute-start.21 = (bf16[128,384]{1,0:T(8,128)(2,1)S(1)}, bf16[128,384]{1,0:T(8,128)(2,1)S(1)}, u32[]{:S(2)}, u32[]{:S(2)}) collective-permute-start(bf16[128,384]{1,0:T(8,128)(2,1)S(1)} %get-tuple-element.57), channel_id=1, source_target_pairs={{0,10},{2,8},{4,14},{6,12},{8,2},{10,0},{12,6},{14,4},{1,11},{3,9}... | collective-permute-start | bytes 294920 | tf_op jit(solution)/shard_map/ppermute | solution.py:218
  7.5 14.7 %collective-permute-start.22 = (bf16[128,384]{1,0:T(8,128)(2,1)S(1)}, bf16[128,384]{1,0:T(8,128)(2,1)S(1)}, u32[]{:S(2)}, u32[]{:S(2)}) collective-permute-start(bf16[128,384]{1,0:T(8,128)(2,1)S(1)} %get-tuple-element.58), channel_id=1, source_target_pairs={{0,12},{2,14},{4,8},{6,10},{8,4},{10,6},{12,0},{14,2},{1,13},{3,15... | collective-permute-start | bytes 294920 | tf_op jit(solution)/shard_map/ppermute | solution.py:218
  9.0 15.7 %collective-permute-start.23 = (bf16[128,384]{1,0:T(8,128)(2,1)S(1)}, bf16[128,384]{1,0:T(8,128)(2,1)S(1)}, u32[]{:S(2)}, u32[]{:S(2)}) collective-permute-start(bf16[128,384]{1,0:T(8,128)(2,1)S(1)} %get-tuple-element.59), channel_id=1, source_target_pairs={{0,14},{2,12},{4,10},{6,8},{8,6},{10,4},{12,2},{14,0},{1,15},{3,13... | collective-permute-start | bytes 294920 | tf_op jit(solution)/shard_map/ppermute | solution.py:218
  9.9 16.4 %collective-permute-start.17 = (bf16[128,384]{1,0:T(8,128)(2,1)S(1)}, bf16[128,384]{1,0:T(8,128)(2,1)S(1)}, u32[]{:S(2)}, u32[]{:S(2)}) collective-permute-start(bf16[128,384]{1,0:T(8,128)(2,1)S(1)} %get-tuple-element.53), channel_id=1, source_target_pairs={{0,2},{2,0},{4,6},{6,4},{8,10},{10,8},{12,14},{14,12},{1,3},{3,1},... | collective-permute-start | bytes 294920 | tf_op jit(solution)/shard_map/ppermute | solution.py:218
  16.6 9.6 %collective-permute-start.18 = (bf16[128,384]{1,0:T(8,128)(2,1)S(1)}, bf16[128,384]{1,0:T(8,128)(2,1)S(1)}, u32[]{:S(2)}, u32[]{:S(2)}) collective-permute-start(bf16[128,384]{1,0:T(8,128)(2,1)S(1)} %get-tuple-element.54), channel_id=1, source_target_pairs={{0,4},{2,6},{4,0},{6,2},{8,12},{10,14},{12,8},{14,10},{1,5},{3,7},... | collective-permute-start | bytes 294920 | tf_op jit(solution)/shard_map/ppermute | solution.py:218
  18.8 7.5 %collective-permute-start.19 = (bf16[128,384]{1,0:T(8,128)(2,1)S(1)}, bf16[128,384]{1,0:T(8,128)(2,1)S(1)}, u32[]{:S(2)}, u32[]{:S(2)}) collective-permute-start(bf16[128,384]{1,0:T(8,128)(2,1)S(1)} %get-tuple-element.55), channel_id=1, source_target_pairs={{0,6},{2,4},{4,2},{6,0},{8,14},{10,12},{12,10},{14,8},{1,7},{3,5},... | collective-permute-start | bytes 294920 | tf_op jit(solution)/shard_map/ppermute | solution.py:218
  22.1 27.4 %collective-permute-start.3 = (bf16[128,384]{1,0:T(8,128)(2,1)S(1)}, bf16[128,384]{1,0:T(8,128)(2,1)S(1)}, u32[]{:S(2)}, u32[]{:S(2)}) collective-permute-start(bf16[128,384]{1,0:T(8,128)(2,1)S(1)} %get-tuple-element.40), channel_id=1, source_target_pairs={{0,8},{2,10},{4,12},{6,14},{8,0},{10,2},{12,4},{14,6},{1,9},{3,11}... | collective-permute-start | bytes 294920 | tf_op jit(solution)/shard_map/ppermute | solution.py:218
  24.7 28.7 %collective-permute-start.4 = (bf16[128,384]{1,0:T(8,128)(2,1)S(1)}, bf16[128,384]{1,0:T(8,128)(2,1)S(1)}, u32[]{:S(2)}, u32[]{:S(2)}) collective-permute-start(bf16[128,384]{1,0:T(8,128)(2,1)S(1)} %get-tuple-element.41), channel_id=1, source_target_pairs={{0,10},{2,8},{4,14},{6,12},{8,2},{10,0},{12,6},{14,4},{1,11},{3,9}... | collective-permute-start | bytes 294920 | tf_op jit(solution)/shard_map/ppermute | solution.py:218
  37.8 6.3 %collective-permute-start.25 = (f32[16,64]{1,0:T(8,128)S(1)}, f32[16,64]{1,0:T(8,128)S(1)}, u32[]{:S(2)}, u32[]{:S(2)}) collective-permute-start(f32[16,64]{1,0:T(8,128)S(1)} %add.41), channel_id=1, source_target_pairs={{0,4},{2,6},{4,0},{6,2},{8,12},{10,14},{12,8},{14,10},{1,5},{3,7},... | collective-permute-start | bytes 12296 | tf_op jit(solution)/shard_map/ppermute | solution.py:218
  40.6 16.1 %collective-permute-start.5 = (bf16[128,384]{1,0:T(8,128)(2,1)S(1)}, bf16[128,384]{1,0:T(8,128)(2,1)S(1)}, u32[]{:S(2)}, u32[]{:S(2)}) collective-permute-start(bf16[128,384]{1,0:T(8,128)(2,1)S(1)} %get-tuple-element.42), channel_id=1, source_target_pairs={{0,12},{2,14},{4,8},{6,10},{8,4},{10,6},{12,0},{14,2},{1,13},{3,15... | collective-permute-start | bytes 294920 | tf_op jit(solution)/shard_map/ppermute | solution.py:218
  41.8 16.4 %collective-permute-start.6 = (bf16[128,384]{1,0:T(8,128)(2,1)S(1)}, bf16[128,384]{1,0:T(8,128)(2,1)S(1)}, u32[]{:S(2)}, u32[]{:S(2)}) collective-permute-start(bf16[128,384]{1,0:T(8,128)(2,1)S(1)} %get-tuple-element.43), channel_id=1, source_target_pairs={{0,14},{2,12},{4,10},{6,8},{8,6},{10,4},{12,2},{14,0},{1,15},{3,13... | collective-permute-start | bytes 294920 | tf_op jit(solution)/shard_map/ppermute | solution.py:218
  44.1 4.7 %collective-permute-start.26 = (f32[16,64]{1,0:T(8,128)S(1)}, f32[16,64]{1,0:T(8,128)S(1)}, u32[]{:S(2)}, u32[]{:S(2)}) collective-permute-start(f32[16,64]{1,0:T(8,128)S(1)} %add.42), channel_id=1, source_target_pairs={{0,8},{2,10},{4,12},{6,14},{8,0},{10,2},{12,4},{14,6},{1,9},{3,11}... | collective-permute-start | bytes 12296 | tf_op jit(solution)/shard_map/ppermute | solution.py:218
  48.8 11.4 %collective-permute-start = (bf16[128,384]{1,0:T(8,128)(2,1)S(1)}, bf16[128,384]{1,0:T(8,128)(2,1)S(1)}, u32[]{:S(2)}, u32[]{:S(2)}) collective-permute-start(bf16[128,384]{1,0:T(8,128)(2,1)S(1)} %get-tuple-element.37), channel_id=1, source_target_pairs={{0,2},{2,0},{4,6},{6,4},{8,10},{10,8},{12,14},{14,12},{1,3},{3,1},... | collective-permute-start | bytes 294920 | tf_op jit(solution)/shard_map/ppermute | solution.py:218
  49.5 10.7 %collective-permute-start.1 = (bf16[128,384]{1,0:T(8,128)(2,1)S(1)}, bf16[128,384]{1,0:T(8,128)(2,1)S(1)}, u32[]{:S(2)}, u32[]{:S(2)}) collective-permute-start(bf16[128,384]{1,0:T(8,128)(2,1)S(1)} %get-tuple-element.38), channel_id=1, source_target_pairs={{0,4},{2,6},{4,0},{6,2},{8,12},{10,14},{12,8},{14,10},{1,5},{3,7},... | collective-permute-start | bytes 294920 | tf_op jit(solution)/shard_map/ppermute | solution.py:218
  53.4 8.8 %collective-permute-start.2 = (bf16[128,384]{1,0:T(8,128)(2,1)S(1)}, bf16[128,384]{1,0:T(8,128)(2,1)S(1)}, u32[]{:S(2)}, u32[]{:S(2)}) collective-permute-start(bf16[128,384]{1,0:T(8,128)(2,1)S(1)} %get-tuple-element.39), channel_id=1, source_target_pairs={{0,6},{2,4},{4,2},{6,0},{8,14},{10,12},{12,10},{14,8},{1,7},{3,5},... | collective-permute-start | bytes 294920 | tf_op jit(solution)/shard_map/ppermute | solution.py:218
  56.7 31.5 %collective-permute-start.27 = (bf16[128,1024]{1,0:T(8,128)(2,1)S(1)}, bf16[128,1024]{1,0:T(8,128)(2,1)S(1)}, u32[]{:S(2)}, u32[]{:S(2)}) collective-permute-start(bf16[128,1024]{1,0:T(8,128)(2,1)S(1)} %get-tuple-element.61), channel_id=1, source_target_pairs={{0,2},{2,0},{4,6},{6,4},{8,10},{10,8},{12,14},{14,12},{1,3},{3,1},... | collective-permute-start | bytes 786440 | tf_op jit(solution)/shard_map/ppermute | solution.py:218
  58.3 32.7 %collective-permute-start.28 = (bf16[128,1024]{1,0:T(8,128)(2,1)S(1)}, bf16[128,1024]{1,0:T(8,128)(2,1)S(1)}, u32[]{:S(2)}, u32[]{:S(2)}) collective-permute-start(bf16[128,1024]{1,0:T(8,128)(2,1)S(1)} %get-tuple-element.62), channel_id=1, source_target_pairs={{0,4},{2,6},{4,0},{6,2},{8,12},{10,14},{12,8},{14,10},{1,5},{3,7},... | collective-permute-start | bytes 786440 | tf_op jit(solution)/shard_map/ppermute | solution.py:218
  60.2 34.8 %collective-permute-start.29 = (bf16[128,1024]{1,0:T(8,128)(2,1)S(1)}, bf16[128,1024]{1,0:T(8,128)(2,1)S(1)}, u32[]{:S(2)}, u32[]{:S(2)}) collective-permute-start(bf16[128,1024]{1,0:T(8,128)(2,1)S(1)} %get-tuple-element.63), channel_id=1, source_target_pairs={{0,6},{2,4},{4,2},{6,0},{8,14},{10,12},{12,10},{14,8},{1,7},{3,5},... | collective-permute-start | bytes 786440 | tf_op jit(solution)/shard_map/ppermute | solution.py:218
  60.2 35.3 %collective-permute-start.30 = (bf16[128,1024]{1,0:T(8,128)(2,1)S(1)}, bf16[128,1024]{1,0:T(8,128)(2,1)S(1)}, u32[]{:S(2)}, u32[]{:S(2)}) collective-permute-start(bf16[128,1024]{1,0:T(8,128)(2,1)S(1)} %get-tuple-element.64), channel_id=1, source_target_pairs={{0,8},{2,10},{4,12},{6,14},{8,0},{10,2},{12,4},{14,6},{1,9},{3,11}... | collective-permute-start | bytes 786440 | tf_op jit(solution)/shard_map/ppermute | solution.py:218
  68.1 7.9 %collective-permute-start.8 = (f32[16,64]{1,0:T(8,128)S(1)}, f32[16,64]{1,0:T(8,128)S(1)}, u32[]{:S(2)}, u32[]{:S(2)}) collective-permute-start(f32[16,64]{1,0:T(8,128)S(1)} %add.38), channel_id=1, source_target_pairs={{0,4},{2,6},{4,0},{6,2},{8,12},{10,14},{12,8},{14,10},{1,5},{3,7},... | collective-permute-start | bytes 12296 | tf_op jit(solution)/shard_map/ppermute | solution.py:218
  75.9 4.7 %collective-permute-start.9 = (f32[16,64]{1,0:T(8,128)S(1)}, f32[16,64]{1,0:T(8,128)S(1)}, u32[]{:S(2)}, u32[]{:S(2)}) collective-permute-start(f32[16,64]{1,0:T(8,128)S(1)} %add.39), channel_id=1, source_target_pairs={{0,8},{2,10},{4,12},{6,14},{8,0},{10,2},{12,4},{14,6},{1,9},{3,11}... | collective-permute-start | bytes 12296 | tf_op jit(solution)/shard_map/ppermute | solution.py:218
  80.7 20.1 %collective-permute-start.31 = (bf16[128,1024]{1,0:T(8,128)(2,1)}, bf16[128,1024]{1,0:T(8,128)(2,1)}, u32[]{:S(2)}, u32[]{:S(2)}) collective-permute-start(bf16[128,1024]{1,0:T(8,128)(2,1)} %get-tuple-element.65), channel_id=1, source_target_pairs={{0,10},{2,8},{4,14},{6,12},{8,2},{10,0},{12,6},{14,4},{1,11},{3,9}... | collective-permute-start | bytes 786440 | tf_op jit(solution)/shard_map/ppermute | solution.py:218
  88.3 22.4 %collective-permute-start.32 = (bf16[128,1024]{1,0:T(8,128)(2,1)S(1)}, bf16[128,1024]{1,0:T(8,128)(2,1)}, u32[]{:S(2)}, u32[]{:S(2)}) collective-permute-start(bf16[128,1024]{1,0:T(8,128)(2,1)S(1)} %get-tuple-element.66), channel_id=1, source_target_pairs={{0,12},{2,14},{4,8},{6,10},{8,4},{10,6},{12,0},{14,2},{1,13},{3,15... | collective-permute-start | bytes 786440 | tf_op jit(solution)/shard_map/ppermute | solution.py:218
  91.0 40.5 %collective-permute-start.33 = (bf16[128,1024]{1,0:T(8,128)(2,1)S(1)}, bf16[128,1024]{1,0:T(8,128)(2,1)}, u32[]{:S(2)}, u32[]{:S(2)}) collective-permute-start(bf16[128,1024]{1,0:T(8,128)(2,1)S(1)} %get-tuple-element.67), channel_id=1, source_target_pairs={{0,14},{2,12},{4,10},{6,8},{8,6},{10,4},{12,2},{14,0},{1,15},{3,13... | collective-permute-start | bytes 786440 | tf_op jit(solution)/shard_map/ppermute | solution.py:218
  95.0 36.5 %collective-permute-start.10 = (bf16[128,1024]{1,0:T(8,128)(2,1)}, bf16[128,1024]{1,0:T(8,128)(2,1)}, u32[]{:S(2)}, u32[]{:S(2)}) collective-permute-start(bf16[128,1024]{1,0:T(8,128)(2,1)} %get-tuple-element.45), channel_id=1, source_target_pairs={{0,2},{2,0},{4,6},{6,4},{8,10},{10,8},{12,14},{14,12},{1,3},{3,1},... | collective-permute-start | bytes 786440 | tf_op jit(solution)/shard_map/ppermute | solution.py:218
  95.5 36.0 %collective-permute-start.11 = (bf16[128,1024]{1,0:T(8,128)(2,1)}, bf16[128,1024]{1,0:T(8,128)(2,1)}, u32[]{:S(2)}, u32[]{:S(2)}) collective-permute-start(bf16[128,1024]{1,0:T(8,128)(2,1)} %get-tuple-element.46), channel_id=1, source_target_pairs={{0,4},{2,6},{4,0},{6,2},{8,12},{10,14},{12,8},{14,10},{1,5},{3,7},... | collective-permute-start | bytes 786440 | tf_op jit(solution)/shard_map/ppermute | solution.py:218
  100.7 36.7 %collective-permute-start.12 = (bf16[128,1024]{1,0:T(8,128)(2,1)}, bf16[128,1024]{1,0:T(8,128)(2,1)S(1)}, u32[]{:S(2)}, u32[]{:S(2)}) collective-permute-start(bf16[128,1024]{1,0:T(8,128)(2,1)} %copy-done.12), channel_id=1, source_target_pairs={{0,6},{2,4},{4,2},{6,0},{8,14},{10,12},{12,10},{14,8},{1,7},{3,5},... | collective-permute-start | bytes 786440 | tf_op jit(solution)/shard_map/ppermute | solution.py:218
  110.6 26.8 %collective-permute-start.13 = (bf16[128,1024]{1,0:T(8,128)(2,1)}, bf16[128,1024]{1,0:T(8,128)(2,1)S(1)}, u32[]{:S(2)}, u32[]{:S(2)}) collective-permute-start(bf16[128,1024]{1,0:T(8,128)(2,1)} %copy-done.11), channel_id=1, source_target_pairs={{0,8},{2,10},{4,12},{6,14},{8,0},{10,2},{12,4},{14,6},{1,9},{3,11}... | collective-permute-start | bytes 786440 | tf_op jit(solution)/shard_map/ppermute | solution.py:218
  131.5 15.6 %collective-permute-start.14 = (bf16[128,1024]{1,0:T(8,128)(2,1)}, bf16[128,1024]{1,0:T(8,128)(2,1)S(1)}, u32[]{:S(2)}, u32[]{:S(2)}) collective-permute-start(bf16[128,1024]{1,0:T(8,128)(2,1)} %copy-done.10), channel_id=1, source_target_pairs={{0,10},{2,8},{4,14},{6,12},{8,2},{10,0},{12,6},{14,4},{1,11},{3,9}... | collective-permute-start | bytes 786440 | tf_op jit(solution)/shard_map/ppermute | solution.py:218
  131.5 24.0 %collective-permute-start.15 = (bf16[128,1024]{1,0:T(8,128)(2,1)}, bf16[128,1024]{1,0:T(8,128)(2,1)S(1)}, u32[]{:S(2)}, u32[]{:S(2)}) collective-permute-start(bf16[128,1024]{1,0:T(8,128)(2,1)} %copy-done.9), channel_id=1, source_target_pairs={{0,12},{2,14},{4,8},{6,10},{8,4},{10,6},{12,0},{14,2},{1,13},{3,15... | collective-permute-start | bytes 786440 | tf_op jit(solution)/shard_map/ppermute | solution.py:218
  131.5 28.2 %collective-permute-start.16 = (bf16[128,1024]{1,0:T(8,128)(2,1)}, bf16[128,1024]{1,0:T(8,128)(2,1)S(1)}, u32[]{:S(2)}, u32[]{:S(2)}) collective-permute-start(bf16[128,1024]{1,0:T(8,128)(2,1)} %copy-done.8), channel_id=1, source_target_pairs={{0,14},{2,12},{4,10},{6,8},{8,6},{10,4},{12,2},{14,0},{1,15},{3,13... | collective-permute-start | bytes 786440 | tf_op jit(solution)/shard_map/ppermute | solution.py:218
  (16 other events, 114.2 us)

commit v3 on v2

v3 whole, which is shorter than its diff:
```python
import functools
import math

import jax
import jax.numpy as jnp
from jax import lax
from jax.experimental import pallas as pl
from jax.experimental.pallas import tpu as pltpu
from jax.sharding import PartitionSpec as P

NOISE_LEVELS = 65536


STEP_ROOT = 0.1
BIAS_CAP = 1.0
ROOT_TWO = 1.4142135623730951
DEGREES = 4
PLANE = ("wa", "col")
ROWS = 16
MOST_PERMUTES = 8
VMEM = 16 * 1024 * 1024
IN_VMEM = pl.BlockSpec(memory_space=pltpu.VMEM)
IN_HBM = pl.BlockSpec(memory_space=pltpu.HBM)
IN_ANY = pl.BlockSpec(memory_space=pl.ANY)


NO_COST = pl.CostEstimate(flops=0, bytes_accessed=0, transcendentals=0)


def kernel_params():
    return pltpu.CompilerParams(vmem_limit_bytes=VMEM)


def quantile(codes):
    level = (codes.astype(jnp.float32) + 0.5) / NOISE_LEVELS
    return ROOT_TWO * lax.erf_inv(2.0 * level - 1.0)


def shifted_field(bias_sum, noise):
    force_bias = jnp.clip(STEP_ROOT * bias_sum, -BIAS_CAP, BIAS_CAP)
    shifted = noise - force_bias
    return shifted, shifted * force_bias - 0.5 * force_bias * force_bias


def iota(shape, dimension):
    return lax.broadcasted_iota(jnp.int32, shape, dimension)


def own_place():
    return lax.axis_index("wa") * lax.axis_size("col") + lax.axis_index("col")


def in_hbm(array):
    return pltpu.with_memory_space_constraint(array, pltpu.HBM)


def device_at(place, relative):
    return jnp.bitwise_xor(own_place(), place) if relative else place


def green_kernel(k, groups, relative, walker_ref, inverse_ref, _, *refs):
    outs, (rows_in, inverse_in, arrived) = refs[: len(groups)], refs[len(groups) :]
    tile_rows = rows_in.shape[1]
    copies = [pltpu.make_async_copy(inverse_ref.at[k], inverse_in, arrived.at[0])]
    places = [place for place in sum(groups, ()) if place is not None]
    for i, place in enumerate(places):
        start = pl.multiple_of(device_at(place, relative) * tile_rows, tile_rows)
        copies.append(
            pltpu.make_async_copy(
                walker_ref.at[k, pl.ds(start, tile_rows), :], rows_in.at[i], arrived.at[i + 1]
            )
        )
    for copy in copies:
        copy.start()
    for copy in copies:
        copy.wait()
    rows = rows_in[...].reshape(-1, rows_in.shape[2])
    product = jnp.dot(rows, inverse_in[...], preferred_element_type=jnp.float32).astype(jnp.bfloat16)
    i = 0
    for group, out_ref in zip(groups, outs):
        for j, place in enumerate(group):
            if place is not None:
                out_ref[j] = product[i * tile_rows : (i + 1) * tile_rows, :]
                i += 1


def green_rows(walkers, inverses, k, tile_rows, groups, relative, after):
    _, orbitals, electrons = walkers.shape
    count = sum(place is not None for group in groups for place in group)
    return pl.pallas_call(
        functools.partial(green_kernel, k, groups, relative),
        in_specs=[IN_HBM, IN_HBM, IN_ANY],
        out_specs=[IN_VMEM] * len(groups),
        out_shape=[jax.ShapeDtypeStruct((len(group), tile_rows, electrons), jnp.bfloat16) for group in groups],
        scratch_shapes=[
            pltpu.VMEM((count, tile_rows, electrons), jnp.bfloat16),
            pltpu.VMEM((electrons, electrons), jnp.bfloat16),
            pltpu.SemaphoreType.DMA((count + 1,)),
        ],
        compiler_params=kernel_params(),
        cost_estimate=NO_COST,
        name="green_rows",
    )(in_hbm(walkers), in_hbm(inverses), after)


def load_kernel(chol_ref, _, held_ref, arrived):
    step = chol_ref.shape[0] // arrived.shape[0]
    copies = [
        pltpu.make_async_copy(chol_ref.at[pl.ds(i * step, step)], held_ref.at[pl.ds(i * step, step)], arrived.at[i])
        for i in range(arrived.shape[0])
    ]
    for copy in copies:
        copy.start()
    for copy in copies:
        copy.wait()


def load(cholesky, after):
    return pl.pallas_call(
        load_kernel,
        in_specs=[IN_HBM, IN_ANY],
        out_specs=IN_VMEM,
        out_shape=pltpu.VMEM(cholesky.shape, cholesky.dtype),
        scratch_shapes=[pltpu.SemaphoreType.DMA((math.gcd(cholesky.shape[0], 8),))],
        compiler_params=kernel_params(),
        cost_estimate=NO_COST,
        name="load_cholesky",
    )(in_hbm(cholesky), after)


def bias_kernel(where, relative, chol_ref, noise_ref, *refs):
    greens, out_ref = refs[:-1], refs[-1]
    count = len(where)
    vectors, tile_rows, _ = chol_ref.shape
    electrons = greens[0].shape[2]
    me = own_place()
    total = jnp.zeros((vectors * ROWS, count * ROWS), jnp.float32)
    for start in range(0, tile_rows, ROWS):
        green = jnp.concatenate([greens[i][j, start : start + ROWS, :] for i, j in where], axis=0)
        tile = chol_ref[:, start : start + ROWS, :electrons].reshape(vectors * ROWS, electrons)
        total += lax.dot_general(tile, green, (((1,), (1,)), ((), ())), preferred_element_type=jnp.float32)
    total = total.reshape(vectors, ROWS, count * ROWS)
    same = iota(total.shape, 1) == iota(total.shape, 2) % ROWS
    summed = jnp.sum(jnp.where(same, total, 0.0), axis=1)
    shape = (count, count * ROWS)
    source = iota(shape, 1) // ROWS
    fold = (jnp.bitwise_xor(source, me) if relative else source) == iota(shape, 0)
    out_ref[:count, :] = lax.dot_general(
        fold.astype(jnp.float32),
        summed,
        (((1,), (1,)), ((), ())),
        preferred_element_type=jnp.float32,
        precision=lax.Precision.HIGHEST,
    )
    out_ref[count:, :] = jnp.where(iota((count, vectors), 0) == me, noise_ref[...], 0.0)


def bias_rows(cholesky, noise, greens, where, relative):
    vectors, tile_rows, _ = cholesky.shape
    count, electrons = len(where), greens[0].shape[2]
    return pl.pallas_call(
        functools.partial(bias_kernel, where, relative),
        in_specs=[IN_VMEM] * (2 + len(greens)),
        out_specs=IN_VMEM,
        out_shape=jax.ShapeDtypeStruct((2 * count, vectors), jnp.float32),
        compiler_params=kernel_params(),
        cost_estimate=NO_COST,
        name="bias_rows",
    )(cholesky, noise, *greens)


def potential_kernel(groups, relative, parts, *refs):
    sums, chol_ref, outs, log_ref = refs[:parts], refs[parts], refs[parts + 2 : -1], refs[-1]
    places = [(place, out_ref, j) for group, out_ref in zip(groups, outs) for j, place in enumerate(group)]
    places = [slot for slot in places if slot[0] is not None]
    count = len(places)
    vectors, tile_rows, orbitals = chol_ref.shape
    totals = [ref[...] for ref in sums]
    total = totals[0] + sum(totals[2:], totals[1])
    shifted, log_terms = shifted_field(total[:count, :], total[count:, :])
    log_ref[...] = jnp.sum(log_terms, axis=1, keepdims=True)
    field = shifted.astype(jnp.bfloat16)
    if relative:
        order = jnp.bitwise_xor(iota((count, count), 0), own_place()) == iota((count, count), 1)
        field = jnp.dot(order.astype(jnp.bfloat16), field, preferred_element_type=jnp.float32).astype(jnp.bfloat16)
    widen = (iota((vectors, vectors * ROWS), 1) // ROWS == iota((vectors, vectors * ROWS), 0)).astype(jnp.bfloat16)
    wide = jnp.dot(field, widen, preferred_element_type=jnp.float32)
    shape = (count, ROWS, vectors * ROWS)
    spread = jnp.where(iota(shape, 1) == iota(shape, 2) % ROWS, wide[:, None, :], 0.0)
    spread = spread.reshape(count * ROWS, vectors * ROWS).astype(jnp.bfloat16)
    for start in range(0, tile_rows, ROWS):
        tile = chol_ref[:, start : start + ROWS, :].reshape(vectors * ROWS, orbitals)
        rows = jnp.dot(spread, tile, preferred_element_type=jnp.float32).astype(jnp.bfloat16)
        for place, out_ref, j in places:
            out_ref[j, start : start + ROWS, :] = rows[place * ROWS : (place + 1) * ROWS, :]


def potential_rows(sums, cholesky, groups, relative, after):
    vectors, tile_rows, orbitals = cholesky.shape
    count = sums[0].shape[0] // 2
    *blocks, log_steps = pl.pallas_call(
        functools.partial(potential_kernel, groups, relative, len(sums)),
        in_specs=[IN_VMEM] * (len(sums) + 1) + [IN_ANY],
        out_specs=[IN_VMEM] * (len(groups) + 1),
        out_shape=[
            *(jax.ShapeDtypeStruct((len(group), tile_rows, orbitals), jnp.bfloat16) for group in groups),
            jax.ShapeDtypeStruct((count, 1), jnp.float32),
        ],
        compiler_params=kernel_params(),
        cost_estimate=NO_COST,
        name="potential_rows",
    )(*sums, cholesky, after)
    return blocks, log_steps


def taylor_steps(potential, term, product_of):
    running = term.astype(jnp.float32)
    for degree in range(1, DEGREES + 1):
        product = (-STEP_ROOT / degree) * product_of(potential, term)
        running = running + product
        term = product.astype(jnp.bfloat16)
    return running.astype(jnp.bfloat16)


def taylor_kernel(k, where, relative, *refs):
    if relative:
        blocks, (walker_ref, _, _, out_ref, walker_in, result, arrived, held) = refs[:-8], refs[-8:]
    else:
        blocks, (walker_ref, _, _, out_ref, walker_in, result, arrived) = refs[:-7], refs[-7:]
        (held,) = blocks
    read = pltpu.make_async_copy(walker_ref.at[k], walker_in, arrived)
    read.start()
    if relative:
        for place, (i, j) in enumerate(where):
            held[device_at(place, relative)] = blocks[i][j]
    read.wait()
    orbitals = held.shape[2]
    result[...] = taylor_steps(
        held[...].reshape(orbitals, orbitals),
        walker_in[...],
        lambda a, b: jnp.dot(a, b, preferred_element_type=jnp.float32),
    )
    write = pltpu.make_async_copy(result, out_ref.at[k], arrived)
    write.start()
    write.wait()


def taylor(blocks, where, relative, walkers, k, new, after):
    _, orbitals, electrons = walkers.shape
    count, tile_rows = len(where), blocks[0].shape[1]
    held = [pltpu.VMEM((count, tile_rows, orbitals), jnp.bfloat16)] if relative else []
    return pl.pallas_call(
        functools.partial(taylor_kernel, k, where, relative),
        in_specs=[IN_VMEM] * len(blocks) + [IN_HBM, IN_HBM, IN_ANY],
        out_specs=IN_HBM,
        out_shape=jax.ShapeDtypeStruct(walkers.shape, jnp.bfloat16),
        scratch_shapes=[
            pltpu.VMEM((orbitals, electrons), jnp.bfloat16),
            pltpu.VMEM((orbitals, electrons), jnp.bfloat16),
            pltpu.SemaphoreType.DMA(()),
            *held,
        ],
        input_output_aliases={} if new is walkers else {len(blocks) + 1: 0},
        compiler_params=kernel_params(),
        cost_estimate=NO_COST,
        name="taylor",
    )(*blocks, in_hbm(walkers), in_hbm(new), after)


def swap(block, place):
    if place == 0:
        return block
    planes = lax.axis_size(PLANE)
    return lax.ppermute(block, PLANE, [(i, i ^ place) for i in range(planes)])


def join_kernel(moves, sources, *refs):
    outs, arrived = refs[-1 - (len(refs) - sources - 1) // 2 : -1], refs[-1]
    copies = [
        pltpu.make_async_copy(refs[i].at[pl.ds(j, 1)], outs[o].at[pl.ds(q, 1)], arrived.at[m])
        for m, ((i, j), (o, q)) in enumerate(moves)
    ]
    for copy in copies:
        copy.start()
    for copy in copies:
        copy.wait()


def join(sources, targets, moves):
    return pl.pallas_call(
        functools.partial(join_kernel, moves, len(sources)),
        in_specs=[IN_ANY] * (len(sources) + len(targets)),
        out_specs=[IN_ANY] * len(targets),
        out_shape=[jax.ShapeDtypeStruct(target.shape, target.dtype) for target in targets],
        input_output_aliases={len(sources) + i: i for i in range(len(targets))},
        scratch_shapes=[pltpu.SemaphoreType.DMA((len(moves),))],
        compiler_params=kernel_params(),
        cost_estimate=NO_COST,
        name="join",
    )(*sources, *targets)


def gate_kernel(*_):
    pass


def gate(block, *after):
    return pl.pallas_call(
        gate_kernel,
        in_specs=[IN_ANY] * (1 + len(after)),
        out_specs=IN_ANY,
        out_shape=jax.ShapeDtypeStruct(block.shape, block.dtype),
        input_output_aliases={0: 0},
        compiler_params=kernel_params(),
        name="gate",
    )(block, *after)


def staged_groups(along_wa, along_col):
    return (
        (0,),
        *(tuple(range(a * along_col, (a + 1) * along_col)) for a in range(1, along_wa)),
        *((c, *(None,) * (along_wa - 1)) for c in range(1, along_col)),
    )


def stage_along_wa(blocks, along_wa, along_col):
    passed = {a: swap(blocks[a], a * along_col) for a in reversed(range(1, along_wa))}
    return [passed[a] for a in range(1, along_wa)]


def stage_along_col(blocks, first, along_wa, along_col, after):
    second = blocks[along_wa:]
    if first and second:
        moves = tuple(((a - 1, c), (c - 1, a)) for a in range(1, along_wa) for c in range(1, along_col))
        second = join([*first, after], second, moves)
    second = [swap(block, c) for c, block in enumerate(second, 1)]
    where = tuple((along_wa + c - 1, a) if c else (a, 0) for a in range(along_wa) for c in range(along_col))
    return [blocks[0], *first, *second], where


def by_permutes(walkers, intersection_inverse, noise_index, cholesky):
    walker_count = walkers.shape[0]
    tile_rows = cholesky.shape[1]
    planes = lax.axis_size(PLANE)
    along_wa, along_col = lax.axis_size("wa"), lax.axis_size("col")
    half, half_wa = planes // 2, along_wa // 2
    far, near = tuple(range(half, planes)), tuple(range(half))
    early, late = far[:2], far[2:]
    noise = quantile(noise_index)
    direct = tuple((p,) for p in range(planes))
    staged = staged_groups(along_wa, along_col)
    staged_near = staged_groups(half_wa, along_col)

    def make_green(k, groups, after):
        return green_rows(walkers, intersection_inverse, k, tile_rows, groups, True, after)

    def ordered(received):
        places = (*far, *near)
        return [received[p] for p in places], tuple((places.index(p), 0) for p in range(planes))

    split = [(p,) for p in early], [(p,) for p in late]
    one = make_green(0, (*split[0], *staged_near[1:half_wa]), walkers)
    two = make_green(0, (*split[1], staged_near[0], *staged_near[half_wa:]), one[0])
    near_blocks = [two[len(late)], *one[len(early) :], *two[len(late) + 1 :]]
    got_early = [swap(block, p) for p, block in zip(early, one)]
    got_near = stage_along_wa(near_blocks, half_wa, along_col)
    got_late = [swap(block, p) for p, block in zip(late, two)]
    got, where = stage_along_col(near_blocks, got_near, half_wa, along_col, two[0])
    held = load(cholesky, two[0])
    shift = len(far)
    greens = (
        [*got_early, *got_late, *got],
        (*((i + shift, j) for i, j in where), *((i, 0) for i in range(shift))),
        True,
    )
    token = held

    def reduced(sums):
        distance = 1
        while distance < half:
            sums = sums + swap(sums, distance)
            distance *= 2
        sums = [sums]
        for j in range(half_wa):
            pairs = ((0, half_wa + j), (along_wa - 1, half_wa - 1 - j))
            sums.append(lax.ppermute(sums[0], "wa", pairs))
        return sums

    new, log_steps = walkers, []
    waiting = None
    for k in range(walker_count):
        last = k == walker_count - 1
        if not last:
            later = make_green(k + 1, staged, token)
            token = later[0]
            coming = stage_along_wa(later, along_wa, along_col)
        parts = reduced(bias_rows(held, noise[k : k + 1], *greens))
        if waiting is not None:
            first = stage_along_wa(waiting, along_wa, along_col)
        groups = direct if last else staged
        blocks, log_all = potential_rows(parts, held, groups, True, later[0] if last else coming[half_wa - 1])
        log_steps.append(lax.dynamic_index_in_dim(log_all[:, 0], lax.axis_index(PLANE), 0, keepdims=True))
        if waiting is not None:
            new = taylor(
                *stage_along_col(waiting, first, along_wa, along_col, log_all), True, walkers, k - 1, new, walkers
            )
        if last:
            got = {p: swap(block, p) for p, block in enumerate(blocks)}
            new = taylor(*ordered(got), True, walkers, k, new, walkers)
        else:
            waiting = blocks
            greens = (*stage_along_col(later, coming, along_wa, along_col, log_all), True)
    return new, jnp.concatenate(log_steps)


def by_all_to_all(walkers, intersection_inverse, noise_index, cholesky):
    walker_count, orbitals, electrons = walkers.shape
    vectors, tile_rows, _ = cholesky.shape
    planes = lax.axis_size(PLANE)
    green = jnp.einsum(
        "kpe,kef->kpf", walkers, intersection_inverse, preferred_element_type=jnp.float32
    ).astype(jnp.bfloat16)
    green = lax.all_to_all(
        green.reshape(walker_count, planes, tile_rows, electrons), PLANE, split_axis=1, concat_axis=1, tiled=True
    )
    partial_sums = jnp.einsum(
        "kspe,gpe->ksg", green, cholesky[:, :, :electrons], preferred_element_type=jnp.float32
    )
    bias_sum = lax.psum(partial_sums, PLANE)
    noise = lax.all_gather(quantile(noise_index), PLANE, axis=1, tiled=False)
    shifted, log_terms = shifted_field(bias_sum, noise)
    log_weight = lax.dynamic_index_in_dim(jnp.sum(log_terms, axis=-1), lax.axis_index(PLANE), 1, keepdims=False)
    rows = jnp.einsum(
        "ksg,gpq->kspq", shifted.astype(jnp.bfloat16), cholesky, preferred_element_type=jnp.float32
    ).astype(jnp.bfloat16)
    potential = lax.all_to_all(rows, PLANE, split_axis=1, concat_axis=1, tiled=True)
    new = taylor_steps(
        potential.reshape(walker_count, orbitals, orbitals),
        walkers,
        lambda a, b: jnp.einsum("kpq,kqe->kpe", a, b, preferred_element_type=jnp.float32),
    )
    return new, log_weight


def per_device(walkers, intersection_inverse, noise_index, cholesky):
    planes = lax.axis_size(PLANE)
    tile_rows = cholesky.shape[1]
    permutes = 2 <= planes <= MOST_PERMUTES and planes & (planes - 1) == 0 and tile_rows % ROWS == 0
    step = by_permutes if permutes else by_all_to_all
    return step(walkers, intersection_inverse, noise_index, cholesky)


def solution(mesh):
    placed = (
        P(("grp", "wa", "col", "row"), None, None),
        P(("grp", "wa", "col", "row"), None, None),
        P(("grp", "wa", "col", "row"), None),
        P(None, ("wa", "col"), None),
    )
    return jax.shard_map(
        per_device,
        mesh=mesh,
        in_specs=placed,
        out_specs=(P(("grp", "wa", "col", "row"), None, None), P(("grp", "wa", "col", "row"))),
        check_vma=False,
    )
```

time: 167 us -> 158 us (0.946); the launches traced: 167 us -> 155 us
  Pallas kernels: 23.9 us -> 36.4 us
  local copies, waits for them, and re-layouts: 13.5 us -> 1.8 us
  starting transfers between devices: 48.3 us -> 39.1 us
  waiting for transfers between devices: 77 us -> 74.7 us
    ppermute x34 -> x25, waiting for transfers between devices: 77 us -> 62.4 us  [swap(): return lax.ppermute(block, PLANE, [(i, i ^ place) for i in range(planes)])]
    ppermute x34 -> x25, starting transfers between devices: 48.3 us -> 35.1 us  [swap(): return lax.ppermute(block, PLANE, [(i, i ^ place) for i in range(planes)])]
    pallas_call x10 -> x13, Pallas kernels: 23.9 us -> 36.4 us  [the longest x2 14.4 us: taylor(): pl.pallas_call(functools.partial(taylor_kernel, k, where, relative), in_s...]
    ppermute x0 -> x4, waiting for transfers between devices: none -> 12.3 us  [reduced(): sums.append(lax.ppermute(sums[0], 'wa', pairs))]
    unnamed x28 -> x6, local copies, waits for them, and re-layouts: 12.4 us -> 0.7 us
    ppermute x0 -> x4, starting transfers between devices: none -> 4.06 us  [reduced(): sums.append(lax.ppermute(sums[0], 'wa', pairs))]
  transfers between devices with their start and end apart: 34 -> 29, of which waited for: 12 -> 11; matrix products, arithmetic and copies ran while one was open for 2% -> 2% of each run, Pallas kernels for 11% -> 17%
where the time goes in v3:
time: 158 us; the launch traced here: 155 us
  waiting for transfers between devices  74.7 us (47%)
  starting transfers between devices  39.1 us (25%)
  Pallas kernels  36.4 us (23%)
  other arithmetic  1.92 us (1%)
  local copies, waits for them, and re-layouts  1.8 us (1%)
    ppermute x25, waiting for transfers between devices, swap(): return lax.ppermute(block, PLANE, [(i, i ^ place) for i in range(planes)])  62.4 us
    ppermute x25, starting transfers between devices, swap(): return lax.ppermute(block, PLANE, [(i, i ^ place) for i in range(planes)])  35.1 us
    pallas_call x2, Pallas kernels, taylor(): pl.pallas_call(functools.partial(taylor_kernel, k, where, relative), in_s...  14.4 us
    ppermute x4, waiting for transfers between devices, reduced(): sums.append(lax.ppermute(sums[0], 'wa', pairs))  12.3 us
    pallas_call x2, Pallas kernels, potential_rows(): pl.pallas_call(functools.partial(potential_kernel, groups, relative, len(...  6.26 us
    pallas_call x1, Pallas kernels, load(): pl.pallas_call(load_kernel, in_specs=[IN_HBM, IN_ANY], out_specs=IN_VMEM,...  5.93 us
    pallas_call x3, Pallas kernels, green_rows(): pl.pallas_call(functools.partial(green_kernel, k, groups, relative), in_s...  5.08 us
    pallas_call x2, Pallas kernels, bias_rows(): pl.pallas_call(functools.partial(bias_kernel, where, relative), in_specs=...  4.16 us
  transfers between devices with their start and end apart: 29, of which 11 were waited for; matrix products, arithmetic and copies ran while one was open for 2% of the time, Pallas kernels for 17%

profile of v3, /device:TPU:8, one launch (start us, length us, event | category | flops | bytes accessed | tf_op | source)
XLA Modules:
  0.0 155.0 jit_solution(10242167361559443944)
XLA Ops:
  0.6 1.6 %green_rows.3 = (bf16[1,128,384]{2,1,0:T(8,128)(2,1)S(1)}, bf16[1,128,384]{2,1,0:T(8,128)(2,1)S(1)}, bf16[2,128,384]{2,1,0:T(8,128)(2,1)S(1)}) custom-call(bf16[2,1024,384]{2,1,0:T(8,128)(2,1)} %refs_10_.1, bf16[2,384,384]{2,1,0:T(8,128)(2,1)} %inverse_ref.5, bf16[2,1024,384]{2,1,0:T(8,128)(2,1)} %refs_10_.1), custom_call_target="tpu_custom_call" | custom-call | tf_op jit(solution)/shard_map/green_rows/pallas_call | solution.py:90
  2.2 3.6 %collective-permute-start.4 = (bf16[1,128,384]{2,1,0:T(8,128)(2,1)S(1)}, bf16[1,128,384]{2,1,0:T(8,128)(2,1)S(1)}, u32[]{:S(2)}, u32[]{:S(2)}) collective-permute-start(bf16[1,128,384]{2,1,0:T(8,128)(2,1)S(1)} %get-tuple-element.35), channel_id=1, source_target_pairs={{0,10},{2,8},{4,14},{6,12},{8,2},{10,0},{12,6},{14,4},{1,11},{3,9}... | collective-permute-start | bytes 294920 | tf_op jit(solution)/shard_map/ppermute | solution.py:274
  6.6 1.6 %green_rows.4 = (bf16[1,128,384]{2,1,0:T(8,128)(2,1)S(1)}, bf16[1,128,384]{2,1,0:T(8,128)(2,1)S(1)}, bf16[1,128,384]{2,1,0:T(8,128)(2,1)S(1)}, bf16[2,128,384]{2,1,0:T(8,128)(2,1)S(1)}) custom-call(bf16[2,1024,384]{2,1,0:T(8,128)(2,1)} %refs_10_.1, bf16[2,384,384]{2,1,0:T(8,128)(2,1)} %inverse_ref.5, bf16[1,128,384]{2,1,0:T(8,128)(2,1)S(1)} %get-tuple-element.29._), custom_call_target="tpu_custom_call" | custom-call | tf_op jit(solution)/shard_map/green_rows/pallas_call | solution.py:90
  8.1 2.7 %collective-permute-start.6 = (bf16[1,128,384]{2,1,0:T(8,128)(2,1)S(1)}, bf16[1,128,384]{2,1,0:T(8,128)(2,1)S(1)}, u32[]{:S(2)}, u32[]{:S(2)}) collective-permute-start(bf16[1,128,384]{2,1,0:T(8,128)(2,1)S(1)} %get-tuple-element.36), channel_id=1, source_target_pairs={{0,14},{2,12},{4,10},{6,8},{8,6},{10,4},{12,2},{14,0},{1,15},{3,13... | collective-permute-start | bytes 294920 | tf_op jit(solution)/shard_map/ppermute | solution.py:274
  11.0 5.9 %load_cholesky.1._.chol_ref.refs_3_ = bf16[64,128,1024]{2,1,0:T(8,128)(2,1)S(1)} custom-call(bf16[64,128,1024]{2,1,0:T(8,128)(2,1)} %chol_ref.1, bf16[1,128,384]{2,1,0:T(8,128)(2,1)S(1)} %get-tuple-element.30._.refs_1_), custom_call_target="tpu_custom_call" | custom-call | tf_op jit(solution)/shard_map/load_cholesky/pallas_call | solution.py:119
  17.0 2.0 %green_rows.5 = (bf16[1,128,384]{2,1,0:T(8,128)(2,1)S(1)}, bf16[2,128,384]{2,1,0:T(8,128)(2,1)S(1)}, bf16[2,128,384]{2,1,0:T(8,128)(2,1)S(1)}, bf16[2,128,384]{2,1,0:T(8,128)(2,1)S(1)}, bf16[4,128,384]{2,1,0:T(8,128)(2,1)S(1)}) custom-call(bf16[2,1024,384]{2,1,0:T(8,128)(2,1)} %refs_10_.1, bf16[2,384,384]{2,1,0:T(8,128)(2,1)} %inverse_ref.5, ...), custom_call_target="tpu_custom_call" | custom-call | tf_op jit(solution)/shard_map/green_rows/pallas_call | solution.py:90
  18.9 2.7 %collective-permute-start = (bf16[2,128,384]{2,1,0:T(8,128)(2,1)S(1)}, bf16[2,128,384]{2,1,0:T(8,128)(2,1)S(1)}, u32[]{:S(2)}, u32[]{:S(2)}) collective-permute-start(bf16[2,128,384]{2,1,0:T(8,128)(2,1)S(1)} %get-tuple-element.32), channel_id=1, source_target_pairs={{0,4},{2,6},{4,0},{6,2},{8,12},{10,14},{12,8},{14,10},{1,5},{3,7},... | collective-permute-start | bytes 589832 | tf_op jit(solution)/shard_map/ppermute | solution.py:274
  21.7 1.6 %collective-permute-start.1 = (bf16[2,128,384]{2,1,0:T(8,128)(2,1)S(1)}, bf16[2,128,384]{2,1,0:T(8,128)(2,1)S(1)}, u32[]{:S(2)}, u32[]{:S(2)}) collective-permute-start(bf16[2,128,384]{2,1,0:T(8,128)(2,1)S(1)} %get-tuple-element.33), channel_id=1, source_target_pairs={{0,8},{2,10},{4,12},{6,14},{8,0},{10,2},{12,4},{14,6},{1,9},{3,11}... | collective-permute-start | bytes 589832 | tf_op jit(solution)/shard_map/ppermute | solution.py:274
  25.0 4.7 %collective-permute-done.8.refs_6_ = bf16[2,128,384]{2,1,0:T(8,128)(2,1)S(1)} collective-permute-done((bf16[2,128,384]{2,1,0:T(8,128)(2,1)S(1)}, bf16[2,128,384]{2,1,0:T(8,128)(2,1)S(1)}, u32[]{:S(2)}, u32[]{:S(2)}) %collective-permute-start.8) | collective-permute-done | bytes 196640 | tf_op jit(solution)/shard_map/ppermute | solution.py:274
  29.6 2.1 %bias_rows.2 = f32[16,64]{1,0:T(8,128)S(1)} custom-call(bf16[64,128,1024]{2,1,0:T(8,128)(2,1)S(1)} %load_cholesky.1._.chol_ref.refs_3_, f32[1,64]{1,0:T(1,128)S(1)} %get-tuple-element.56.noise_ref, bf16[1,128,384]{2,1,0:T(8,128)(2,1)S(1)} %collective-permute-done.3.refs_0_, bf16[1,128,384]{2,1,0:T(8,128)(2,1)S(1)} %collective-permute-done.4.refs_1_, ...), custom_call_target="tpu_custom_call" | custom-call | tf_op jit(solution)/shard_map/bias_rows/pallas_call | solution.py:161
  32.7 2.7 %collective-permute-done.9 = f32[16,64]{1,0:T(8,128)S(1)} collective-permute-done((f32[16,64]{1,0:T(8,128)S(1)}, f32[16,64]{1,0:T(8,128)S(1)}, u32[]{:S(2)}, u32[]{:S(2)}) %collective-permute-start.9) | collective-permute-done | bytes 4128 | tf_op jit(solution)/shard_map/ppermute | solution.py:274
  35.4 2.2 %collective-permute-start.10 = (f32[16,64]{1,0:T(8,128)S(1)}, f32[16,64]{1,0:T(8,128)S(1)}, u32[]{:S(2)}, u32[]{:S(2)}) collective-permute-start(f32[16,64]{1,0:T(8,128)S(1)} %add.32), channel_id=1, source_target_pairs={{0,4},{2,6},{4,0},{6,2},{8,12},{10,14},{12,8},{14,10},{1,5},{3,7},... | collective-permute-start | bytes 12296 | tf_op jit(solution)/shard_map/ppermute | solution.py:274
  37.6 1.6 %collective-permute-done.10 = f32[16,64]{1,0:T(8,128)S(1)} collective-permute-done((f32[16,64]{1,0:T(8,128)S(1)}, f32[16,64]{1,0:T(8,128)S(1)}, u32[]{:S(2)}, u32[]{:S(2)}) %collective-permute-start.10) | collective-permute-done | bytes 4128 | tf_op jit(solution)/shard_map/ppermute | solution.py:274
  41.3 7.2 %collective-permute-done.11.refs_1_ = f32[16,64]{1,0:T(8,128)S(1)} collective-permute-done((f32[16,64]{1,0:T(8,128)S(1)}, f32[16,64]{1,0:T(8,128)S(1)}, u32[]{:S(2)}, u32[]{:S(2)}) %collective-permute-start.11) | collective-permute-done | bytes 4128 | tf_op jit(solution)/shard_map/ppermute | solution.py:387
  48.5 2.6 %potential_rows.2 = (bf16[1,128,1024]{2,1,0:T(8,128)(2,1)S(1)}, bf16[2,128,1024]{2,1,0:T(8,128)(2,1)S(1)}, bf16[2,128,1024]{2,1,0:T(8,128)(2,1)S(1)}, bf16[2,128...) custom-call(f32[16,64]{1,0:T(8,128)S(1)} %add.33.refs_0_, ...), custom_call_target="tpu_custom_call" | custom-call | tf_op jit(solution)/shard_map/potential_rows/pallas_call | solution.py:201
  51.5 3.3 %collective-permute-start.26 = (bf16[2,128,1024]{2,1,0:T(8,128)(2,1)S(1)}, bf16[2,128,1024]{2,1,0:T(8,128)(2,1)S(1)}, u32[]{:S(2)}, u32[]{:S(2)}) collective-permute-start(bf16[2,128,1024]{2,1,0:T(8,128)(2,1)S(1)} %get-tuple-element.52), channel_id=1, source_target_pairs={{0,8},{2,10},{4,12},{6,14},{8,0},{10,2},{12,4},{14,6},{1,9},{3,11}... | collective-permute-start | bytes 1572872 | tf_op jit(solution)/shard_map/ppermute | solution.py:274
  56.6 6.6 %collective-permute-done.13.refs_4_ = bf16[4,128,384]{2,1,0:T(8,128)(2,1)S(1)} collective-permute-done((bf16[4,128,384]{2,1,0:T(8,128)(2,1)S(1)}, bf16[4,128,384]{2,1,0:T(8,128)(2,1)S(1)}, u32[]{:S(2)}, u32[]{:S(2)}) %collective-permute-start.13) | collective-permute-done | bytes 393248 | tf_op jit(solution)/shard_map/ppermute | solution.py:274
  63.2 2.1 %bias_rows.3 = f32[16,64]{1,0:T(8,128)S(1)} custom-call(bf16[64,128,1024]{2,1,0:T(8,128)(2,1)S(1)} %load_cholesky.1._.chol_ref.refs_3_, f32[1,64]{1,0:T(1,128)S(1)} %get-tuple-element.57.noise_ref, bf16[1,128,384]{2,1,0:T(8,128)(2,1)S(1)} %get-tuple-element.31.refs_0_.refs_4_, bf16[2,128,384]{2,1,0:T(8,128)(2,1)S(1)} %collective-permute-done.refs_0_.refs_1_, ...), custom_call_target="tpu_custom_call" | custom-call | tf_op jit(solution)/shard_map/bias_rows/pallas_call | solution.py:161
  66.6 2.3 %collective-permute-done.14 = f32[16,64]{1,0:T(8,128)S(1)} collective-permute-done((f32[16,64]{1,0:T(8,128)S(1)}, f32[16,64]{1,0:T(8,128)S(1)}, u32[]{:S(2)}, u32[]{:S(2)}) %collective-permute-start.14) | collective-permute-done | bytes 4128 | tf_op jit(solution)/shard_map/ppermute | solution.py:274
  70.4 11.6 %collective-permute-done.15 = f32[16,64]{1,0:T(8,128)S(1)} collective-permute-done((f32[16,64]{1,0:T(8,128)S(1)}, f32[16,64]{1,0:T(8,128)S(1)}, u32[]{:S(2)}, u32[]{:S(2)}) %collective-permute-start.15) | collective-permute-done | bytes 4128 | tf_op jit(solution)/shard_map/ppermute | solution.py:274
  82.6 1.5 collective-permute-start.16
  84.1 5.1 %collective-permute-done.16.refs_1_ = f32[16,64]{1,0:T(8,128)S(1)} collective-permute-done((f32[16,64]{1,0:T(8,128)S(1)}, f32[16,64]{1,0:T(8,128)S(1)}, u32[]{:S(2)}, u32[]{:S(2)}) %collective-permute-start.16) | collective-permute-done | bytes 4128 | tf_op jit(solution)/shard_map/ppermute | solution.py:387
  89.2 3.7 %potential_rows.3 = (bf16[1,128,1024]{2,1,0:T(8,128)(2,1)S(1)}, bf16[1,128,1024]{2,1,0:T(8,128)(2,1)}, bf16[1,128,1024]{2,1,0:T(8,128)(2,1)}, bf16[1,128,1024]{2...) custom-call(f32[16,64]{1,0:T(8,128)S(1)} %add.35.refs_0_, ...), custom_call_target="tpu_custom_call" | custom-call | tf_op jit(solution)/shard_map/potential_rows/pallas_call | solution.py:201
  92.8 15.8 %collective-permute-done.27.refs_2_.refs_3_ = bf16[2,128,1024]{2,1,0:T(8,128)(2,1)S(1)} collective-permute-done((bf16[2,128,1024]{2,1,0:T(8,128)(2,1)S(1)}, bf16[2,128,1024]{2,1,0:T(8,128)(2,1)S(1)}, u32[]{:S(2)}, u32[]{:S(2)}) %collective-permute-start.27) | collective-permute-done | bytes 524320 | tf_op jit(solution)/shard_map/ppermute | solution.py:274
  110.0 3.2 %collective-permute-start.19 = (bf16[1,128,1024]{2,1,0:T(8,128)(2,1)S(1)}, bf16[1,128,1024]{2,1,0:T(8,128)(2,1)S(1)}, u32[]{:S(2)}, u32[]{:S(2)}) collective-permute-start(bf16[1,128,1024]{2,1,0:T(8,128)(2,1)S(1)} %get-tuple-element.43), channel_id=1, source_target_pairs={{0,10},{2,8},{4,14},{6,12},{8,2},{10,0},{12,6},{14,4},{1,11},{3,9}... | collective-permute-start | bytes 786440 | tf_op jit(solution)/shard_map/ppermute | solution.py:274
  113.2 2.5 %collective-permute-start.20 = (bf16[1,128,1024]{2,1,0:T(8,128)(2,1)}, bf16[1,128,1024]{2,1,0:T(8,128)(2,1)}, u32[]{:S(2)}, u32[]{:S(2)}) collective-permute-start(bf16[1,128,1024]{2,1,0:T(8,128)(2,1)} %get-tuple-element.44), channel_id=1, source_target_pairs={{0,12},{2,14},{4,8},{6,10},{8,4},{10,6},{12,0},{14,2},{1,13},{3,15... | collective-permute-start | bytes 786440 | tf_op jit(solution)/shard_map/ppermute | solution.py:274
  116.3 2.4 %collective-permute-done.18.refs_0_ = bf16[1,128,1024]{2,1,0:T(8,128)(2,1)S(1)} collective-permute-done((bf16[1,128,1024]{2,1,0:T(8,128)(2,1)S(1)}, bf16[1,128,1024]{2,1,0:T(8,128)(2,1)S(1)}, u32[]{:S(2)}, u32[]{:S(2)}) %collective-permute-start.18) | collective-permute-done | bytes 262176 | tf_op jit(solution)/shard_map/ppermute | solution.py:274
  119.5 14.7 %collective-permute-done.19.refs_1_ = bf16[1,128,1024]{2,1,0:T(8,128)(2,1)S(1)} collective-permute-done((bf16[1,128,1024]{2,1,0:T(8,128)(2,1)S(1)}, bf16[1,128,1024]{2,1,0:T(8,128)(2,1)S(1)}, u32[]{:S(2)}, u32[]{:S(2)}) %collective-permute-start.19) | collective-permute-done | bytes 262176 | tf_op jit(solution)/shard_map/ppermute | solution.py:274
  134.9 2.2 %collective-permute-start.23 = (bf16[1,128,1024]{2,1,0:T(8,128)(2,1)}, bf16[1,128,1024]{2,1,0:T(8,128)(2,1)}, u32[]{:S(2)}, u32[]{:S(2)}) collective-permute-start(bf16[1,128,1024]{2,1,0:T(8,128)(2,1)} %get-tuple-element.48), channel_id=1, source_target_pairs={{0,4},{2,6},{4,0},{6,2},{8,12},{10,14},{12,8},{14,10},{1,5},{3,7},... | collective-permute-start | bytes 786440 | tf_op jit(solution)/shard_map/ppermute | solution.py:274
  138.5 1.9 %pad_maximum_fusion = f32[2]{0:T(128)} fusion(f32[1]{0:T(128)} %bitcast.1, f32[1]{0:T(128)} %bitcast), kind=kLoop, calls=%fused_computation.6 | loop fusion | flops 2 | bytes 16 | tf_op jit(solution)/shard_map/concatenate | solution.py:414
  140.4 6.6 %taylor.2.refs_9_ = bf16[2,1024,384]{2,1,0:T(8,128)(2,1)} custom-call(bf16[1,128,1024]{2,1,0:T(8,128)(2,1)S(1)} %get-tuple-element.50.refs_0_, bf16[2,128,1024]{2,1,0:T(8,128)(2,1)S(1)} %collective-permute-done.25.refs_0_.refs_1_, bf16[2,128,1024]{2,1,0:T(8,128)(2,1)S(1)} %collective-permute-done.26.refs_1_.refs_2_, ...), custom_call_target="tpu_custom_call" | custom-call | tf_op jit(solution)/shard_map/taylor/pallas_call | solution.py:252
  147.0 7.8 %taylor.3 = bf16[2,1024,384]{2,1,0:T(8,128)(2,1)} custom-call(bf16[1,128,1024]{2,1,0:T(8,128)(2,1)S(1)} %collective-permute-done.18.refs_0_, bf16[1,128,1024]{2,1,0:T(8,128)(2,1)S(1)} %copy-done.1, bf16[1,128,1024]{2,1,0:T(8,128)(2,1)} %collective-permute-done.20.refs_2_, ...), custom_call_target="tpu_custom_call", output_to_operand_aliasing={{}: (9, {})} | custom-call | tf_op jit(solution)/shard_map/taylor/pallas_call | solution.py:252
  (54 shorter events, 16.2 us)
Async XLA Ops:
  2.2 8.8 %copy-start.2 = (s32[2,64]{1,0:T(2,128)S(1)}, s32[2,64]{1,0:T(2,128)}, u32[]{:S(2)}) copy-start(s32[2,64]{1,0:T(2,128)} %param.6) | copy-start | bytes 1540
  2.2 19.5 %collective-permute-start.4 = (bf16[1,128,384]{2,1,0:T(8,128)(2,1)S(1)}, bf16[1,128,384]{2,1,0:T(8,128)(2,1)S(1)}, u32[]{:S(2)}, u32[]{:S(2)}) collective-permute-start(bf16[1,128,384]{2,1,0:T(8,128)(2,1)S(1)} %get-tuple-element.35), channel_id=1, source_target_pairs={{0,10},{2,8},{4,14},{6,12},{8,2},{10,0},{12,6},{14,4},{1,11},{3,9}... | collective-permute-start | bytes 294920 | tf_op jit(solution)/shard_map/ppermute | solution.py:274
  5.8 17.5 %collective-permute-start.3 = (bf16[1,128,384]{2,1,0:T(8,128)(2,1)S(1)}, bf16[1,128,384]{2,1,0:T(8,128)(2,1)S(1)}, u32[]{:S(2)}, u32[]{:S(2)}) collective-permute-start(bf16[1,128,384]{2,1,0:T(8,128)(2,1)S(1)} %get-tuple-element.29._), channel_id=1, source_target_pairs={{0,8},{2,10},{4,12},{6,14},{8,0},{10,2},{12,4},{14,6},{1,9},{3,11}... | collective-permute-start | bytes 294920 | tf_op jit(solution)/shard_map/ppermute | solution.py:274
  6.1 12.8 %collective-permute-start.7 = (bf16[2,128,384]{2,1,0:T(8,128)(2,1)S(1)}, bf16[2,128,384]{2,1,0:T(8,128)(2,1)S(1)}, u32[]{:S(2)}, u32[]{:S(2)}) collective-permute-start(bf16[2,128,384]{2,1,0:T(8,128)(2,1)S(1)} %get-tuple-element.38), channel_id=1, source_target_pairs={{0,4},{2,6},{4,0},{6,2},{8,12},{10,14},{12,8},{14,10},{1,5},{3,7},... | collective-permute-start | bytes 589832 | tf_op jit(solution)/shard_map/ppermute | solution.py:274
  8.1 15.8 %collective-permute-start.6 = (bf16[1,128,384]{2,1,0:T(8,128)(2,1)S(1)}, bf16[1,128,384]{2,1,0:T(8,128)(2,1)S(1)}, u32[]{:S(2)}, u32[]{:S(2)}) collective-permute-start(bf16[1,128,384]{2,1,0:T(8,128)(2,1)S(1)} %get-tuple-element.36), channel_id=1, source_target_pairs={{0,14},{2,12},{4,10},{6,8},{8,6},{10,4},{12,2},{14,0},{1,15},{3,13... | collective-permute-start | bytes 294920 | tf_op jit(solution)/shard_map/ppermute | solution.py:274
  10.9 14.1 %collective-permute-start.5 = (bf16[1,128,384]{2,1,0:T(8,128)(2,1)S(1)}, bf16[1,128,384]{2,1,0:T(8,128)(2,1)S(1)}, u32[]{:S(2)}, u32[]{:S(2)}) collective-permute-start(bf16[1,128,384]{2,1,0:T(8,128)(2,1)S(1)} %get-tuple-element.30._.refs_1_), channel_id=1, source_target_pairs={{0,12},{2,14},{4,8},{6,10},{8,4},{10,6},{12,0},{14,2},{1,13},{3,15... | collective-permute-start | bytes 294920 | tf_op jit(solution)/shard_map/ppermute | solution.py:274
  18.9 35.9 %collective-permute-start = (bf16[2,128,384]{2,1,0:T(8,128)(2,1)S(1)}, bf16[2,128,384]{2,1,0:T(8,128)(2,1)S(1)}, u32[]{:S(2)}, u32[]{:S(2)}) collective-permute-start(bf16[2,128,384]{2,1,0:T(8,128)(2,1)S(1)} %get-tuple-element.32), channel_id=1, source_target_pairs={{0,4},{2,6},{4,0},{6,2},{8,12},{10,14},{12,8},{14,10},{1,5},{3,7},... | collective-permute-start | bytes 589832 | tf_op jit(solution)/shard_map/ppermute | solution.py:274
  21.7 19.5 %collective-permute-start.1 = (bf16[2,128,384]{2,1,0:T(8,128)(2,1)S(1)}, bf16[2,128,384]{2,1,0:T(8,128)(2,1)S(1)}, u32[]{:S(2)}, u32[]{:S(2)}) collective-permute-start(bf16[2,128,384]{2,1,0:T(8,128)(2,1)S(1)} %get-tuple-element.33), channel_id=1, source_target_pairs={{0,8},{2,10},{4,12},{6,14},{8,0},{10,2},{12,4},{14,6},{1,9},{3,11}... | collective-permute-start | bytes 589832 | tf_op jit(solution)/shard_map/ppermute | solution.py:274
  23.3 31.5 %collective-permute-start.2 = (bf16[2,128,384]{2,1,0:T(8,128)(2,1)S(1)}, bf16[2,128,384]{2,1,0:T(8,128)(2,1)S(1)}, u32[]{:S(2)}, u32[]{:S(2)}) collective-permute-start(bf16[2,128,384]{2,1,0:T(8,128)(2,1)S(1)} %get-tuple-element.34), channel_id=1, source_target_pairs={{0,12},{2,14},{4,8},{6,10},{8,4},{10,6},{12,0},{14,2},{1,13},{3,15... | collective-permute-start | bytes 589832 | tf_op jit(solution)/shard_map/ppermute | solution.py:274
  24.0 5.7 %collective-permute-start.8 = (bf16[2,128,384]{2,1,0:T(8,128)(2,1)S(1)}, bf16[2,128,384]{2,1,0:T(8,128)(2,1)S(1)}, u32[]{:S(2)}, u32[]{:S(2)}) collective-permute-start(bf16[2,128,384]{2,1,0:T(8,128)(2,1)S(1)} %join.3), channel_id=1, source_target_pairs={{0,2},{2,0},{4,6},{6,4},{8,10},{10,8},{12,14},{14,12},{1,3},{3,1},... | collective-permute-start | bytes 589832 | tf_op jit(solution)/shard_map/ppermute | solution.py:274
  31.7 3.7 %collective-permute-start.9 = (f32[16,64]{1,0:T(8,128)S(1)}, f32[16,64]{1,0:T(8,128)S(1)}, u32[]{:S(2)}, u32[]{:S(2)}) collective-permute-start(f32[16,64]{1,0:T(8,128)S(1)} %bias_rows.2), channel_id=1, source_target_pairs={{0,2},{2,0},{4,6},{6,4},{8,10},{10,8},{12,14},{14,12},{1,3},{3,1},... | collective-permute-start | bytes 12296 | tf_op jit(solution)/shard_map/ppermute | solution.py:274
  35.4 3.9 %collective-permute-start.10 = (f32[16,64]{1,0:T(8,128)S(1)}, f32[16,64]{1,0:T(8,128)S(1)}, u32[]{:S(2)}, u32[]{:S(2)}) collective-permute-start(f32[16,64]{1,0:T(8,128)S(1)} %add.32), channel_id=1, source_target_pairs={{0,4},{2,6},{4,0},{6,2},{8,12},{10,14},{12,8},{14,10},{1,5},{3,7},... | collective-permute-start | bytes 12296 | tf_op jit(solution)/shard_map/ppermute | solution.py:274
  39.3 2.0 %collective-permute-start.12 = (f32[16,64]{1,0:T(8,128)S(1)}, f32[16,64]{1,0:T(8,128)S(1)}, u32[]{:S(2)}, u32[]{:S(2)}) collective-permute-start(f32[16,64]{1,0:T(8,128)S(1)} %add.33.refs_0_), channel_id=1, source_target_pairs={{0,12},{12,0},{1,13},{13,1},{2,14},{14,2},{3,15},{15,3},{16,28},{2... | collective-permute-start | bytes 12296 | tf_op jit(solution)/shard_map/ppermute | solution.py:387
  39.9 8.5 %collective-permute-start.11 = (f32[16,64]{1,0:T(8,128)S(1)}, f32[16,64]{1,0:T(8,128)S(1)}, u32[]{:S(2)}, u32[]{:S(2)}) collective-permute-start(f32[16,64]{1,0:T(8,128)S(1)} %add.33.refs_0_), channel_id=1, source_target_pairs={{0,8},{12,4},{1,9},{13,5},{2,10},{14,6},{3,11},{15,7},{16,24},{28,... | collective-permute-start | bytes 12296 | tf_op jit(solution)/shard_map/ppermute | solution.py:387
  51.1 41.8 %collective-permute-start.25 = (bf16[2,128,1024]{2,1,0:T(8,128)(2,1)S(1)}, bf16[2,128,1024]{2,1,0:T(8,128)(2,1)S(1)}, u32[]{:S(2)}, u32[]{:S(2)}) collective-permute-start(bf16[2,128,1024]{2,1,0:T(8,128)(2,1)S(1)} %get-tuple-element.51), channel_id=1, source_target_pairs={{0,4},{2,6},{4,0},{6,2},{8,12},{10,14},{12,8},{14,10},{1,5},{3,7},... | collective-permute-start | bytes 1572872 | tf_op jit(solution)/shard_map/ppermute | solution.py:274
  51.5 41.4 %collective-permute-start.26 = (bf16[2,128,1024]{2,1,0:T(8,128)(2,1)S(1)}, bf16[2,128,1024]{2,1,0:T(8,128)(2,1)S(1)}, u32[]{:S(2)}, u32[]{:S(2)}) collective-permute-start(bf16[2,128,1024]{2,1,0:T(8,128)(2,1)S(1)} %get-tuple-element.52), channel_id=1, source_target_pairs={{0,8},{2,10},{4,12},{6,14},{8,0},{10,2},{12,4},{14,6},{1,9},{3,11}... | collective-permute-start | bytes 1572872 | tf_op jit(solution)/shard_map/ppermute | solution.py:274
  54.8 53.9 %collective-permute-start.27 = (bf16[2,128,1024]{2,1,0:T(8,128)(2,1)S(1)}, bf16[2,128,1024]{2,1,0:T(8,128)(2,1)S(1)}, u32[]{:S(2)}, u32[]{:S(2)}) collective-permute-start(bf16[2,128,1024]{2,1,0:T(8,128)(2,1)S(1)} %get-tuple-element.53), channel_id=1, source_target_pairs={{0,12},{2,14},{4,8},{6,10},{8,4},{10,6},{12,0},{14,2},{1,13},{3,15... | collective-permute-start | bytes 1572872 | tf_op jit(solution)/shard_map/ppermute | solution.py:274
  55.2 7.9 %collective-permute-start.13 = (bf16[4,128,384]{2,1,0:T(8,128)(2,1)S(1)}, bf16[4,128,384]{2,1,0:T(8,128)(2,1)S(1)}, u32[]{:S(2)}, u32[]{:S(2)}) collective-permute-start(bf16[4,128,384]{2,1,0:T(8,128)(2,1)S(1)} %join.4), channel_id=1, source_target_pairs={{0,2},{2,0},{4,6},{6,4},{8,10},{10,8},{12,14},{14,12},{1,3},{3,1},... | collective-permute-start | bytes 1179656 | tf_op jit(solution)/shard_map/ppermute | solution.py:274
  65.2 3.7 %collective-permute-start.14 = (f32[16,64]{1,0:T(8,128)S(1)}, f32[16,64]{1,0:T(8,128)S(1)}, u32[]{:S(2)}, u32[]{:S(2)}) collective-permute-start(f32[16,64]{1,0:T(8,128)S(1)} %bias_rows.3), channel_id=1, source_target_pairs={{0,2},{2,0},{4,6},{6,4},{8,10},{10,8},{12,14},{14,12},{1,3},{3,1},... | collective-permute-start | bytes 12296 | tf_op jit(solution)/shard_map/ppermute | solution.py:274
  68.9 13.0 %collective-permute-start.15 = (f32[16,64]{1,0:T(8,128)S(1)}, f32[16,64]{1,0:T(8,128)S(1)}, u32[]{:S(2)}, u32[]{:S(2)}) collective-permute-start(f32[16,64]{1,0:T(8,128)S(1)} %add.34), channel_id=1, source_target_pairs={{0,4},{2,6},{4,0},{6,2},{8,12},{10,14},{12,8},{14,10},{1,5},{3,7},... | collective-permute-start | bytes 12296 | tf_op jit(solution)/shard_map/ppermute | solution.py:274
  82.0 2.1 %collective-permute-start.17 = (f32[16,64]{1,0:T(8,128)S(1)}, f32[16,64]{1,0:T(8,128)S(1)}, u32[]{:S(2)}, u32[]{:S(2)}) collective-permute-start(f32[16,64]{1,0:T(8,128)S(1)} %add.35.refs_0_), channel_id=1, source_target_pairs={{0,12},{12,0},{1,13},{13,1},{2,14},{14,2},{3,15},{15,3},{16,28},{2... | collective-permute-start | bytes 12296 | tf_op jit(solution)/shard_map/ppermute | solution.py:387
  82.6 6.6 %collective-permute-start.16 = (f32[16,64]{1,0:T(8,128)S(1)}, f32[16,64]{1,0:T(8,128)S(1)}, u32[]{:S(2)}, u32[]{:S(2)}) collective-permute-start(f32[16,64]{1,0:T(8,128)S(1)} %add.35.refs_0_), channel_id=1, source_target_pairs={{0,8},{12,4},{1,9},{13,5},{2,10},{14,6},{3,11},{15,7},{16,24},{28,... | collective-permute-start | bytes 12296 | tf_op jit(solution)/shard_map/ppermute | solution.py:387
  108.8 28.3 %collective-permute-start.28 = (bf16[4,128,1024]{2,1,0:T(8,128)(2,1)S(1)}, bf16[4,128,1024]{2,1,0:T(8,128)(2,1)S(1)}, u32[]{:S(2)}, u32[]{:S(2)}) collective-permute-start(bf16[4,128,1024]{2,1,0:T(8,128)(2,1)S(1)} %join.5), channel_id=1, source_target_pairs={{0,2},{2,0},{4,6},{6,4},{8,10},{10,8},{12,14},{14,12},{1,3},{3,1},... | collective-permute-start | bytes 3145736 | tf_op jit(solution)/shard_map/ppermute | solution.py:274
  110.0 8.7 %collective-permute-start.18 = (bf16[1,128,1024]{2,1,0:T(8,128)(2,1)S(1)}, bf16[1,128,1024]{2,1,0:T(8,128)(2,1)S(1)}, u32[]{:S(2)}, u32[]{:S(2)}) collective-permute-start(bf16[1,128,1024]{2,1,0:T(8,128)(2,1)S(1)} %get-tuple-element.42), channel_id=1, source_target_pairs={{0,8},{2,10},{4,12},{6,14},{8,0},{10,2},{12,4},{14,6},{1,9},{3,11}... | collective-permute-start | bytes 786440 | tf_op jit(solution)/shard_map/ppermute | solution.py:274
  110.0 24.2 %collective-permute-start.19 = (bf16[1,128,1024]{2,1,0:T(8,128)(2,1)S(1)}, bf16[1,128,1024]{2,1,0:T(8,128)(2,1)S(1)}, u32[]{:S(2)}, u32[]{:S(2)}) collective-permute-start(bf16[1,128,1024]{2,1,0:T(8,128)(2,1)S(1)} %get-tuple-element.43), channel_id=1, source_target_pairs={{0,10},{2,8},{4,14},{6,12},{8,2},{10,0},{12,6},{14,4},{1,11},{3,9}... | collective-permute-start | bytes 786440 | tf_op jit(solution)/shard_map/ppermute | solution.py:274
  113.2 33.8 %collective-permute-start.20 = (bf16[1,128,1024]{2,1,0:T(8,128)(2,1)}, bf16[1,128,1024]{2,1,0:T(8,128)(2,1)}, u32[]{:S(2)}, u32[]{:S(2)}) collective-permute-start(bf16[1,128,1024]{2,1,0:T(8,128)(2,1)} %get-tuple-element.44), channel_id=1, source_target_pairs={{0,12},{2,14},{4,8},{6,10},{8,4},{10,6},{12,0},{14,2},{1,13},{3,15... | collective-permute-start | bytes 786440 | tf_op jit(solution)/shard_map/ppermute | solution.py:274
  115.7 31.3 %collective-permute-start.21 = (bf16[1,128,1024]{2,1,0:T(8,128)(2,1)}, bf16[1,128,1024]{2,1,0:T(8,128)(2,1)}, u32[]{:S(2)}, u32[]{:S(2)}) collective-permute-start(bf16[1,128,1024]{2,1,0:T(8,128)(2,1)} %get-tuple-element.45), channel_id=1, source_target_pairs={{0,14},{2,12},{4,10},{6,8},{8,6},{10,4},{12,2},{14,0},{1,15},{3,13... | collective-permute-start | bytes 786440 | tf_op jit(solution)/shard_map/ppermute | solution.py:274
  118.7 28.3 %collective-permute-start.22 = (bf16[1,128,1024]{2,1,0:T(8,128)(2,1)}, bf16[1,128,1024]{2,1,0:T(8,128)(2,1)}, u32[]{:S(2)}, u32[]{:S(2)}) collective-permute-start(bf16[1,128,1024]{2,1,0:T(8,128)(2,1)} %get-tuple-element.47), channel_id=1, source_target_pairs={{0,2},{2,0},{4,6},{6,4},{8,10},{10,8},{12,14},{14,12},{1,3},{3,1},... | collective-permute-start | bytes 786440 | tf_op jit(solution)/shard_map/ppermute | solution.py:274
  134.2 0.7 copy-start
  134.9 12.1 %collective-permute-start.23 = (bf16[1,128,1024]{2,1,0:T(8,128)(2,1)}, bf16[1,128,1024]{2,1,0:T(8,128)(2,1)}, u32[]{:S(2)}, u32[]{:S(2)}) collective-permute-start(bf16[1,128,1024]{2,1,0:T(8,128)(2,1)} %get-tuple-element.48), channel_id=1, source_target_pairs={{0,4},{2,6},{4,0},{6,2},{8,12},{10,14},{12,8},{14,10},{1,5},{3,7},... | collective-permute-start | bytes 786440 | tf_op jit(solution)/shard_map/ppermute | solution.py:274
  137.1 9.9 %collective-permute-start.24 = (bf16[1,128,1024]{2,1,0:T(8,128)(2,1)}, bf16[1,128,1024]{2,1,0:T(8,128)(2,1)}, u32[]{:S(2)}, u32[]{:S(2)}) collective-permute-start(bf16[1,128,1024]{2,1,0:T(8,128)(2,1)} %get-tuple-element.49), channel_id=1, source_target_pairs={{0,6},{2,4},{4,2},{6,0},{8,14},{10,12},{12,10},{14,8},{1,7},{3,5},... | collective-permute-start | bytes 786440 | tf_op jit(solution)/shard_map/ppermute | solution.py:274
  140.4 6.6 %copy-start.1 = (bf16[1,128,1024]{2,1,0:T(8,128)(2,1)S(1)}, bf16[1,128,1024]{2,1,0:T(8,128)(2,1)}, u32[]{:S(2)}) copy-start(bf16[1,128,1024]{2,1,0:T(8,128)(2,1)} %copy-done) | copy-start | bytes 786436

commit v4 on v3

--- a/solution.py
+++ b/solution.py
@@ -20,6 +20,7 @@
 MOST_PERMUTES = 8
 VMEM = 16 * 1024 * 1024
 IN_VMEM = pl.BlockSpec(memory_space=pltpu.VMEM)
+IN_SMEM = pl.BlockSpec(memory_space=pltpu.SMEM)
 IN_HBM = pl.BlockSpec(memory_space=pltpu.HBM)
 IN_ANY = pl.BlockSpec(memory_space=pl.ANY)
 
@@ -48,6 +49,10 @@
 
 def own_place():
     return lax.axis_index("wa") * lax.axis_size("col") + lax.axis_index("col")
+
+
+def in_vmem(array):
+    return pltpu.with_memory_space_constraint(array, pltpu.VMEM)
 
 
 def in_hbm(array):
@@ -103,10 +108,13 @@
     )(in_hbm(walkers), in_hbm(inverses), after)
 
 
-def load_kernel(chol_ref, _, held_ref, arrived):
+def load_kernel(start, chol_ref, _, held_ref, arrived):
     step = chol_ref.shape[0] // arrived.shape[0]
+    columns = pl.ds(start, held_ref.shape[2])
     copies = [
-        pltpu.make_async_copy(chol_ref.at[pl.ds(i * step, step)], held_ref.at[pl.ds(i * step, step)], arrived.at[i])
+        pltpu.make_async_copy(
+            chol_ref.at[pl.ds(i * step, step), :, columns], held_ref.at[pl.ds(i * step, step)], arrived.at[i]
+        )
         for i in range(arrived.shape[0])
     ]
     for copy in copies:
@@ -115,17 +123,37 @@
         copy.wait()
 
 
-def load(cholesky, after):
+def load(cholesky, start, stop, after):
+    vectors, tile_rows, _ = cholesky.shape
     return pl.pallas_call(
-        load_kernel,
+        functools.partial(load_kernel, start),
         in_specs=[IN_HBM, IN_ANY],
         out_specs=IN_VMEM,
-        out_shape=pltpu.VMEM(cholesky.shape, cholesky.dtype),
-        scratch_shapes=[pltpu.SemaphoreType.DMA((math.gcd(cholesky.shape[0], 8),))],
+        out_shape=pltpu.VMEM((vectors, tile_rows, stop - start), cholesky.dtype),
+        scratch_shapes=[pltpu.SemaphoreType.DMA((math.gcd(vectors, 8),))],
         compiler_params=kernel_params(),
         cost_estimate=NO_COST,
         name="load_cholesky",
     )(in_hbm(cholesky), after)
+
+
+def bring_kernel(k, walkers_ref, _, held_ref, arrived):
+    copy = pltpu.make_async_copy(walkers_ref.at[k], held_ref, arrived)
+    copy.start()
+    copy.wait()
+
+
+def bring(walkers, k, after):
+    return pl.pallas_call(
+        functools.partial(bring_kernel, k),
+        in_specs=[IN_HBM, IN_ANY],
+        out_specs=IN_VMEM,
+        out_shape=pltpu.VMEM(walkers.shape[1:], walkers.dtype),
+        scratch_shapes=[pltpu.SemaphoreType.DMA(())],
+        compiler_params=kernel_params(),
+        cost_estimate=NO_COST,
+        name="bring_walker",
+    )(in_hbm(walkers), after)
 
 
 def bias_kernel(where, relative, chol_ref, noise_ref, *refs):
@@ -169,16 +197,21 @@
     )(cholesky, noise, *greens)
 
 
-def potential_kernel(groups, relative, parts, *refs):
-    sums, chol_ref, outs, log_ref = refs[:parts], refs[parts], refs[parts + 2 : -1], refs[-1]
+def potential_kernel(groups, relative, parts, pieces, *refs):
+    sums, chols, refs = refs[:parts], refs[parts : parts + pieces], refs[parts + pieces :]
+    before_ref, outs, log_ref = refs[0], refs[2:-1], refs[-1]
     places = [(place, out_ref, j) for group, out_ref in zip(groups, outs) for j, place in enumerate(group)]
     places = [slot for slot in places if slot[0] is not None]
     count = len(places)
-    vectors, tile_rows, orbitals = chol_ref.shape
+    vectors, tile_rows, _ = chols[0].shape
     totals = [ref[...] for ref in sums]
     total = totals[0] + sum(totals[2:], totals[1])
     shifted, log_terms = shifted_field(total[:count, :], total[count:, :])
-    log_ref[...] = jnp.sum(log_terms, axis=1, keepdims=True)
+    own = iota(log_terms.shape, 0) == own_place()
+    known = log_ref.shape[0] - 1
+    for i in range(known):
+        log_ref[i] = before_ref[i]
+    log_ref[known] = jnp.sum(jnp.where(own, log_terms, 0.0))
     field = shifted.astype(jnp.bfloat16)
     if relative:
         order = jnp.bitwise_xor(iota((count, count), 0), own_place()) == iota((count, count), 1)
@@ -189,27 +222,34 @@
     spread = jnp.where(iota(shape, 1) == iota(shape, 2) % ROWS, wide[:, None, :], 0.0)
     spread = spread.reshape(count * ROWS, vectors * ROWS).astype(jnp.bfloat16)
     for start in range(0, tile_rows, ROWS):
-        tile = chol_ref[:, start : start + ROWS, :].reshape(vectors * ROWS, orbitals)
-        rows = jnp.dot(spread, tile, preferred_element_type=jnp.float32).astype(jnp.bfloat16)
-        for place, out_ref, j in places:
-            out_ref[j, start : start + ROWS, :] = rows[place * ROWS : (place + 1) * ROWS, :]
-
-
-def potential_rows(sums, cholesky, groups, relative, after):
-    vectors, tile_rows, orbitals = cholesky.shape
+        column = 0
+        for chol_ref in chols:
+            width = chol_ref.shape[2]
+            tile = chol_ref[:, start : start + ROWS, :].reshape(vectors * ROWS, width)
+            rows = jnp.dot(spread, tile, preferred_element_type=jnp.float32).astype(jnp.bfloat16)
+            for place, out_ref, j in places:
+                out_ref[j, start : start + ROWS, column : column + width] = rows[place * ROWS : (place + 1) * ROWS, :]
+            column += width
+
+
+def potential_rows(sums, cholesky, groups, relative, log_steps, after):
+    vectors, tile_rows, _ = cholesky[0].shape
+    orbitals = sum(piece.shape[2] for piece in cholesky)
     count = sums[0].shape[0] // 2
+    known = 0 if log_steps is None else log_steps.shape[0]
+    before = jnp.zeros((1,), jnp.float32) if log_steps is None else log_steps
     *blocks, log_steps = pl.pallas_call(
-        functools.partial(potential_kernel, groups, relative, len(sums)),
-        in_specs=[IN_VMEM] * (len(sums) + 1) + [IN_ANY],
-        out_specs=[IN_VMEM] * (len(groups) + 1),
+        functools.partial(potential_kernel, groups, relative, len(sums), len(cholesky)),
+        in_specs=[IN_VMEM] * (len(sums) + len(cholesky)) + [IN_SMEM, IN_ANY],
+        out_specs=[IN_VMEM] * len(groups) + [IN_SMEM],
         out_shape=[
             *(jax.ShapeDtypeStruct((len(group), tile_rows, orbitals), jnp.bfloat16) for group in groups),
-            jax.ShapeDtypeStruct((count, 1), jnp.float32),
+            jax.ShapeDtypeStruct((known + 1,), jnp.float32),
         ],
         compiler_params=kernel_params(),
         cost_estimate=NO_COST,
         name="potential_rows",
-    )(*sums, cholesky, after)
+    )(*sums, *cholesky, before, after)
     return blocks, log_steps
 
 
@@ -222,49 +262,55 @@
     return running.astype(jnp.bfloat16)
 
 
-def taylor_kernel(k, where, relative, *refs):
-    if relative:
-        blocks, (walker_ref, _, _, out_ref, walker_in, result, arrived, held) = refs[:-8], refs[-8:]
-    else:
-        blocks, (walker_ref, _, _, out_ref, walker_in, result, arrived) = refs[:-7], refs[-7:]
-        (held,) = blocks
-    read = pltpu.make_async_copy(walker_ref.at[k], walker_in, arrived)
-    read.start()
-    if relative:
-        for place, (i, j) in enumerate(where):
-            held[device_at(place, relative)] = blocks[i][j]
-    read.wait()
-    orbitals = held.shape[2]
-    result[...] = taylor_steps(
-        held[...].reshape(orbitals, orbitals),
-        walker_in[...],
-        lambda a, b: jnp.dot(a, b, preferred_element_type=jnp.float32),
-    )
-    write = pltpu.make_async_copy(result, out_ref.at[k], arrived)
-    write.start()
-    write.wait()
-
-
-def taylor(blocks, where, relative, walkers, k, new, after):
-    _, orbitals, electrons = walkers.shape
+def taylor_kernel(k, where, *refs):
+    blocks, (walker_ref, _, _, out_ref, held, terms, running, result, written) = refs[:-9], refs[-9:]
+    for place, (i, j) in enumerate(where):
+        held[device_at(place, True)] = blocks[i][j]
+    count, tile_rows, orbitals = held.shape
+    source = walker_ref
+    for degree in range(1, DEGREES):
+        product = (-STEP_ROOT / degree) * jnp.dot(
+            held[...].reshape(orbitals, orbitals), source[...], preferred_element_type=jnp.float32
+        )
+        source = terms.at[degree % 2]
+        source[...] = product.astype(jnp.bfloat16)
+        running[...] = product + (walker_ref[...].astype(jnp.float32) if degree == 1 else running[...])
+    step = max(count // 4, 1)
+    writes = []
+    for i in range(count // step):
+        rows = pl.ds(i * step * tile_rows, step * tile_rows)
+        product = (-STEP_ROOT / DEGREES) * jnp.dot(
+            held[i * step : (i + 1) * step].reshape(step * tile_rows, orbitals),
+            source[...],
+            preferred_element_type=jnp.float32,
+        )
+        result[rows, :] = (running[rows, :] + product).astype(jnp.bfloat16)
+        writes.append(pltpu.make_async_copy(result.at[rows], out_ref.at[k, rows], written.at[i]))
+        writes[-1].start()
+    for write in writes:
+        write.wait()
+
+
+def taylor(blocks, where, walker, k, new, after):
+    orbitals, electrons = walker.shape
     count, tile_rows = len(where), blocks[0].shape[1]
-    held = [pltpu.VMEM((count, tile_rows, orbitals), jnp.bfloat16)] if relative else []
     return pl.pallas_call(
-        functools.partial(taylor_kernel, k, where, relative),
-        in_specs=[IN_VMEM] * len(blocks) + [IN_HBM, IN_HBM, IN_ANY],
+        functools.partial(taylor_kernel, k, where),
+        in_specs=[IN_VMEM] * (len(blocks) + 1) + [IN_HBM, IN_ANY],
         out_specs=IN_HBM,
-        out_shape=jax.ShapeDtypeStruct(walkers.shape, jnp.bfloat16),
+        out_shape=jax.ShapeDtypeStruct(new.shape, jnp.bfloat16),
         scratch_shapes=[
+            pltpu.VMEM((count, tile_rows, orbitals), jnp.bfloat16),
+            pltpu.VMEM((2, orbitals, electrons), jnp.bfloat16),
+            pltpu.VMEM((orbitals, electrons), jnp.float32),
             pltpu.VMEM((orbitals, electrons), jnp.bfloat16),
-            pltpu.VMEM((orbitals, electrons), jnp.bfloat16),
-            pltpu.SemaphoreType.DMA(()),
-            *held,
+            pltpu.SemaphoreType.DMA((count,)),
         ],
-        input_output_aliases={} if new is walkers else {len(blocks) + 1: 0},
+        input_output_aliases={len(blocks) + 1: 0} if k else {},
         compiler_params=kernel_params(),
         cost_estimate=NO_COST,
         name="taylor",
-    )(*blocks, in_hbm(walkers), in_hbm(new), after)
+    )(*(in_vmem(block) for block in blocks), walker, in_hbm(new), after)
 
 
 def swap(block, place):
@@ -300,22 +346,6 @@
     )(*sources, *targets)
 
 
-def gate_kernel(*_):
-    pass
-
-
-def gate(block, *after):
-    return pl.pallas_call(
-        gate_kernel,
-        in_specs=[IN_ANY] * (1 + len(after)),
-        out_specs=IN_ANY,
-        out_shape=jax.ShapeDtypeStruct(block.shape, block.dtype),
-        input_output_aliases={0: 0},
-        compiler_params=kernel_params(),
-        name="gate",
-    )(block, *after)
-
-
 def staged_groups(along_wa, along_col):
     return (
         (0,),
@@ -332,8 +362,8 @@
 def stage_along_col(blocks, first, along_wa, along_col, after):
     second = blocks[along_wa:]
     if first and second:
-        moves = tuple(((a - 1, c), (c - 1, a)) for a in range(1, along_wa) for c in range(1, along_col))
-        second = join([*first, after], second, moves)
+        moves = tuple(((along_wa - 1 - a, c), (c - 1, a)) for a in range(1, along_wa) for c in range(1, along_col))
+        second = join([*reversed(first), *after], second, moves)
     second = [swap(block, c) for c, block in enumerate(second, 1)]
     where = tuple((along_wa + c - 1, a) if c else (a, 0) for a in range(along_wa) for c in range(along_col))
     return [blocks[0], *first, *second], where
@@ -346,35 +376,35 @@
     along_wa, along_col = lax.axis_size("wa"), lax.axis_size("col")
     half, half_wa = planes // 2, along_wa // 2
     far, near = tuple(range(half, planes)), tuple(range(half))
-    early, late = far[:2], far[2:]
     noise = quantile(noise_index)
     direct = tuple((p,) for p in range(planes))
     staged = staged_groups(along_wa, along_col)
-    staged_near = staged_groups(half_wa, along_col)
 
     def make_green(k, groups, after):
         return green_rows(walkers, intersection_inverse, k, tile_rows, groups, True, after)
 
     def ordered(received):
-        places = (*far, *near)
+        places = (*near[2:], *far, *near[:2])
         return [received[p] for p in places], tuple((places.index(p), 0) for p in range(planes))
 
-    split = [(p,) for p in early], [(p,) for p in late]
-    one = make_green(0, (*split[0], *staged_near[1:half_wa]), walkers)
-    two = make_green(0, (*split[1], staged_near[0], *staged_near[half_wa:]), one[0])
-    near_blocks = [two[len(late)], *one[len(early) :], *two[len(late) + 1 :]]
-    got_early = [swap(block, p) for p, block in zip(early, one)]
-    got_near = stage_along_wa(near_blocks, half_wa, along_col)
-    got_late = [swap(block, p) for p, block in zip(late, two)]
-    got, where = stage_along_col(near_blocks, got_near, half_wa, along_col, two[0])
-    held = load(cholesky, two[0])
-    shift = len(far)
+    short = along_wa - 1
+    staged_short = staged_groups(short, along_col)
+    last_ones = tuple((p,) for p in range(short * along_col, planes))
+    one = make_green(0, staged_short[1:short], walkers)
+    two = make_green(0, (*last_ones, staged_short[0], *staged_short[short:]), one[0])
+    blocks = [two[along_col], *one, *two[along_col + 1 :]]
+    orbitals, electrons = walkers.shape[1:]
+    cut = orbitals // 2 if orbitals % 256 == 0 and electrons <= orbitals // 2 else orbitals
+    held = [load(cholesky, 0, cut, two[0])]
+    direct_ones = [swap(block, p) for (p,), block in zip(last_ones, two)]
+    passing = stage_along_wa(blocks, short, along_col)
+    staged_ones, where = stage_along_col(blocks, passing, short, along_col, held)
     greens = (
-        [*got_early, *got_late, *got],
-        (*((i + shift, j) for i, j in where), *((i, 0) for i in range(shift))),
+        [*direct_ones, *staged_ones],
+        (*((i + along_col, j) for i, j in where), *((i, 0) for i in range(along_col))),
         True,
     )
-    token = held
+    token = passing[-1]
 
     def reduced(sums):
         distance = 1
@@ -387,7 +417,7 @@
             sums.append(lax.ppermute(sums[0], "wa", pairs))
         return sums
 
-    new, log_steps = walkers, []
+    new, log_steps = walkers, None
     waiting = None
     for k in range(walker_count):
         last = k == walker_count - 1
@@ -395,23 +425,27 @@
             later = make_green(k + 1, staged, token)
             token = later[0]
             coming = stage_along_wa(later, along_wa, along_col)
-        parts = reduced(bias_rows(held, noise[k : k + 1], *greens))
+        sums = bias_rows(held[0], noise[k : k + 1], *greens)
+        if k == 0 and cut < orbitals:
+            held.append(load(cholesky, cut, orbitals, sums))
+        parts = reduced(sums)
         if waiting is not None:
             first = stage_along_wa(waiting, along_wa, along_col)
         groups = direct if last else staged
-        blocks, log_all = potential_rows(parts, held, groups, True, later[0] if last else coming[half_wa - 1])
-        log_steps.append(lax.dynamic_index_in_dim(log_all[:, 0], lax.axis_index(PLANE), 0, keepdims=True))
+        after = later[0] if last else coming[half_wa - 1]
+        blocks, log_steps = potential_rows(parts, held, groups, True, log_steps, after)
+        walker = bring(walkers, k, log_steps)
+        got = {p: swap(blocks[p], p) for p in (*near[2:], *far, *near[:2])} if last else {}
         if waiting is not None:
-            new = taylor(
-                *stage_along_col(waiting, first, along_wa, along_col, log_all), True, walkers, k - 1, new, walkers
-            )
+            passed = [walker, before, log_steps]
+            new = taylor(*stage_along_col(waiting, first, along_wa, along_col, passed), before, k - 1, new, walkers)
+        before = walker
         if last:
-            got = {p: swap(block, p) for p, block in enumerate(blocks)}
-            new = taylor(*ordered(got), True, walkers, k, new, walkers)
+            new = taylor(*ordered(got), walker, k, new, walkers)
         else:
             waiting = blocks
-            greens = (*stage_along_col(later, coming, along_wa, along_col, log_all), True)
-    return new, jnp.concatenate(log_steps)
+            greens = (*stage_along_col(later, coming, along_wa, along_col, [log_steps]), True)
+    return new, log_steps
 
 
 def by_all_to_all(walkers, intersection_inverse, noise_index, cholesky):

time: 158 us -> 146 us (0.924); the launches traced: 155 us -> 145 us
  waiting for transfers between devices: 74.7 us -> 66.2 us
  Pallas kernels: 36.4 us -> 38.4 us
  other arithmetic: 1.92 us -> 0.05 us
    ppermute x4, waiting for transfers between devices: 12.3 us -> 7.06 us  [reduced(): sums.append(lax.ppermute(sums[0], 'wa', pairs))]
    ppermute x25 -> x24, waiting for transfers between devices: 62.4 us -> 59.2 us  [swap(): return lax.ppermute(block, PLANE, [(i, i ^ place) for i in range(planes)])]
    concatenate x1 -> x0, other arithmetic: 1.86 us -> none  [by_permutes(): return (new, jnp.concatenate(log_steps))]
    pallas_call x3 -> x6, Pallas kernels: 20.3 us -> 21.2 us  [the longest x2 11.1 us: taylor(): pl.pallas_call(functools.partial(taylor_kernel, k, where), in_specs=[IN_V...]
    ppermute x25 -> x24, starting transfers between devices: 35.1 us -> 34.7 us  [swap(): return lax.ppermute(block, PLANE, [(i, i ^ place) for i in range(planes)])]
  transfers between devices with their start and end apart: 29 -> 28, of which waited for: 11 -> 15; matrix products, arithmetic and copies ran while one was open for 2% -> 0% of each run, Pallas kernels for 17% -> 22%
where the time goes in v4:
time: 146 us; the launch traced here: 145 us
  waiting for transfers between devices  66.2 us (45%)
  starting transfers between devices  38.8 us (27%)
  Pallas kernels  38.4 us (26%)
    ppermute x24, waiting for transfers between devices, swap(): return lax.ppermute(block, PLANE, [(i, i ^ place) for i in range(planes)])  59.2 us
    ppermute x24, starting transfers between devices, swap(): return lax.ppermute(block, PLANE, [(i, i ^ place) for i in range(planes)])  34.7 us
    pallas_call x2, Pallas kernels, taylor(): pl.pallas_call(functools.partial(taylor_kernel, k, where), in_specs=[IN_V...  11.1 us
    pallas_call x2, Pallas kernels, load(): pl.pallas_call(functools.partial(load_kernel, start), in_specs=[IN_HBM, I...  7.22 us
    ppermute x4, waiting for transfers between devices, reduced(): sums.append(lax.ppermute(sums[0], 'wa', pairs))  7.06 us
    pallas_call x2, Pallas kernels, potential_rows(): pl.pallas_call(functools.partial(potential_kernel, groups, relative, len(...  6.69 us
    pallas_call x3, Pallas kernels, green_rows(): pl.pallas_call(functools.partial(green_kernel, k, groups, relative), in_s...  5.08 us
    ppermute x4, starting transfers between devices, reduced(): sums.append(lax.ppermute(sums[0], 'wa', pairs))  4.06 us
  transfers between devices with their start and end apart: 28, of which 15 were waited for; matrix products, arithmetic and copies ran while one was open for 0% of the time, Pallas kernels for 22%

profile of v4, /device:TPU:8, one launch (start us, length us, event | category | flops | bytes accessed | tf_op | source)
XLA Modules:
  0.0 145.3 jit_solution(12696065723992508000)
XLA Ops:
  0.6 1.6 %green_rows.3 = (bf16[2,128,384]{2,1,0:T(8,128)(2,1)S(1)}, bf16[2,128,384]{2,1,0:T(8,128)(2,1)S(1)}) custom-call(bf16[2,1024,384]{2,1,0:T(8,128)(2,1)} %refs_10_.1, bf16[2,384,384]{2,1,0:T(8,128)(2,1)} %inverse_ref.5, bf16[2,1024,384]{2,1,0:T(8,128)(2,1)} %refs_10_.1), custom_call_target="tpu_custom_call" | custom-call | tf_op jit(solution)/shard_map/green_rows/pallas_call | solution.py:95
  2.2 2.7 %collective-permute-start = (bf16[2,128,384]{2,1,0:T(8,128)(2,1)S(1)}, bf16[2,128,384]{2,1,0:T(8,128)(2,1)S(1)}, u32[]{:S(2)}, u32[]{:S(2)}) collective-permute-start(bf16[2,128,384]{2,1,0:T(8,128)(2,1)S(1)} %get-tuple-element.30), channel_id=1, source_target_pairs={{0,8},{2,10},{4,12},{6,14},{8,0},{10,2},{12,4},{14,6},{1,9},{3,11}... | collective-permute-start | bytes 589832 | tf_op jit(solution)/shard_map/ppermute | solution.py:320
  8.3 1.6 %collective-permute-start.4 = (bf16[1,128,384]{2,1,0:T(8,128)(2,1)S(1)}, bf16[1,128,384]{2,1,0:T(8,128)(2,1)S(1)}, u32[]{:S(2)}, u32[]{:S(2)}) collective-permute-start(bf16[1,128,384]{2,1,0:T(8,128)(2,1)S(1)} %get-tuple-element.29._), channel_id=1, source_target_pairs={{0,12},{2,14},{4,8},{6,10},{8,4},{10,6},{12,0},{14,2},{1,13},{3,15... | collective-permute-start | bytes 294920 | tf_op jit(solution)/shard_map/ppermute | solution.py:320
  9.9 3.6 %load_cholesky.2.refs_2_.chol_ref.refs_3_ = bf16[64,128,512]{2,1,0:T(8,128)(2,1)S(1)} custom-call(bf16[64,128,1024]{2,1,0:T(8,128)(2,1)} %chol_ref.3, bf16[1,128,384]{2,1,0:T(8,128)(2,1)S(1)} %get-tuple-element.29._), custom_call_target="tpu_custom_call" | custom-call | tf_op jit(solution)/shard_map/load_cholesky/pallas_call | solution.py:128
  17.2 2.0 %green_rows.5 = (bf16[1,128,384]{2,1,0:T(8,128)(2,1)S(1)}, bf16[2,128,384]{2,1,0:T(8,128)(2,1)S(1)}, bf16[2,128,384]{2,1,0:T(8,128)(2,1)S(1)}, bf16[2,128,384]{2,1,0:T(8,128)(2,1)S(1)}, bf16[4,128,384]{2,1,0:T(8,128)(2,1)S(1)}) custom-call(bf16[2,1024,384]{2,1,0:T(8,128)(2,1)} %refs_10_.1, bf16[2,384,384]{2,1,0:T(8,128)(2,1)} %inverse_ref.5, ...), custom_call_target="tpu_custom_call" | custom-call | tf_op jit(solution)/shard_map/green_rows/pallas_call | solution.py:95
  23.9 2.0 %bias_rows.2._ = f32[16,64]{1,0:T(8,128)S(1)} custom-call(bf16[64,128,512]{2,1,0:T(8,128)(2,1)S(1)} %load_cholesky.2.refs_2_.chol_ref.refs_3_, f32[1,64]{1,0:T(1,128)S(1)} %get-tuple-element.54.noise_ref, bf16[1,128,384]{2,1,0:T(8,128)(2,1)S(1)} %collective-permute-done.4.refs_0_, bf16[1,128,384]{2,1,0:T(8,128)(2,1)S(1)} %collective-permute-done.5.refs_1_, ...), custom_call_target="tpu_custom_call" | custom-call | tf_op jit(solution)/shard_map/bias_rows/pallas_call | solution.py:189
  27.4 2.3 %collective-permute-done.8 = f32[16,64]{1,0:T(8,128)S(1)} collective-permute-done((f32[16,64]{1,0:T(8,128)S(1)}, f32[16,64]{1,0:T(8,128)S(1)}, u32[]{:S(2)}, u32[]{:S(2)}) %collective-permute-start.8) | collective-permute-done | bytes 4128 | tf_op jit(solution)/shard_map/ppermute | solution.py:320
  29.6 1.6 %collective-permute-start.9 = (f32[16,64]{1,0:T(8,128)S(1)}, f32[16,64]{1,0:T(8,128)S(1)}, u32[]{:S(2)}, u32[]{:S(2)}) collective-permute-start(f32[16,64]{1,0:T(8,128)S(1)} %add.23), channel_id=1, source_target_pairs={{0,4},{2,6},{4,0},{6,2},{8,12},{10,14},{12,8},{14,10},{1,5},{3,7},... | collective-permute-start | bytes 12296 | tf_op jit(solution)/shard_map/ppermute | solution.py:320
  31.2 2.3 %collective-permute-done.9 = f32[16,64]{1,0:T(8,128)S(1)} collective-permute-done((f32[16,64]{1,0:T(8,128)S(1)}, f32[16,64]{1,0:T(8,128)S(1)}, u32[]{:S(2)}, u32[]{:S(2)}) %collective-permute-start.9) | collective-permute-done | bytes 4128 | tf_op jit(solution)/shard_map/ppermute | solution.py:320
  35.4 3.6 %load_cholesky.3.refs_4_ = bf16[64,128,512]{2,1,0:T(8,128)(2,1)S(1)} custom-call(bf16[64,128,1024]{2,1,0:T(8,128)(2,1)} %chol_ref.3, f32[16,64]{1,0:T(8,128)S(1)} %bias_rows.2._), custom_call_target="tpu_custom_call" | custom-call | tf_op jit(solution)/shard_map/load_cholesky/pallas_call | solution.py:128
  39.1 3.8 %collective-permute-done.10.refs_1_ = f32[16,64]{1,0:T(8,128)S(1)} collective-permute-done((f32[16,64]{1,0:T(8,128)S(1)}, f32[16,64]{1,0:T(8,128)S(1)}, u32[]{:S(2)}, u32[]{:S(2)}) %collective-permute-start.10) | collective-permute-done | bytes 4128 | tf_op jit(solution)/shard_map/ppermute | solution.py:417
  42.8 3.0 %potential_rows.2 = (bf16[1,128,1024]{2,1,0:T(8,128)(2,1)S(1)}, bf16[2,128,1024]{2,1,0:T(8,128)(2,1)S(1)}, bf16[2,128,1024]{2,1,0:T(8,128)(2,1)S(1)}, bf16[2,128...) custom-call(f32[16,64]{1,0:T(8,128)S(1)} %add.24.refs_0_, ...), custom_call_target="tpu_custom_call" | custom-call | tf_op jit(solution)/shard_map/potential_rows/pallas_call | solution.py:241
  45.9 2.3 %collective-permute-start.24 = (bf16[2,128,1024]{2,1,0:T(8,128)(2,1)S(1)}, bf16[2,128,1024]{2,1,0:T(8,128)(2,1)S(1)}, u32[]{:S(2)}, u32[]{:S(2)}) collective-permute-start(bf16[2,128,1024]{2,1,0:T(8,128)(2,1)S(1)} %get-tuple-element.50), channel_id=1, source_target_pairs={{0,4},{2,6},{4,0},{6,2},{8,12},{10,14},{12,8},{14,10},{1,5},{3,7},... | collective-permute-start | bytes 1572872 | tf_op jit(solution)/shard_map/ppermute | solution.py:320
  50.8 2.5 %collective-permute-start.12 = (bf16[4,128,384]{2,1,0:T(8,128)(2,1)S(1)}, bf16[4,128,384]{2,1,0:T(8,128)(2,1)S(1)}, u32[]{:S(2)}, u32[]{:S(2)}) collective-permute-start(bf16[4,128,384]{2,1,0:T(8,128)(2,1)S(1)} %join.4), channel_id=1, source_target_pairs={{0,2},{2,0},{4,6},{6,4},{8,10},{10,8},{12,14},{14,12},{1,3},{3,1},... | collective-permute-start | bytes 1179656 | tf_op jit(solution)/shard_map/ppermute | solution.py:320
  53.3 5.8 %collective-permute-done.12.refs_4_ = bf16[4,128,384]{2,1,0:T(8,128)(2,1)S(1)} collective-permute-done((bf16[4,128,384]{2,1,0:T(8,128)(2,1)S(1)}, bf16[4,128,384]{2,1,0:T(8,128)(2,1)S(1)}, u32[]{:S(2)}, u32[]{:S(2)}) %collective-permute-start.12) | collective-permute-done | bytes 393248 | tf_op jit(solution)/shard_map/ppermute | solution.py:320
  59.1 2.0 %bias_rows.3 = f32[16,64]{1,0:T(8,128)S(1)} custom-call(bf16[64,128,512]{2,1,0:T(8,128)(2,1)S(1)} %load_cholesky.2.refs_2_.chol_ref.refs_3_, f32[1,64]{1,0:T(1,128)S(1)} %get-tuple-element.55.noise_ref, bf16[1,128,384]{2,1,0:T(8,128)(2,1)S(1)} %get-tuple-element.31.refs_0_.refs_6_, bf16[2,128,384]{2,1,0:T(8,128)(2,1)S(1)} %collective-permute-done.1.refs_2_.refs_1_, ...), custom_call_target="tpu_custom_call" | custom-call | tf_op jit(solution)/shard_map/bias_rows/pallas_call | solution.py:189
  61.1 2.1 %collective-permute-start.13 = (f32[16,64]{1,0:T(8,128)S(1)}, f32[16,64]{1,0:T(8,128)S(1)}, u32[]{:S(2)}, u32[]{:S(2)}) collective-permute-start(f32[16,64]{1,0:T(8,128)S(1)} %bias_rows.3), channel_id=1, source_target_pairs={{0,2},{2,0},{4,6},{6,4},{8,10},{10,8},{12,14},{14,12},{1,3},{3,1},... | collective-permute-start | bytes 12296 | tf_op jit(solution)/shard_map/ppermute | solution.py:320
  63.3 1.6 %collective-permute-done.13 = f32[16,64]{1,0:T(8,128)S(1)} collective-permute-done((f32[16,64]{1,0:T(8,128)S(1)}, f32[16,64]{1,0:T(8,128)S(1)}, u32[]{:S(2)}, u32[]{:S(2)}) %collective-permute-start.13) | collective-permute-done | bytes 4128 | tf_op jit(solution)/shard_map/ppermute | solution.py:320
  64.9 2.8 %collective-permute-start.14 = (f32[16,64]{1,0:T(8,128)S(1)}, f32[16,64]{1,0:T(8,128)S(1)}, u32[]{:S(2)}, u32[]{:S(2)}) collective-permute-start(f32[16,64]{1,0:T(8,128)S(1)} %add.25), channel_id=1, source_target_pairs={{0,4},{2,6},{4,0},{6,2},{8,12},{10,14},{12,8},{14,10},{1,5},{3,7},... | collective-permute-start | bytes 12296 | tf_op jit(solution)/shard_map/ppermute | solution.py:320
  67.7 12.7 %collective-permute-done.14 = f32[16,64]{1,0:T(8,128)S(1)} collective-permute-done((f32[16,64]{1,0:T(8,128)S(1)}, f32[16,64]{1,0:T(8,128)S(1)}, u32[]{:S(2)}, u32[]{:S(2)}) %collective-permute-start.14) | collective-permute-done | bytes 4128 | tf_op jit(solution)/shard_map/ppermute | solution.py:320
  82.6 1.8 %bring_walker.3.refs_4_.refs_5_ = bf16[1024,384]{1,0:T(8,128)(2,1)S(1)} custom-call(bf16[2,1024,384]{2,1,0:T(8,128)(2,1)} %refs_10_.1, f32[1]{0:T(128)} %get-tuple-element.38.refs_3_.refs_5_._), custom_call_target="tpu_custom_call" | custom-call | tf_op jit(solution)/shard_map/bring_walker/pallas_call | solution.py:147
  84.4 3.3 %collective-permute-done.15.refs_1_ = f32[16,64]{1,0:T(8,128)S(1)} collective-permute-done((f32[16,64]{1,0:T(8,128)S(1)}, f32[16,64]{1,0:T(8,128)S(1)}, u32[]{:S(2)}, u32[]{:S(2)}) %collective-permute-start.15) | collective-permute-done | bytes 4128 | tf_op jit(solution)/shard_map/ppermute | solution.py:417
  87.7 3.7 %potential_rows.3 = (bf16[1,128,1024]{2,1,0:T(8,128)(2,1)S(1)}, bf16[1,128,1024]{2,1,0:T(8,128)(2,1)S(1)}, bf16[1,128,1024]{2,1,0:T(8,128)(2,1)S(1)}, bf16[1,128...) custom-call(f32[16,64]{1,0:T(8,128)S(1)} %add.26.refs_0_, ...), custom_call_target="tpu_custom_call" | custom-call | tf_op jit(solution)/shard_map/potential_rows/pallas_call | solution.py:241
  94.7 2.3 %collective-permute-start.18 = (bf16[1,128,1024]{2,1,0:T(8,128)(2,1)S(1)}, bf16[1,128,1024]{2,1,0:T(8,128)(2,1)S(1)}, u32[]{:S(2)}, u32[]{:S(2)}) collective-permute-start(bf16[1,128,1024]{2,1,0:T(8,128)(2,1)S(1)} %get-tuple-element.41), channel_id=1, source_target_pairs={{0,6},{2,4},{4,2},{6,0},{8,14},{10,12},{12,10},{14,8},{1,7},{3,5},... | collective-permute-start | bytes 786440 | tf_op jit(solution)/shard_map/ppermute | solution.py:320
  97.3 3.3 %collective-permute-start.20 = (bf16[1,128,1024]{2,1,0:T(8,128)(2,1)S(1)}, bf16[1,128,1024]{2,1,0:T(8,128)(2,1)S(1)}, u32[]{:S(2)}, u32[]{:S(2)}) collective-permute-start(bf16[1,128,1024]{2,1,0:T(8,128)(2,1)S(1)} %get-tuple-element.43), channel_id=1, source_target_pairs={{0,10},{2,8},{4,14},{6,12},{8,2},{10,0},{12,6},{14,4},{1,11},{3,9}... | collective-permute-start | bytes 786440 | tf_op jit(solution)/shard_map/ppermute | solution.py:320
  100.5 4.3 %collective-permute-done.17.refs_0_ = bf16[1,128,1024]{2,1,0:T(8,128)(2,1)S(1)} collective-permute-done((bf16[1,128,1024]{2,1,0:T(8,128)(2,1)S(1)}, bf16[1,128,1024]{2,1,0:T(8,128)(2,1)S(1)}, u32[]{:S(2)}, u32[]{:S(2)}) %collective-permute-start.17) | collective-permute-done | bytes 262176 | tf_op jit(solution)/shard_map/ppermute | solution.py:320
  106.2 5.8 %collective-permute-done.18.refs_1_ = bf16[1,128,1024]{2,1,0:T(8,128)(2,1)S(1)} collective-permute-done((bf16[1,128,1024]{2,1,0:T(8,128)(2,1)S(1)}, bf16[1,128,1024]{2,1,0:T(8,128)(2,1)S(1)}, u32[]{:S(2)}, u32[]{:S(2)}) %collective-permute-start.18) | collective-permute-done | bytes 262176 | tf_op jit(solution)/shard_map/ppermute | solution.py:320
  112.1 15.3 %collective-permute-done.27.refs_4_ = bf16[4,128,1024]{2,1,0:T(8,128)(2,1)S(1)} collective-permute-done((bf16[4,128,1024]{2,1,0:T(8,128)(2,1)S(1)}, bf16[4,128,1024]{2,1,0:T(8,128)(2,1)S(1)}, u32[]{:S(2)}, u32[]{:S(2)}) %collective-permute-start.27) | collective-permute-done | bytes 1048608 | tf_op jit(solution)/shard_map/ppermute | solution.py:320
  127.7 5.6 %taylor.2.refs_9_ = bf16[2,1024,384]{2,1,0:T(8,128)(2,1)} custom-call(bf16[1,128,1024]{2,1,0:T(8,128)(2,1)S(1)} %get-tuple-element.49.refs_0_, bf16[2,128,1024]{2,1,0:T(8,128)(2,1)S(1)} %collective-permute-done.24.refs_2_.refs_1_, bf16[2,128,1024]{2,1,0:T(8,128)(2,1)S(1)} %collective-permute-done.25.refs_1_.refs_2_, ...), custom_call_target="tpu_custom_call" | custom-call | tf_op jit(solution)/shard_map/taylor/pallas_call | solution.py:297
  133.2 3.6 %collective-permute-done.21.refs_4_ = bf16[1,128,1024]{2,1,0:T(8,128)(2,1)S(1)} collective-permute-done((bf16[1,128,1024]{2,1,0:T(8,128)(2,1)S(1)}, bf16[1,128,1024]{2,1,0:T(8,128)(2,1)S(1)}, u32[]{:S(2)}, u32[]{:S(2)}) %collective-permute-start.21) | collective-permute-done | bytes 262176 | tf_op jit(solution)/shard_map/ppermute | solution.py:320
  136.9 2.8 %collective-permute-done.22.refs_5_ = bf16[1,128,1024]{2,1,0:T(8,128)(2,1)S(1)} collective-permute-done((bf16[1,128,1024]{2,1,0:T(8,128)(2,1)S(1)}, bf16[1,128,1024]{2,1,0:T(8,128)(2,1)S(1)}, u32[]{:S(2)}, u32[]{:S(2)}) %collective-permute-start.22) | collective-permute-done | bytes 262176 | tf_op jit(solution)/shard_map/ppermute | solution.py:320
  139.6 5.5 %taylor.3 = bf16[2,1024,384]{2,1,0:T(8,128)(2,1)} custom-call(bf16[1,128,1024]{2,1,0:T(8,128)(2,1)S(1)} %collective-permute-done.17.refs_0_, bf16[1,128,1024]{2,1,0:T(8,128)(2,1)S(1)} %collective-permute-done.18.refs_1_, bf16[1,128,1024]{2,1,0:T(8,128)(2,1)S(1)} %collective-permute-done.19.refs_2_, ...), custom_call_target="tpu_custom_call", output_to_operand_aliasing={{}: (9, {})} | custom-call | tf_op jit(solution)/shard_map/taylor/pallas_call | solution.py:297
  (52 shorter events, 25.3 us)
Async XLA Ops:
  2.2 11.9 %collective-permute-start = (bf16[2,128,384]{2,1,0:T(8,128)(2,1)S(1)}, bf16[2,128,384]{2,1,0:T(8,128)(2,1)S(1)}, u32[]{:S(2)}, u32[]{:S(2)}) collective-permute-start(bf16[2,128,384]{2,1,0:T(8,128)(2,1)S(1)} %get-tuple-element.30), channel_id=1, source_target_pairs={{0,8},{2,10},{4,12},{6,14},{8,0},{10,2},{12,4},{14,6},{1,9},{3,11}... | collective-permute-start | bytes 589832 | tf_op jit(solution)/shard_map/ppermute | solution.py:320
  4.9 10.5 %collective-permute-start.6 = (bf16[2,128,384]{2,1,0:T(8,128)(2,1)S(1)}, bf16[2,128,384]{2,1,0:T(8,128)(2,1)S(1)}, u32[]{:S(2)}, u32[]{:S(2)}) collective-permute-start(bf16[2,128,384]{2,1,0:T(8,128)(2,1)S(1)} %get-tuple-element.28._), channel_id=1, source_target_pairs={{0,4},{2,6},{4,0},{6,2},{8,12},{10,14},{12,8},{14,10},{1,5},{3,7},... | collective-permute-start | bytes 589832 | tf_op jit(solution)/shard_map/ppermute | solution.py:320
  6.9 14.9 %collective-permute-start.5 = (bf16[1,128,384]{2,1,0:T(8,128)(2,1)S(1)}, bf16[1,128,384]{2,1,0:T(8,128)(2,1)S(1)}, u32[]{:S(2)}, u32[]{:S(2)}) collective-permute-start(bf16[1,128,384]{2,1,0:T(8,128)(2,1)S(1)} %get-tuple-element.35), channel_id=1, source_target_pairs={{0,14},{2,12},{4,10},{6,8},{8,6},{10,4},{12,2},{14,0},{1,15},{3,13... | collective-permute-start | bytes 294920 | tf_op jit(solution)/shard_map/ppermute | solution.py:320
  8.3 14.7 %collective-permute-start.4 = (bf16[1,128,384]{2,1,0:T(8,128)(2,1)S(1)}, bf16[1,128,384]{2,1,0:T(8,128)(2,1)S(1)}, u32[]{:S(2)}, u32[]{:S(2)}) collective-permute-start(bf16[1,128,384]{2,1,0:T(8,128)(2,1)S(1)} %get-tuple-element.29._), channel_id=1, source_target_pairs={{0,12},{2,14},{4,8},{6,10},{8,4},{10,6},{12,0},{14,2},{1,13},{3,15... | collective-permute-start | bytes 294920 | tf_op jit(solution)/shard_map/ppermute | solution.py:320
  13.5 3.6 %copy-start.2 = (s32[2,64]{1,0:T(2,128)S(1)}, s32[2,64]{1,0:T(2,128)}, u32[]{:S(2)}) copy-start(s32[2,64]{1,0:T(2,128)} %param.6) | copy-start | bytes 1540
  15.6 8.3 %collective-permute-start.7 = (bf16[3,128,384]{2,1,0:T(8,128)(2,1)S(1)}, bf16[3,128,384]{2,1,0:T(8,128)(2,1)S(1)}, u32[]{:S(2)}, u32[]{:S(2)}) collective-permute-start(bf16[3,128,384]{2,1,0:T(8,128)(2,1)S(1)} %join.3), channel_id=1, source_target_pairs={{0,2},{2,0},{4,6},{6,4},{8,10},{10,8},{12,14},{14,12},{1,3},{3,1},... | collective-permute-start | bytes 884744 | tf_op jit(solution)/shard_map/ppermute | solution.py:320
  19.1 30.6 %collective-permute-start.1 = (bf16[2,128,384]{2,1,0:T(8,128)(2,1)S(1)}, bf16[2,128,384]{2,1,0:T(8,128)(2,1)S(1)}, u32[]{:S(2)}, u32[]{:S(2)}) collective-permute-start(bf16[2,128,384]{2,1,0:T(8,128)(2,1)S(1)} %get-tuple-element.32), channel_id=1, source_target_pairs={{0,4},{2,6},{4,0},{6,2},{8,12},{10,14},{12,8},{14,10},{1,5},{3,7},... | collective-permute-start | bytes 589832 | tf_op jit(solution)/shard_map/ppermute | solution.py:320
  20.6 18.4 %collective-permute-start.2 = (bf16[2,128,384]{2,1,0:T(8,128)(2,1)S(1)}, bf16[2,128,384]{2,1,0:T(8,128)(2,1)S(1)}, u32[]{:S(2)}, u32[]{:S(2)}) collective-permute-start(bf16[2,128,384]{2,1,0:T(8,128)(2,1)S(1)} %get-tuple-element.33), channel_id=1, source_target_pairs={{0,8},{2,10},{4,12},{6,14},{8,0},{10,2},{12,4},{14,6},{1,9},{3,11}... | collective-permute-start | bytes 589832 | tf_op jit(solution)/shard_map/ppermute | solution.py:320
  21.7 28.0 %collective-permute-start.3 = (bf16[2,128,384]{2,1,0:T(8,128)(2,1)S(1)}, bf16[2,128,384]{2,1,0:T(8,128)(2,1)S(1)}, u32[]{:S(2)}, u32[]{:S(2)}) collective-permute-start(bf16[2,128,384]{2,1,0:T(8,128)(2,1)S(1)} %get-tuple-element.34), channel_id=1, source_target_pairs={{0,12},{2,14},{4,8},{6,10},{8,4},{10,6},{12,0},{14,2},{1,13},{3,15... | collective-permute-start | bytes 589832 | tf_op jit(solution)/shard_map/ppermute | solution.py:320
  25.9 3.7 %collective-permute-start.8 = (f32[16,64]{1,0:T(8,128)S(1)}, f32[16,64]{1,0:T(8,128)S(1)}, u32[]{:S(2)}, u32[]{:S(2)}) collective-permute-start(f32[16,64]{1,0:T(8,128)S(1)} %bias_rows.2._), channel_id=1, source_target_pairs={{0,2},{2,0},{4,6},{6,4},{8,10},{10,8},{12,14},{14,12},{1,3},{3,1},... | collective-permute-start | bytes 12296 | tf_op jit(solution)/shard_map/ppermute | solution.py:320
  29.6 3.9 %collective-permute-start.9 = (f32[16,64]{1,0:T(8,128)S(1)}, f32[16,64]{1,0:T(8,128)S(1)}, u32[]{:S(2)}, u32[]{:S(2)}) collective-permute-start(f32[16,64]{1,0:T(8,128)S(1)} %add.23), channel_id=1, source_target_pairs={{0,4},{2,6},{4,0},{6,2},{8,12},{10,14},{12,8},{14,10},{1,5},{3,7},... | collective-permute-start | bytes 12296 | tf_op jit(solution)/shard_map/ppermute | solution.py:320
  33.5 5.6 %collective-permute-start.11 = (f32[16,64]{1,0:T(8,128)S(1)}, f32[16,64]{1,0:T(8,128)S(1)}, u32[]{:S(2)}, u32[]{:S(2)}) collective-permute-start(f32[16,64]{1,0:T(8,128)S(1)} %add.24.refs_0_), channel_id=1, source_target_pairs={{0,12},{12,0},{1,13},{13,1},{2,14},{14,2},{3,15},{15,3},{16,28},{2... | collective-permute-start | bytes 12296 | tf_op jit(solution)/shard_map/ppermute | solution.py:417
  34.1 8.7 %collective-permute-start.10 = (f32[16,64]{1,0:T(8,128)S(1)}, f32[16,64]{1,0:T(8,128)S(1)}, u32[]{:S(2)}, u32[]{:S(2)}) collective-permute-start(f32[16,64]{1,0:T(8,128)S(1)} %add.24.refs_0_), channel_id=1, source_target_pairs={{0,8},{12,4},{1,9},{13,5},{2,10},{14,6},{3,11},{15,7},{16,24},{28,... | collective-permute-start | bytes 12296 | tf_op jit(solution)/shard_map/ppermute | solution.py:417
  45.9 47.4 %collective-permute-start.24 = (bf16[2,128,1024]{2,1,0:T(8,128)(2,1)S(1)}, bf16[2,128,1024]{2,1,0:T(8,128)(2,1)S(1)}, u32[]{:S(2)}, u32[]{:S(2)}) collective-permute-start(bf16[2,128,1024]{2,1,0:T(8,128)(2,1)S(1)} %get-tuple-element.50), channel_id=1, source_target_pairs={{0,4},{2,6},{4,0},{6,2},{8,12},{10,14},{12,8},{14,10},{1,5},{3,7},... | collective-permute-start | bytes 1572872 | tf_op jit(solution)/shard_map/ppermute | solution.py:320
  48.2 45.1 %collective-permute-start.25 = (bf16[2,128,1024]{2,1,0:T(8,128)(2,1)S(1)}, bf16[2,128,1024]{2,1,0:T(8,128)(2,1)S(1)}, u32[]{:S(2)}, u32[]{:S(2)}) collective-permute-start(bf16[2,128,1024]{2,1,0:T(8,128)(2,1)S(1)} %get-tuple-element.51), channel_id=1, source_target_pairs={{0,8},{2,10},{4,12},{6,14},{8,0},{10,2},{12,4},{14,6},{1,9},{3,11}... | collective-permute-start | bytes 1572872 | tf_op jit(solution)/shard_map/ppermute | solution.py:320
  49.1 44.2 %collective-permute-start.26 = (bf16[2,128,1024]{2,1,0:T(8,128)(2,1)S(1)}, bf16[2,128,1024]{2,1,0:T(8,128)(2,1)S(1)}, u32[]{:S(2)}, u32[]{:S(2)}) collective-permute-start(bf16[2,128,1024]{2,1,0:T(8,128)(2,1)S(1)} %get-tuple-element.52), channel_id=1, source_target_pairs={{0,12},{2,14},{4,8},{6,10},{8,4},{10,6},{12,0},{14,2},{1,13},{3,15... | collective-permute-start | bytes 1572872 | tf_op jit(solution)/shard_map/ppermute | solution.py:320
  50.8 8.3 %collective-permute-start.12 = (bf16[4,128,384]{2,1,0:T(8,128)(2,1)S(1)}, bf16[4,128,384]{2,1,0:T(8,128)(2,1)S(1)}, u32[]{:S(2)}, u32[]{:S(2)}) collective-permute-start(bf16[4,128,384]{2,1,0:T(8,128)(2,1)S(1)} %join.4), channel_id=1, source_target_pairs={{0,2},{2,0},{4,6},{6,4},{8,10},{10,8},{12,14},{14,12},{1,3},{3,1},... | collective-permute-start | bytes 1179656 | tf_op jit(solution)/shard_map/ppermute | solution.py:320
  61.1 3.8 %collective-permute-start.13 = (f32[16,64]{1,0:T(8,128)S(1)}, f32[16,64]{1,0:T(8,128)S(1)}, u32[]{:S(2)}, u32[]{:S(2)}) collective-permute-start(f32[16,64]{1,0:T(8,128)S(1)} %bias_rows.3), channel_id=1, source_target_pairs={{0,2},{2,0},{4,6},{6,4},{8,10},{10,8},{12,14},{14,12},{1,3},{3,1},... | collective-permute-start | bytes 12296 | tf_op jit(solution)/shard_map/ppermute | solution.py:320
  64.9 15.6 %collective-permute-start.14 = (f32[16,64]{1,0:T(8,128)S(1)}, f32[16,64]{1,0:T(8,128)S(1)}, u32[]{:S(2)}, u32[]{:S(2)}) collective-permute-start(f32[16,64]{1,0:T(8,128)S(1)} %add.25), channel_id=1, source_target_pairs={{0,4},{2,6},{4,0},{6,2},{8,12},{10,14},{12,8},{14,10},{1,5},{3,7},... | collective-permute-start | bytes 12296 | tf_op jit(solution)/shard_map/ppermute | solution.py:320
  80.5 3.9 %collective-permute-start.16 = (f32[16,64]{1,0:T(8,128)S(1)}, f32[16,64]{1,0:T(8,128)S(1)}, u32[]{:S(2)}, u32[]{:S(2)}) collective-permute-start(f32[16,64]{1,0:T(8,128)S(1)} %add.26.refs_0_), channel_id=1, source_target_pairs={{0,12},{12,0},{1,13},{13,1},{2,14},{14,2},{3,15},{15,3},{16,28},{2... | collective-permute-start | bytes 12296 | tf_op jit(solution)/shard_map/ppermute | solution.py:417
  81.1 6.6 %collective-permute-start.15 = (f32[16,64]{1,0:T(8,128)S(1)}, f32[16,64]{1,0:T(8,128)S(1)}, u32[]{:S(2)}, u32[]{:S(2)}) collective-permute-start(f32[16,64]{1,0:T(8,128)S(1)} %add.26.refs_0_), channel_id=1, source_target_pairs={{0,8},{12,4},{1,9},{13,5},{2,10},{14,6},{3,11},{15,7},{16,24},{28,... | collective-permute-start | bytes 12296 | tf_op jit(solution)/shard_map/ppermute | solution.py:417
  91.3 48.3 %copy-start = (bf16[2,1024,384]{2,1,0:T(8,128)(2,1)S(1)}, bf16[2,1024,384]{2,1,0:T(8,128)(2,1)}, u32[]{:S(2)}) copy-start(bf16[2,1024,384]{2,1,0:T(8,128)(2,1)} %refs_10_.1) | copy-start | bytes 4718596
  91.4 0.8 copy-start.1
  93.4 34.0 %collective-permute-start.27 = (bf16[4,128,1024]{2,1,0:T(8,128)(2,1)S(1)}, bf16[4,128,1024]{2,1,0:T(8,128)(2,1)S(1)}, u32[]{:S(2)}, u32[]{:S(2)}) collective-permute-start(bf16[4,128,1024]{2,1,0:T(8,128)(2,1)S(1)} %join.5), channel_id=1, source_target_pairs={{0,2},{2,0},{4,6},{6,4},{8,10},{10,8},{12,14},{14,12},{1,3},{3,1},... | collective-permute-start | bytes 3145736 | tf_op jit(solution)/shard_map/ppermute | solution.py:320
  94.7 10.1 %collective-permute-start.17 = (bf16[1,128,1024]{2,1,0:T(8,128)(2,1)S(1)}, bf16[1,128,1024]{2,1,0:T(8,128)(2,1)S(1)}, u32[]{:S(2)}, u32[]{:S(2)}) collective-permute-start(bf16[1,128,1024]{2,1,0:T(8,128)(2,1)S(1)} %get-tuple-element.40), channel_id=1, source_target_pairs={{0,4},{2,6},{4,0},{6,2},{8,12},{10,14},{12,8},{14,10},{1,5},{3,7},... | collective-permute-start | bytes 786440 | tf_op jit(solution)/shard_map/ppermute | solution.py:320
  94.7 17.4 %collective-permute-start.18 = (bf16[1,128,1024]{2,1,0:T(8,128)(2,1)S(1)}, bf16[1,128,1024]{2,1,0:T(8,128)(2,1)S(1)}, u32[]{:S(2)}, u32[]{:S(2)}) collective-permute-start(bf16[1,128,1024]{2,1,0:T(8,128)(2,1)S(1)} %get-tuple-element.41), channel_id=1, source_target_pairs={{0,6},{2,4},{4,2},{6,0},{8,14},{10,12},{12,10},{14,8},{1,7},{3,5},... | collective-permute-start | bytes 786440 | tf_op jit(solution)/shard_map/ppermute | solution.py:320
  97.0 36.3 %collective-permute-start.19 = (bf16[1,128,1024]{2,1,0:T(8,128)(2,1)S(1)}, bf16[1,128,1024]{2,1,0:T(8,128)(2,1)S(1)}, u32[]{:S(2)}, u32[]{:S(2)}) collective-permute-start(bf16[1,128,1024]{2,1,0:T(8,128)(2,1)S(1)} %get-tuple-element.42), channel_id=1, source_target_pairs={{0,8},{2,10},{4,12},{6,14},{8,0},{10,2},{12,4},{14,6},{1,9},{3,11}... | collective-permute-start | bytes 786440 | tf_op jit(solution)/shard_map/ppermute | solution.py:320
  97.3 36.0 %collective-permute-start.20 = (bf16[1,128,1024]{2,1,0:T(8,128)(2,1)S(1)}, bf16[1,128,1024]{2,1,0:T(8,128)(2,1)S(1)}, u32[]{:S(2)}, u32[]{:S(2)}) collective-permute-start(bf16[1,128,1024]{2,1,0:T(8,128)(2,1)S(1)} %get-tuple-element.43), channel_id=1, source_target_pairs={{0,10},{2,8},{4,14},{6,12},{8,2},{10,0},{12,6},{14,4},{1,11},{3,9}... | collective-permute-start | bytes 786440 | tf_op jit(solution)/shard_map/ppermute | solution.py:320
  104.8 32.1 %collective-permute-start.21 = (bf16[1,128,1024]{2,1,0:T(8,128)(2,1)S(1)}, bf16[1,128,1024]{2,1,0:T(8,128)(2,1)S(1)}, u32[]{:S(2)}, u32[]{:S(2)}) collective-permute-start(bf16[1,128,1024]{2,1,0:T(8,128)(2,1)S(1)} %get-tuple-element.44), channel_id=1, source_target_pairs={{0,12},{2,14},{4,8},{6,10},{8,4},{10,6},{12,0},{14,2},{1,13},{3,15... | collective-permute-start | bytes 786440 | tf_op jit(solution)/shard_map/ppermute | solution.py:320
  112.0 27.6 %collective-permute-start.22 = (bf16[1,128,1024]{2,1,0:T(8,128)(2,1)S(1)}, bf16[1,128,1024]{2,1,0:T(8,128)(2,1)S(1)}, u32[]{:S(2)}, u32[]{:S(2)}) collective-permute-start(bf16[1,128,1024]{2,1,0:T(8,128)(2,1)S(1)} %get-tuple-element.45), channel_id=1, source_target_pairs={{0,14},{2,12},{4,10},{6,8},{8,6},{10,4},{12,2},{14,0},{1,15},{3,13... | collective-permute-start | bytes 786440 | tf_op jit(solution)/shard_map/ppermute | solution.py:320
  127.4 12.3 %collective-permute-start.23 = (bf16[1,128,1024]{2,1,0:T(8,128)(2,1)S(1)}, bf16[1,128,1024]{2,1,0:T(8,128)(2,1)S(1)}, u32[]{:S(2)}, u32[]{:S(2)}) collective-permute-start(bf16[1,128,1024]{2,1,0:T(8,128)(2,1)S(1)} %get-tuple-element.47), channel_id=1, source_target_pairs={{0,2},{2,0},{4,6},{6,4},{8,10},{10,8},{12,14},{14,12},{1,3},{3,1},... | collective-permute-start | bytes 786440 | tf_op jit(solution)/shard_map/ppermute | solution.py:320

commit v5 on v4

--- a/solution.py
+++ b/solution.py
@@ -320,6 +320,22 @@
     return lax.ppermute(block, PLANE, [(i, i ^ place) for i in range(planes)])
 
 
+def plus_kernel(a_ref, b_ref, _, out_ref):
+    out_ref[...] = a_ref[...] + b_ref[...]
+
+
+def plus(a, b, after):
+    return pl.pallas_call(
+        plus_kernel,
+        in_specs=[IN_VMEM, IN_VMEM, IN_ANY],
+        out_specs=IN_VMEM,
+        out_shape=jax.ShapeDtypeStruct(a.shape, a.dtype),
+        compiler_params=kernel_params(),
+        cost_estimate=NO_COST,
+        name="plus",
+    )(a, b, after)
+
+
 def join_kernel(moves, sources, *refs):
     outs, arrived = refs[-1 - (len(refs) - sources - 1) // 2 : -1], refs[-1]
     copies = [
@@ -384,7 +400,7 @@
         return green_rows(walkers, intersection_inverse, k, tile_rows, groups, True, after)
 
     def ordered(received):
-        places = (*near[2:], *far, *near[:2])
+        places = (*near[along_col:], *far, *near[:along_col])
         return [received[p] for p in places], tuple((places.index(p), 0) for p in range(planes))
 
     short = along_wa - 1
@@ -394,8 +410,9 @@
     two = make_green(0, (*last_ones, staged_short[0], *staged_short[short:]), one[0])
     blocks = [two[along_col], *one, *two[along_col + 1 :]]
     orbitals, electrons = walkers.shape[1:]
-    cut = orbitals // 2 if orbitals % 256 == 0 and electrons <= orbitals // 2 else orbitals
+    cut = orbitals // 2 if orbitals % 512 == 0 and electrons <= orbitals // 2 else orbitals
     held = [load(cholesky, 0, cut, two[0])]
+    rest = [(cut, cut + (orbitals - cut) // 2), (cut + (orbitals - cut) // 2, orbitals)] if cut < orbitals else []
     direct_ones = [swap(block, p) for (p,), block in zip(last_ones, two)]
     passing = stage_along_wa(blocks, short, along_col)
     staged_ones, where = stage_along_col(blocks, passing, short, along_col, held)
@@ -409,7 +426,9 @@
     def reduced(sums):
         distance = 1
         while distance < half:
-            sums = sums + swap(sums, distance)
+            if rest:
+                held.append(load(cholesky, *rest.pop(0), sums))
+            sums = plus(sums, swap(sums, distance), held[-1])
             distance *= 2
         sums = [sums]
         for j in range(half_wa):
@@ -426,16 +445,14 @@
             token = later[0]
             coming = stage_along_wa(later, along_wa, along_col)
         sums = bias_rows(held[0], noise[k : k + 1], *greens)
-        if k == 0 and cut < orbitals:
-            held.append(load(cholesky, cut, orbitals, sums))
         parts = reduced(sums)
         if waiting is not None:
             first = stage_along_wa(waiting, along_wa, along_col)
         groups = direct if last else staged
-        after = later[0] if last else coming[half_wa - 1]
+        after = sums if last else coming[half_wa - 1]
         blocks, log_steps = potential_rows(parts, held, groups, True, log_steps, after)
         walker = bring(walkers, k, log_steps)
-        got = {p: swap(blocks[p], p) for p in (*near[2:], *far, *near[:2])} if last else {}
+        got = {p: swap(blocks[p], p) for p in (*near[along_col:], *far, *near[:along_col])} if last else {}
         if waiting is not None:
             passed = [walker, before, log_steps]
             new = taylor(*stage_along_col(waiting, first, along_wa, along_col, passed), before, k - 1, new, walkers)
@@ -480,7 +497,12 @@
 def per_device(walkers, intersection_inverse, noise_index, cholesky):
     planes = lax.axis_size(PLANE)
     tile_rows = cholesky.shape[1]
-    permutes = 2 <= planes <= MOST_PERMUTES and planes & (planes - 1) == 0 and tile_rows % ROWS == 0
+    permutes = (
+        4 <= lax.axis_size("wa")
+        and planes <= MOST_PERMUTES
+        and planes & (planes - 1) == 0
+        and tile_rows % ROWS == 0
+    )
     step = by_permutes if permutes else by_all_to_all
     return step(walkers, intersection_inverse, noise_index, cholesky)
 

time: 146 us -> 145 us (level)
  waiting for transfers between devices: 66.2 us -> 62.9 us
    ppermute x24, waiting for transfers between devices: 59.2 us -> 52.3 us  [swap(): return lax.ppermute(block, PLANE, [(i, i ^ place) for i in range(planes)])]
    ppermute x4, waiting for transfers between devices: 7.06 us -> 10.6 us  [reduced(): sums.append(lax.ppermute(sums[0], 'wa', pairs))]
    pallas_call x2 -> x3, Pallas kernels: 7.22 us -> 8.21 us  [load(): pl.pallas_call(functools.partial(load_kernel, start), in_specs=[IN_HBM, I...]
  transfers between devices with their start and end apart: 28 -> 28, of which waited for: 15 -> 13; matrix products, arithmetic and copies ran while one was open for 0% -> 0% of each run, Pallas kernels for 22% -> 22%
where the time goes in v5:
time: 145 us; the launch traced here: 144 us
  waiting for transfers between devices  62.9 us (43%)
  starting transfers between devices  40.2 us (28%)
  Pallas kernels  39.5 us (27%)
    ppermute x24, waiting for transfers between devices, swap(): return lax.ppermute(block, PLANE, [(i, i ^ place) for i in range(planes)])  52.3 us
    ppermute x24, starting transfers between devices, swap(): return lax.ppermute(block, PLANE, [(i, i ^ place) for i in range(planes)])  36.1 us
    pallas_call x2, Pallas kernels, taylor(): pl.pallas_call(functools.partial(taylor_kernel, k, where), in_specs=[IN_V...  11.1 us
    ppermute x4, waiting for transfers between devices, reduced(): sums.append(lax.ppermute(sums[0], 'wa', pairs))  10.6 us
    pallas_call x3, Pallas kernels, load(): pl.pallas_call(functools.partial(load_kernel, start), in_specs=[IN_HBM, I...  8.21 us
    pallas_call x2, Pallas kernels, potential_rows(): pl.pallas_call(functools.partial(potential_kernel, groups, relative, len(...  6.69 us
    pallas_call x3, Pallas kernels, green_rows(): pl.pallas_call(functools.partial(green_kernel, k, groups, relative), in_s...  5.08 us
    ppermute x4, starting transfers between devices, reduced(): sums.append(lax.ppermute(sums[0], 'wa', pairs))  4.08 us
  transfers between devices with their start and end apart: 28, of which 13 were waited for; matrix products, arithmetic and copies ran while one was open for 0% of the time, Pallas kernels for 22%

profile of v5, /device:TPU:8, one launch (start us, length us, event | category | flops | bytes accessed | tf_op | source)
XLA Modules:
  0.0 144.4 jit_solution(4743116268288855273)
XLA Ops:
  0.6 1.6 %green_rows.3 = (bf16[2,128,384]{2,1,0:T(8,128)(2,1)S(1)}, bf16[2,128,384]{2,1,0:T(8,128)(2,1)S(1)}) custom-call(bf16[2,1024,384]{2,1,0:T(8,128)(2,1)} %refs_10_.1, bf16[2,384,384]{2,1,0:T(8,128)(2,1)} %inverse_ref.5, bf16[2,1024,384]{2,1,0:T(8,128)(2,1)} %refs_10_.1), custom_call_target="tpu_custom_call" | custom-call | tf_op jit(solution)/shard_map/green_rows/pallas_call | solution.py:95
  2.2 2.7 %collective-permute-start = (bf16[2,128,384]{2,1,0:T(8,128)(2,1)S(1)}, bf16[2,128,384]{2,1,0:T(8,128)(2,1)S(1)}, u32[]{:S(2)}, u32[]{:S(2)}) collective-permute-start(bf16[2,128,384]{2,1,0:T(8,128)(2,1)S(1)} %get-tuple-element.30), channel_id=1, source_target_pairs={{0,8},{2,10},{4,12},{6,14},{8,0},{10,2},{12,4},{14,6},{1,9},{3,11}... | collective-permute-start | bytes 589832 | tf_op jit(solution)/shard_map/ppermute | solution.py:320
  8.3 1.6 %collective-permute-start.4 = (bf16[1,128,384]{2,1,0:T(8,128)(2,1)S(1)}, bf16[1,128,384]{2,1,0:T(8,128)(2,1)S(1)}, u32[]{:S(2)}, u32[]{:S(2)}) collective-permute-start(bf16[1,128,384]{2,1,0:T(8,128)(2,1)S(1)} %get-tuple-element.29._), channel_id=1, source_target_pairs={{0,12},{2,14},{4,8},{6,10},{8,4},{10,6},{12,0},{14,2},{1,13},{3,15... | collective-permute-start | bytes 294920 | tf_op jit(solution)/shard_map/ppermute | solution.py:320
  9.9 3.6 %load_cholesky.3.refs_2_.chol_ref.refs_3_ = bf16[64,128,512]{2,1,0:T(8,128)(2,1)S(1)} custom-call(bf16[64,128,1024]{2,1,0:T(8,128)(2,1)} %chol_ref.5, bf16[1,128,384]{2,1,0:T(8,128)(2,1)S(1)} %get-tuple-element.29._), custom_call_target="tpu_custom_call" | custom-call | tf_op jit(solution)/shard_map/load_cholesky/pallas_call | solution.py:128
  15.6 1.6 %collective-permute-start.7 = (bf16[3,128,384]{2,1,0:T(8,128)(2,1)S(1)}, bf16[3,128,384]{2,1,0:T(8,128)(2,1)S(1)}, u32[]{:S(2)}, u32[]{:S(2)}) collective-permute-start(bf16[3,128,384]{2,1,0:T(8,128)(2,1)S(1)} %join.3), channel_id=1, source_target_pairs={{0,2},{2,0},{4,6},{6,4},{8,10},{10,8},{12,14},{14,12},{1,3},{3,1},... | collective-permute-start | bytes 884744 | tf_op jit(solution)/shard_map/ppermute | solution.py:320
  17.2 2.0 %green_rows.5 = (bf16[1,128,384]{2,1,0:T(8,128)(2,1)S(1)}, bf16[2,128,384]{2,1,0:T(8,128)(2,1)S(1)}, bf16[2,128,384]{2,1,0:T(8,128)(2,1)S(1)}, bf16[2,128,384]{2,1,0:T(8,128)(2,1)S(1)}, bf16[4,128,384]{2,1,0:T(8,128)(2,1)S(1)}) custom-call(bf16[2,1024,384]{2,1,0:T(8,128)(2,1)} %refs_10_.1, bf16[2,384,384]{2,1,0:T(8,128)(2,1)} %inverse_ref.5, ...), custom_call_target="tpu_custom_call" | custom-call | tf_op jit(solution)/shard_map/green_rows/pallas_call | solution.py:95
  23.9 2.0 %bias_rows.2._.a_ref = f32[16,64]{1,0:T(8,128)S(1)} custom-call(bf16[64,128,512]{2,1,0:T(8,128)(2,1)S(1)} %load_cholesky.3.refs_2_.chol_ref.refs_3_, f32[1,64]{1,0:T(1,128)S(1)} %get-tuple-element.54.noise_ref, bf16[1,128,384]{2,1,0:T(8,128)(2,1)S(1)} %collective-permute-done.4.refs_0_, bf16[1,128,384]{2,1,0:T(8,128)(2,1)S(1)} %collective-permute-done.5.refs_1_, ...), custom_call_target="tpu_custom_call" | custom-call | tf_op jit(solution)/shard_map/bias_rows/pallas_call | solution.py:189
  27.4 2.3 %load_cholesky.4._.refs_4_ = bf16[64,128,256]{2,1,0:T(8,128)(2,1)S(1)} custom-call(bf16[64,128,1024]{2,1,0:T(8,128)(2,1)} %chol_ref.5, f32[16,64]{1,0:T(8,128)S(1)} %bias_rows.2._.a_ref), custom_call_target="tpu_custom_call" | custom-call | tf_op jit(solution)/shard_map/load_cholesky/pallas_call | solution.py:128
  31.2 2.3 %load_cholesky.5._.refs_5_ = bf16[64,128,256]{2,1,0:T(8,128)(2,1)S(1)} custom-call(bf16[64,128,1024]{2,1,0:T(8,128)(2,1)} %chol_ref.5, f32[16,64]{1,0:T(8,128)S(1)} %plus.4._.a_ref), custom_call_target="tpu_custom_call" | custom-call | tf_op jit(solution)/shard_map/load_cholesky/pallas_call | solution.py:128
  35.5 7.3 %collective-permute-done.10.refs_1_ = f32[16,64]{1,0:T(8,128)S(1)} collective-permute-done((f32[16,64]{1,0:T(8,128)S(1)}, f32[16,64]{1,0:T(8,128)S(1)}, u32[]{:S(2)}, u32[]{:S(2)}) %collective-permute-start.10) | collective-permute-done | bytes 4128 | tf_op jit(solution)/shard_map/ppermute | solution.py:436
  42.8 3.0 %potential_rows.2 = (bf16[1,128,1024]{2,1,0:T(8,128)(2,1)S(1)}, bf16[2,128,1024]{2,1,0:T(8,128)(2,1)S(1)}, bf16[2,128,1024]{2,1,0:T(8,128)(2,1)S(1)}, bf16[2,128...) custom-call(f32[16,64]{1,0:T(8,128)S(1)} %plus.5.refs_0_, ...), custom_call_target="tpu_custom_call" | custom-call | tf_op jit(solution)/shard_map/potential_rows/pallas_call | solution.py:241
  46.1 3.0 %collective-permute-start.25 = (bf16[2,128,1024]{2,1,0:T(8,128)(2,1)S(1)}, bf16[2,128,1024]{2,1,0:T(8,128)(2,1)S(1)}, u32[]{:S(2)}, u32[]{:S(2)}) collective-permute-start(bf16[2,128,1024]{2,1,0:T(8,128)(2,1)S(1)} %get-tuple-element.51), channel_id=1, source_target_pairs={{0,8},{2,10},{4,12},{6,14},{8,0},{10,2},{12,4},{14,6},{1,9},{3,11}... | collective-permute-start | bytes 1572872 | tf_op jit(solution)/shard_map/ppermute | solution.py:320
  50.5 2.2 %collective-permute-start.12 = (bf16[4,128,384]{2,1,0:T(8,128)(2,1)S(1)}, bf16[4,128,384]{2,1,0:T(8,128)(2,1)S(1)}, u32[]{:S(2)}, u32[]{:S(2)}) collective-permute-start(bf16[4,128,384]{2,1,0:T(8,128)(2,1)S(1)} %join.4), channel_id=1, source_target_pairs={{0,2},{2,0},{4,6},{6,4},{8,10},{10,8},{12,14},{14,12},{1,3},{3,1},... | collective-permute-start | bytes 1179656 | tf_op jit(solution)/shard_map/ppermute | solution.py:320
  52.7 5.8 %collective-permute-done.12.refs_4_ = bf16[4,128,384]{2,1,0:T(8,128)(2,1)S(1)} collective-permute-done((bf16[4,128,384]{2,1,0:T(8,128)(2,1)S(1)}, bf16[4,128,384]{2,1,0:T(8,128)(2,1)S(1)}, u32[]{:S(2)}, u32[]{:S(2)}) %collective-permute-start.12) | collective-permute-done | bytes 393248 | tf_op jit(solution)/shard_map/ppermute | solution.py:320
  58.5 2.0 %bias_rows.3.a_ref.refs_7_ = f32[16,64]{1,0:T(8,128)S(1)} custom-call(bf16[64,128,512]{2,1,0:T(8,128)(2,1)S(1)} %load_cholesky.3.refs_2_.chol_ref.refs_3_, f32[1,64]{1,0:T(1,128)S(1)} %get-tuple-element.55.noise_ref, bf16[1,128,384]{2,1,0:T(8,128)(2,1)S(1)} %get-tuple-element.31.refs_0_, bf16[2,128,384]{2,1,0:T(8,128)(2,1)S(1)} %collective-permute-done.1.refs_2_.refs_1_, ...), custom_call_target="tpu_custom_call" | custom-call | tf_op jit(solution)/shard_map/bias_rows/pallas_call | solution.py:189
  60.5 2.1 %collective-permute-start.13 = (f32[16,64]{1,0:T(8,128)S(1)}, f32[16,64]{1,0:T(8,128)S(1)}, u32[]{:S(2)}, u32[]{:S(2)}) collective-permute-start(f32[16,64]{1,0:T(8,128)S(1)} %bias_rows.3.a_ref.refs_7_), channel_id=1, source_target_pairs={{0,2},{2,0},{4,6},{6,4},{8,10},{10,8},{12,14},{14,12},{1,3},{3,1},... | collective-permute-start | bytes 12296 | tf_op jit(solution)/shard_map/ppermute | solution.py:320
  62.6 1.6 %collective-permute-done.13.b_ref = f32[16,64]{1,0:T(8,128)S(1)} collective-permute-done((f32[16,64]{1,0:T(8,128)S(1)}, f32[16,64]{1,0:T(8,128)S(1)}, u32[]{:S(2)}, u32[]{:S(2)}) %collective-permute-start.13) | collective-permute-done | bytes 4128 | tf_op jit(solution)/shard_map/ppermute | solution.py:320
  65.7 12.9 %collective-permute-done.14.b_ref = f32[16,64]{1,0:T(8,128)S(1)} collective-permute-done((f32[16,64]{1,0:T(8,128)S(1)}, f32[16,64]{1,0:T(8,128)S(1)}, u32[]{:S(2)}, u32[]{:S(2)}) %collective-permute-start.14) | collective-permute-done | bytes 4128 | tf_op jit(solution)/shard_map/ppermute | solution.py:320
  80.7 1.8 %bring_walker.3.refs_4_.refs_5_ = bf16[1024,384]{1,0:T(8,128)(2,1)S(1)} custom-call(bf16[2,1024,384]{2,1,0:T(8,128)(2,1)} %refs_10_.1, f32[1]{0:T(128)} %get-tuple-element.38.refs_3_.refs_6_._), custom_call_target="tpu_custom_call" | custom-call | tf_op jit(solution)/shard_map/bring_walker/pallas_call | solution.py:147
  82.5 3.3 %collective-permute-done.15.refs_1_ = f32[16,64]{1,0:T(8,128)S(1)} collective-permute-done((f32[16,64]{1,0:T(8,128)S(1)}, f32[16,64]{1,0:T(8,128)S(1)}, u32[]{:S(2)}, u32[]{:S(2)}) %collective-permute-start.15) | collective-permute-done | bytes 4128 | tf_op jit(solution)/shard_map/ppermute | solution.py:436
  85.8 3.7 %potential_rows.3 = (bf16[1,128,1024]{2,1,0:T(8,128)(2,1)S(1)}, bf16[1,128,1024]{2,1,0:T(8,128)(2,1)S(1)}, bf16[1,128,1024]{2,1,0:T(8,128)(2,1)S(1)}, bf16[1,128...) custom-call(f32[16,64]{1,0:T(8,128)S(1)} %plus.7.refs_0_, ...), custom_call_target="tpu_custom_call" | custom-call | tf_op jit(solution)/shard_map/potential_rows/pallas_call | solution.py:241
  92.3 1.6 %collective-permute-start.17 = (bf16[1,128,1024]{2,1,0:T(8,128)(2,1)S(1)}, bf16[1,128,1024]{2,1,0:T(8,128)(2,1)S(1)}, u32[]{:S(2)}, u32[]{:S(2)}) collective-permute-start(bf16[1,128,1024]{2,1,0:T(8,128)(2,1)S(1)} %get-tuple-element.40), channel_id=1, source_target_pairs={{0,4},{2,6},{4,0},{6,2},{8,12},{10,14},{12,8},{14,10},{1,5},{3,7},... | collective-permute-start | bytes 786440 | tf_op jit(solution)/shard_map/ppermute | solution.py:320
  95.0 2.1 %collective-permute-start.19 = (bf16[1,128,1024]{2,1,0:T(8,128)(2,1)S(1)}, bf16[1,128,1024]{2,1,0:T(8,128)(2,1)S(1)}, u32[]{:S(2)}, u32[]{:S(2)}) collective-permute-start(bf16[1,128,1024]{2,1,0:T(8,128)(2,1)S(1)} %get-tuple-element.42), channel_id=1, source_target_pairs={{0,8},{2,10},{4,12},{6,14},{8,0},{10,2},{12,4},{14,6},{1,9},{3,11}... | collective-permute-start | bytes 786440 | tf_op jit(solution)/shard_map/ppermute | solution.py:320
  98.2 5.6 %collective-permute-done.17.refs_0_ = bf16[1,128,1024]{2,1,0:T(8,128)(2,1)S(1)} collective-permute-done((bf16[1,128,1024]{2,1,0:T(8,128)(2,1)S(1)}, bf16[1,128,1024]{2,1,0:T(8,128)(2,1)S(1)}, u32[]{:S(2)}, u32[]{:S(2)}) %collective-permute-start.17) | collective-permute-done | bytes 262176 | tf_op jit(solution)/shard_map/ppermute | solution.py:320
  103.8 1.8 %collective-permute-start.21 = (bf16[1,128,1024]{2,1,0:T(8,128)(2,1)S(1)}, bf16[1,128,1024]{2,1,0:T(8,128)(2,1)S(1)}, u32[]{:S(2)}, u32[]{:S(2)}) collective-permute-start(bf16[1,128,1024]{2,1,0:T(8,128)(2,1)S(1)} %get-tuple-element.44), channel_id=1, source_target_pairs={{0,12},{2,14},{4,8},{6,10},{8,4},{10,6},{12,0},{14,2},{1,13},{3,15... | collective-permute-start | bytes 786440 | tf_op jit(solution)/shard_map/ppermute | solution.py:320
  105.6 2.3 %collective-permute-done.18.refs_1_ = bf16[1,128,1024]{2,1,0:T(8,128)(2,1)S(1)} collective-permute-done((bf16[1,128,1024]{2,1,0:T(8,128)(2,1)S(1)}, bf16[1,128,1024]{2,1,0:T(8,128)(2,1)S(1)}, u32[]{:S(2)}, u32[]{:S(2)}) %collective-permute-start.18) | collective-permute-done | bytes 262176 | tf_op jit(solution)/shard_map/ppermute | solution.py:320
  107.9 3.8 %collective-permute-start.22 = (bf16[1,128,1024]{2,1,0:T(8,128)(2,1)S(1)}, bf16[1,128,1024]{2,1,0:T(8,128)(2,1)S(1)}, u32[]{:S(2)}, u32[]{:S(2)}) collective-permute-start(bf16[1,128,1024]{2,1,0:T(8,128)(2,1)S(1)} %get-tuple-element.45), channel_id=1, source_target_pairs={{0,14},{2,12},{4,10},{6,8},{8,6},{10,4},{12,2},{14,0},{1,15},{3,13... | collective-permute-start | bytes 786440 | tf_op jit(solution)/shard_map/ppermute | solution.py:320
  111.7 14.6 %collective-permute-done.27.refs_4_ = bf16[4,128,1024]{2,1,0:T(8,128)(2,1)S(1)} collective-permute-done((bf16[4,128,1024]{2,1,0:T(8,128)(2,1)S(1)}, bf16[4,128,1024]{2,1,0:T(8,128)(2,1)S(1)}, u32[]{:S(2)}, u32[]{:S(2)}) %collective-permute-start.27) | collective-permute-done | bytes 1048608 | tf_op jit(solution)/shard_map/ppermute | solution.py:320
  126.4 5.6 %taylor.2.refs_9_ = bf16[2,1024,384]{2,1,0:T(8,128)(2,1)} custom-call(bf16[1,128,1024]{2,1,0:T(8,128)(2,1)S(1)} %get-tuple-element.49.refs_0_, bf16[2,128,1024]{2,1,0:T(8,128)(2,1)S(1)} %collective-permute-done.24.refs_2_.refs_1_, bf16[2,128,1024]{2,1,0:T(8,128)(2,1)S(1)} %collective-permute-done.25.refs_1_.refs_2_, ...), custom_call_target="tpu_custom_call" | custom-call | tf_op jit(solution)/shard_map/taylor/pallas_call | solution.py:297
  132.0 3.5 %collective-permute-done.21.refs_4_ = bf16[1,128,1024]{2,1,0:T(8,128)(2,1)S(1)} collective-permute-done((bf16[1,128,1024]{2,1,0:T(8,128)(2,1)S(1)}, bf16[1,128,1024]{2,1,0:T(8,128)(2,1)S(1)}, u32[]{:S(2)}, u32[]{:S(2)}) %collective-permute-start.21) | collective-permute-done | bytes 262176 | tf_op jit(solution)/shard_map/ppermute | solution.py:320
  135.4 3.2 %collective-permute-done.22.refs_5_ = bf16[1,128,1024]{2,1,0:T(8,128)(2,1)S(1)} collective-permute-done((bf16[1,128,1024]{2,1,0:T(8,128)(2,1)S(1)}, bf16[1,128,1024]{2,1,0:T(8,128)(2,1)S(1)}, u32[]{:S(2)}, u32[]{:S(2)}) %collective-permute-start.22) | collective-permute-done | bytes 262176 | tf_op jit(solution)/shard_map/ppermute | solution.py:320
  138.7 5.5 %taylor.3 = bf16[2,1024,384]{2,1,0:T(8,128)(2,1)} custom-call(bf16[1,128,1024]{2,1,0:T(8,128)(2,1)S(1)} %collective-permute-done.17.refs_0_, bf16[1,128,1024]{2,1,0:T(8,128)(2,1)S(1)} %collective-permute-done.18.refs_1_, bf16[1,128,1024]{2,1,0:T(8,128)(2,1)S(1)} %collective-permute-done.19.refs_2_, ...), custom_call_target="tpu_custom_call", output_to_operand_aliasing={{}: (9, {})} | custom-call | tf_op jit(solution)/shard_map/taylor/pallas_call | solution.py:297
  (53 shorter events, 25.4 us)
Async XLA Ops:
  2.2 11.9 %collective-permute-start = (bf16[2,128,384]{2,1,0:T(8,128)(2,1)S(1)}, bf16[2,128,384]{2,1,0:T(8,128)(2,1)S(1)}, u32[]{:S(2)}, u32[]{:S(2)}) collective-permute-start(bf16[2,128,384]{2,1,0:T(8,128)(2,1)S(1)} %get-tuple-element.30), channel_id=1, source_target_pairs={{0,8},{2,10},{4,12},{6,14},{8,0},{10,2},{12,4},{14,6},{1,9},{3,11}... | collective-permute-start | bytes 589832 | tf_op jit(solution)/shard_map/ppermute | solution.py:320
  4.9 10.5 %collective-permute-start.6 = (bf16[2,128,384]{2,1,0:T(8,128)(2,1)S(1)}, bf16[2,128,384]{2,1,0:T(8,128)(2,1)S(1)}, u32[]{:S(2)}, u32[]{:S(2)}) collective-permute-start(bf16[2,128,384]{2,1,0:T(8,128)(2,1)S(1)} %get-tuple-element.28._), channel_id=1, source_target_pairs={{0,4},{2,6},{4,0},{6,2},{8,12},{10,14},{12,8},{14,10},{1,5},{3,7},... | collective-permute-start | bytes 589832 | tf_op jit(solution)/shard_map/ppermute | solution.py:320
  6.9 14.9 %collective-permute-start.5 = (bf16[1,128,384]{2,1,0:T(8,128)(2,1)S(1)}, bf16[1,128,384]{2,1,0:T(8,128)(2,1)S(1)}, u32[]{:S(2)}, u32[]{:S(2)}) collective-permute-start(bf16[1,128,384]{2,1,0:T(8,128)(2,1)S(1)} %get-tuple-element.35), channel_id=1, source_target_pairs={{0,14},{2,12},{4,10},{6,8},{8,6},{10,4},{12,2},{14,0},{1,15},{3,13... | collective-permute-start | bytes 294920 | tf_op jit(solution)/shard_map/ppermute | solution.py:320
  8.3 14.7 %collective-permute-start.4 = (bf16[1,128,384]{2,1,0:T(8,128)(2,1)S(1)}, bf16[1,128,384]{2,1,0:T(8,128)(2,1)S(1)}, u32[]{:S(2)}, u32[]{:S(2)}) collective-permute-start(bf16[1,128,384]{2,1,0:T(8,128)(2,1)S(1)} %get-tuple-element.29._), channel_id=1, source_target_pairs={{0,12},{2,14},{4,8},{6,10},{8,4},{10,6},{12,0},{14,2},{1,13},{3,15... | collective-permute-start | bytes 294920 | tf_op jit(solution)/shard_map/ppermute | solution.py:320
  15.3 1.8 %copy-start.2 = (s32[2,64]{1,0:T(2,128)S(1)}, s32[2,64]{1,0:T(2,128)}, u32[]{:S(2)}) copy-start(s32[2,64]{1,0:T(2,128)} %param.6) | copy-start | bytes 1540
  15.6 8.3 %collective-permute-start.7 = (bf16[3,128,384]{2,1,0:T(8,128)(2,1)S(1)}, bf16[3,128,384]{2,1,0:T(8,128)(2,1)S(1)}, u32[]{:S(2)}, u32[]{:S(2)}) collective-permute-start(bf16[3,128,384]{2,1,0:T(8,128)(2,1)S(1)} %join.3), channel_id=1, source_target_pairs={{0,2},{2,0},{4,6},{6,4},{8,10},{10,8},{12,14},{14,12},{1,3},{3,1},... | collective-permute-start | bytes 884744 | tf_op jit(solution)/shard_map/ppermute | solution.py:320
  19.2 30.3 %collective-permute-start.1 = (bf16[2,128,384]{2,1,0:T(8,128)(2,1)S(1)}, bf16[2,128,384]{2,1,0:T(8,128)(2,1)S(1)}, u32[]{:S(2)}, u32[]{:S(2)}) collective-permute-start(bf16[2,128,384]{2,1,0:T(8,128)(2,1)S(1)} %get-tuple-element.32), channel_id=1, source_target_pairs={{0,4},{2,6},{4,0},{6,2},{8,12},{10,14},{12,8},{14,10},{1,5},{3,7},... | collective-permute-start | bytes 589832 | tf_op jit(solution)/shard_map/ppermute | solution.py:320
  20.6 14.9 %collective-permute-start.2 = (bf16[2,128,384]{2,1,0:T(8,128)(2,1)S(1)}, bf16[2,128,384]{2,1,0:T(8,128)(2,1)S(1)}, u32[]{:S(2)}, u32[]{:S(2)}) collective-permute-start(bf16[2,128,384]{2,1,0:T(8,128)(2,1)S(1)} %get-tuple-element.33), channel_id=1, source_target_pairs={{0,8},{2,10},{4,12},{6,14},{8,0},{10,2},{12,4},{14,6},{1,9},{3,11}... | collective-permute-start | bytes 589832 | tf_op jit(solution)/shard_map/ppermute | solution.py:320
  21.7 27.7 %collective-permute-start.3 = (bf16[2,128,384]{2,1,0:T(8,128)(2,1)S(1)}, bf16[2,128,384]{2,1,0:T(8,128)(2,1)S(1)}, u32[]{:S(2)}, u32[]{:S(2)}) collective-permute-start(bf16[2,128,384]{2,1,0:T(8,128)(2,1)S(1)} %get-tuple-element.34), channel_id=1, source_target_pairs={{0,12},{2,14},{4,8},{6,10},{8,4},{10,6},{12,0},{14,2},{1,13},{3,15... | collective-permute-start | bytes 589832 | tf_op jit(solution)/shard_map/ppermute | solution.py:320
  26.0 3.7 %collective-permute-start.8 = (f32[16,64]{1,0:T(8,128)S(1)}, f32[16,64]{1,0:T(8,128)S(1)}, u32[]{:S(2)}, u32[]{:S(2)}) collective-permute-start(f32[16,64]{1,0:T(8,128)S(1)} %bias_rows.2._.a_ref), channel_id=1, source_target_pairs={{0,2},{2,0},{4,6},{6,4},{8,10},{10,8},{12,14},{14,12},{1,3},{3,1},... | collective-permute-start | bytes 12296 | tf_op jit(solution)/shard_map/ppermute | solution.py:320
  29.7 3.8 %collective-permute-start.9 = (f32[16,64]{1,0:T(8,128)S(1)}, f32[16,64]{1,0:T(8,128)S(1)}, u32[]{:S(2)}, u32[]{:S(2)}) collective-permute-start(f32[16,64]{1,0:T(8,128)S(1)} %plus.4._.a_ref), channel_id=1, source_target_pairs={{0,4},{2,6},{4,0},{6,2},{8,12},{10,14},{12,8},{14,10},{1,5},{3,7},... | collective-permute-start | bytes 12296 | tf_op jit(solution)/shard_map/ppermute | solution.py:320
  33.6 2.0 %collective-permute-start.11 = (f32[16,64]{1,0:T(8,128)S(1)}, f32[16,64]{1,0:T(8,128)S(1)}, u32[]{:S(2)}, u32[]{:S(2)}) collective-permute-start(f32[16,64]{1,0:T(8,128)S(1)} %plus.5.refs_0_), channel_id=1, source_target_pairs={{0,12},{12,0},{1,13},{13,1},{2,14},{14,2},{3,15},{15,3},{16,28},{2... | collective-permute-start | bytes 12296 | tf_op jit(solution)/shard_map/ppermute | solution.py:436
  34.2 8.6 %collective-permute-start.10 = (f32[16,64]{1,0:T(8,128)S(1)}, f32[16,64]{1,0:T(8,128)S(1)}, u32[]{:S(2)}, u32[]{:S(2)}) collective-permute-start(f32[16,64]{1,0:T(8,128)S(1)} %plus.5.refs_0_), channel_id=1, source_target_pairs={{0,8},{12,4},{1,9},{13,5},{2,10},{14,6},{3,11},{15,7},{16,24},{28,... | collective-permute-start | bytes 12296 | tf_op jit(solution)/shard_map/ppermute | solution.py:436
  45.9 45.4 %collective-permute-start.24 = (bf16[2,128,1024]{2,1,0:T(8,128)(2,1)S(1)}, bf16[2,128,1024]{2,1,0:T(8,128)(2,1)S(1)}, u32[]{:S(2)}, u32[]{:S(2)}) collective-permute-start(bf16[2,128,1024]{2,1,0:T(8,128)(2,1)S(1)} %get-tuple-element.50), channel_id=1, source_target_pairs={{0,4},{2,6},{4,0},{6,2},{8,12},{10,14},{12,8},{14,10},{1,5},{3,7},... | collective-permute-start | bytes 1572872 | tf_op jit(solution)/shard_map/ppermute | solution.py:320
  46.1 45.2 %collective-permute-start.25 = (bf16[2,128,1024]{2,1,0:T(8,128)(2,1)S(1)}, bf16[2,128,1024]{2,1,0:T(8,128)(2,1)S(1)}, u32[]{:S(2)}, u32[]{:S(2)}) collective-permute-start(bf16[2,128,1024]{2,1,0:T(8,128)(2,1)S(1)} %get-tuple-element.51), channel_id=1, source_target_pairs={{0,8},{2,10},{4,12},{6,14},{8,0},{10,2},{12,4},{14,6},{1,9},{3,11}... | collective-permute-start | bytes 1572872 | tf_op jit(solution)/shard_map/ppermute | solution.py:320
  49.1 42.2 %collective-permute-start.26 = (bf16[2,128,1024]{2,1,0:T(8,128)(2,1)S(1)}, bf16[2,128,1024]{2,1,0:T(8,128)(2,1)S(1)}, u32[]{:S(2)}, u32[]{:S(2)}) collective-permute-start(bf16[2,128,1024]{2,1,0:T(8,128)(2,1)S(1)} %get-tuple-element.52), channel_id=1, source_target_pairs={{0,12},{2,14},{4,8},{6,10},{8,4},{10,6},{12,0},{14,2},{1,13},{3,15... | collective-permute-start | bytes 1572872 | tf_op jit(solution)/shard_map/ppermute | solution.py:320
  50.5 8.0 %collective-permute-start.12 = (bf16[4,128,384]{2,1,0:T(8,128)(2,1)S(1)}, bf16[4,128,384]{2,1,0:T(8,128)(2,1)S(1)}, u32[]{:S(2)}, u32[]{:S(2)}) collective-permute-start(bf16[4,128,384]{2,1,0:T(8,128)(2,1)S(1)} %join.4), channel_id=1, source_target_pairs={{0,2},{2,0},{4,6},{6,4},{8,10},{10,8},{12,14},{14,12},{1,3},{3,1},... | collective-permute-start | bytes 1179656 | tf_op jit(solution)/shard_map/ppermute | solution.py:320
  60.5 3.7 %collective-permute-start.13 = (f32[16,64]{1,0:T(8,128)S(1)}, f32[16,64]{1,0:T(8,128)S(1)}, u32[]{:S(2)}, u32[]{:S(2)}) collective-permute-start(f32[16,64]{1,0:T(8,128)S(1)} %bias_rows.3.a_ref.refs_7_), channel_id=1, source_target_pairs={{0,2},{2,0},{4,6},{6,4},{8,10},{10,8},{12,14},{14,12},{1,3},{3,1},... | collective-permute-start | bytes 12296 | tf_op jit(solution)/shard_map/ppermute | solution.py:320
  64.2 14.3 %collective-permute-start.14 = (f32[16,64]{1,0:T(8,128)S(1)}, f32[16,64]{1,0:T(8,128)S(1)}, u32[]{:S(2)}, u32[]{:S(2)}) collective-permute-start(f32[16,64]{1,0:T(8,128)S(1)} %plus.6.a_ref), channel_id=1, source_target_pairs={{0,4},{2,6},{4,0},{6,2},{8,12},{10,14},{12,8},{14,10},{1,5},{3,7},... | collective-permute-start | bytes 12296 | tf_op jit(solution)/shard_map/ppermute | solution.py:320
  78.6 3.9 %collective-permute-start.16 = (f32[16,64]{1,0:T(8,128)S(1)}, f32[16,64]{1,0:T(8,128)S(1)}, u32[]{:S(2)}, u32[]{:S(2)}) collective-permute-start(f32[16,64]{1,0:T(8,128)S(1)} %plus.7.refs_0_), channel_id=1, source_target_pairs={{0,12},{12,0},{1,13},{13,1},{2,14},{14,2},{3,15},{15,3},{16,28},{2... | collective-permute-start | bytes 12296 | tf_op jit(solution)/shard_map/ppermute | solution.py:436
  79.2 6.6 %collective-permute-start.15 = (f32[16,64]{1,0:T(8,128)S(1)}, f32[16,64]{1,0:T(8,128)S(1)}, u32[]{:S(2)}, u32[]{:S(2)}) collective-permute-start(f32[16,64]{1,0:T(8,128)S(1)} %plus.7.refs_0_), channel_id=1, source_target_pairs={{0,8},{12,4},{1,9},{13,5},{2,10},{14,6},{3,11},{15,7},{16,24},{28,... | collective-permute-start | bytes 12296 | tf_op jit(solution)/shard_map/ppermute | solution.py:436
  89.5 0.7 copy-start.1
  91.4 34.9 %collective-permute-start.27 = (bf16[4,128,1024]{2,1,0:T(8,128)(2,1)S(1)}, bf16[4,128,1024]{2,1,0:T(8,128)(2,1)S(1)}, u32[]{:S(2)}, u32[]{:S(2)}) collective-permute-start(bf16[4,128,1024]{2,1,0:T(8,128)(2,1)S(1)} %join.5), channel_id=1, source_target_pairs={{0,2},{2,0},{4,6},{6,4},{8,10},{10,8},{12,14},{14,12},{1,3},{3,1},... | collective-permute-start | bytes 3145736 | tf_op jit(solution)/shard_map/ppermute | solution.py:320
  92.3 11.5 %collective-permute-start.17 = (bf16[1,128,1024]{2,1,0:T(8,128)(2,1)S(1)}, bf16[1,128,1024]{2,1,0:T(8,128)(2,1)S(1)}, u32[]{:S(2)}, u32[]{:S(2)}) collective-permute-start(bf16[1,128,1024]{2,1,0:T(8,128)(2,1)S(1)} %get-tuple-element.40), channel_id=1, source_target_pairs={{0,4},{2,6},{4,0},{6,2},{8,12},{10,14},{12,8},{14,10},{1,5},{3,7},... | collective-permute-start | bytes 786440 | tf_op jit(solution)/shard_map/ppermute | solution.py:320
  94.0 13.9 %collective-permute-start.18 = (bf16[1,128,1024]{2,1,0:T(8,128)(2,1)S(1)}, bf16[1,128,1024]{2,1,0:T(8,128)(2,1)S(1)}, u32[]{:S(2)}, u32[]{:S(2)}) collective-permute-start(bf16[1,128,1024]{2,1,0:T(8,128)(2,1)S(1)} %get-tuple-element.41), channel_id=1, source_target_pairs={{0,6},{2,4},{4,2},{6,0},{8,14},{10,12},{12,10},{14,8},{1,7},{3,5},... | collective-permute-start | bytes 786440 | tf_op jit(solution)/shard_map/ppermute | solution.py:320
  95.0 37.0 %collective-permute-start.19 = (bf16[1,128,1024]{2,1,0:T(8,128)(2,1)S(1)}, bf16[1,128,1024]{2,1,0:T(8,128)(2,1)S(1)}, u32[]{:S(2)}, u32[]{:S(2)}) collective-permute-start(bf16[1,128,1024]{2,1,0:T(8,128)(2,1)S(1)} %get-tuple-element.42), channel_id=1, source_target_pairs={{0,8},{2,10},{4,12},{6,14},{8,0},{10,2},{12,4},{14,6},{1,9},{3,11}... | collective-permute-start | bytes 786440 | tf_op jit(solution)/shard_map/ppermute | solution.py:320
  97.1 34.9 %collective-permute-start.20 = (bf16[1,128,1024]{2,1,0:T(8,128)(2,1)S(1)}, bf16[1,128,1024]{2,1,0:T(8,128)(2,1)S(1)}, u32[]{:S(2)}, u32[]{:S(2)}) collective-permute-start(bf16[1,128,1024]{2,1,0:T(8,128)(2,1)S(1)} %get-tuple-element.43), channel_id=1, source_target_pairs={{0,10},{2,8},{4,14},{6,12},{8,2},{10,0},{12,6},{14,4},{1,11},{3,9}... | collective-permute-start | bytes 786440 | tf_op jit(solution)/shard_map/ppermute | solution.py:320
  103.8 31.6 %collective-permute-start.21 = (bf16[1,128,1024]{2,1,0:T(8,128)(2,1)S(1)}, bf16[1,128,1024]{2,1,0:T(8,128)(2,1)S(1)}, u32[]{:S(2)}, u32[]{:S(2)}) collective-permute-start(bf16[1,128,1024]{2,1,0:T(8,128)(2,1)S(1)} %get-tuple-element.44), channel_id=1, source_target_pairs={{0,12},{2,14},{4,8},{6,10},{8,4},{10,6},{12,0},{14,2},{1,13},{3,15... | collective-permute-start | bytes 786440 | tf_op jit(solution)/shard_map/ppermute | solution.py:320
  107.9 30.8 %collective-permute-start.22 = (bf16[1,128,1024]{2,1,0:T(8,128)(2,1)S(1)}, bf16[1,128,1024]{2,1,0:T(8,128)(2,1)S(1)}, u32[]{:S(2)}, u32[]{:S(2)}) collective-permute-start(bf16[1,128,1024]{2,1,0:T(8,128)(2,1)S(1)} %get-tuple-element.45), channel_id=1, source_target_pairs={{0,14},{2,12},{4,10},{6,8},{8,6},{10,4},{12,2},{14,0},{1,15},{3,13... | collective-permute-start | bytes 786440 | tf_op jit(solution)/shard_map/ppermute | solution.py:320
  126.3 12.3 %collective-permute-start.23 = (bf16[1,128,1024]{2,1,0:T(8,128)(2,1)S(1)}, bf16[1,128,1024]{2,1,0:T(8,128)(2,1)S(1)}, u32[]{:S(2)}, u32[]{:S(2)}) collective-permute-start(bf16[1,128,1024]{2,1,0:T(8,128)(2,1)S(1)} %get-tuple-element.47), channel_id=1, source_target_pairs={{0,2},{2,0},{4,6},{6,4},{8,10},{10,8},{12,14},{14,12},{1,3},{3,1},... | collective-permute-start | bytes 786440 | tf_op jit(solution)/shard_map/ppermute | solution.py:320
  126.4 12.3 %copy-start = (bf16[2,1024,384]{2,1,0:T(8,128)(2,1)S(1)}, bf16[2,1024,384]{2,1,0:T(8,128)(2,1)}, u32[]{:S(2)}) copy-start(bf16[2,1024,384]{2,1,0:T(8,128)(2,1)} %refs_10_.1) | copy-start | bytes 4718596

commit v6 on v5

--- a/solution.py
+++ b/solution.py
@@ -137,19 +137,21 @@
     )(in_hbm(cholesky), after)
 
 
-def bring_kernel(k, walkers_ref, _, held_ref, arrived):
-    copy = pltpu.make_async_copy(walkers_ref.at[k], held_ref, arrived)
+def bring_kernel(k, walkers_ref, _, held_ref, read, arrived):
+    copy = pltpu.make_async_copy(walkers_ref.at[k], read, arrived)
     copy.start()
     copy.wait()
+    held_ref[...] = read[...].T
 
 
 def bring(walkers, k, after):
+    _, orbitals, electrons = walkers.shape
     return pl.pallas_call(
         functools.partial(bring_kernel, k),
         in_specs=[IN_HBM, IN_ANY],
         out_specs=IN_VMEM,
-        out_shape=pltpu.VMEM(walkers.shape[1:], walkers.dtype),
-        scratch_shapes=[pltpu.SemaphoreType.DMA(())],
+        out_shape=pltpu.VMEM((electrons, orbitals), walkers.dtype),
+        scratch_shapes=[pltpu.VMEM((orbitals, electrons), walkers.dtype), pltpu.SemaphoreType.DMA(())],
         compiler_params=kernel_params(),
         cost_estimate=NO_COST,
         name="bring_walker",
@@ -267,24 +269,25 @@
     for place, (i, j) in enumerate(where):
         held[device_at(place, True)] = blocks[i][j]
     count, tile_rows, orbitals = held.shape
+
+    def product(degree, term, tiles):
+        rows = held[tiles].reshape(-1, orbitals)
+        return (-STEP_ROOT / degree) * lax.dot_general(
+            term, rows, (((1,), (1,)), ((), ())), preferred_element_type=jnp.float32
+        )
+
     source = walker_ref
     for degree in range(1, DEGREES):
-        product = (-STEP_ROOT / degree) * jnp.dot(
-            held[...].reshape(orbitals, orbitals), source[...], preferred_element_type=jnp.float32
-        )
+        grown = product(degree, source[...], slice(None))
         source = terms.at[degree % 2]
-        source[...] = product.astype(jnp.bfloat16)
-        running[...] = product + (walker_ref[...].astype(jnp.float32) if degree == 1 else running[...])
+        source[...] = grown.astype(jnp.bfloat16)
+        running[...] = grown + (walker_ref[...].astype(jnp.float32) if degree == 1 else running[...])
     step = max(count // 4, 1)
     writes = []
     for i in range(count // step):
         rows = pl.ds(i * step * tile_rows, step * tile_rows)
-        product = (-STEP_ROOT / DEGREES) * jnp.dot(
-            held[i * step : (i + 1) * step].reshape(step * tile_rows, orbitals),
-            source[...],
-            preferred_element_type=jnp.float32,
-        )
-        result[rows, :] = (running[rows, :] + product).astype(jnp.bfloat16)
+        grown = running[:, rows] + product(DEGREES, source[...], slice(i * step, (i + 1) * step))
+        result[rows, :] = grown.T.astype(jnp.bfloat16)
         writes.append(pltpu.make_async_copy(result.at[rows], out_ref.at[k, rows], written.at[i]))
         writes[-1].start()
     for write in writes:
@@ -292,7 +295,7 @@
 
 
 def taylor(blocks, where, walker, k, new, after):
-    orbitals, electrons = walker.shape
+    electrons, orbitals = walker.shape
     count, tile_rows = len(where), blocks[0].shape[1]
     return pl.pallas_call(
         functools.partial(taylor_kernel, k, where),
@@ -301,8 +304,8 @@
         out_shape=jax.ShapeDtypeStruct(new.shape, jnp.bfloat16),
         scratch_shapes=[
             pltpu.VMEM((count, tile_rows, orbitals), jnp.bfloat16),
-            pltpu.VMEM((2, orbitals, electrons), jnp.bfloat16),
-            pltpu.VMEM((orbitals, electrons), jnp.float32),
+            pltpu.VMEM((2, electrons, orbitals), jnp.bfloat16),
+            pltpu.VMEM((electrons, orbitals), jnp.float32),
             pltpu.VMEM((orbitals, electrons), jnp.bfloat16),
             pltpu.SemaphoreType.DMA((count,)),
         ],
@@ -320,20 +323,20 @@
     return lax.ppermute(block, PLANE, [(i, i ^ place) for i in range(planes)])
 
 
-def plus_kernel(a_ref, b_ref, _, out_ref):
-    out_ref[...] = a_ref[...] + b_ref[...]
+def plus_kernel(a_ref, b_ref, *refs):
+    refs[-1][...] = a_ref[...] + b_ref[...]
 
 
 def plus(a, b, after):
     return pl.pallas_call(
         plus_kernel,
-        in_specs=[IN_VMEM, IN_VMEM, IN_ANY],
+        in_specs=[IN_VMEM, IN_VMEM] + [IN_ANY] * len(after),
         out_specs=IN_VMEM,
         out_shape=jax.ShapeDtypeStruct(a.shape, a.dtype),
         compiler_params=kernel_params(),
         cost_estimate=NO_COST,
         name="plus",
-    )(a, b, after)
+    )(a, b, *after)
 
 
 def join_kernel(moves, sources, *refs):
@@ -423,12 +426,14 @@
     )
     token = passing[-1]
 
-    def reduced(sums):
+    def reduced(sums, wanted):
         distance = 1
         while distance < half:
             if rest:
                 held.append(load(cholesky, *rest.pop(0), sums))
-            sums = plus(sums, swap(sums, distance), held[-1])
+            if 2 * distance == half:
+                brought.update({i: bring(walkers, i, sums) for i in wanted})
+            sums = plus(sums, swap(sums, distance), [held[-1], *brought.values()])
             distance *= 2
         sums = [sums]
         for j in range(half_wa):
@@ -436,7 +441,7 @@
             sums.append(lax.ppermute(sums[0], "wa", pairs))
         return sums
 
-    new, log_steps = walkers, None
+    new, log_steps, brought = walkers, None, {}
     waiting = None
     for k in range(walker_count):
         last = k == walker_count - 1
@@ -445,20 +450,19 @@
             token = later[0]
             coming = stage_along_wa(later, along_wa, along_col)
         sums = bias_rows(held[0], noise[k : k + 1], *greens)
-        parts = reduced(sums)
+        wanted = [i for i in (k - 1, k) if 0 <= i and (i < k or last)]
+        parts = reduced(sums, wanted)
         if waiting is not None:
             first = stage_along_wa(waiting, along_wa, along_col)
         groups = direct if last else staged
         after = sums if last else coming[half_wa - 1]
         blocks, log_steps = potential_rows(parts, held, groups, True, log_steps, after)
-        walker = bring(walkers, k, log_steps)
         got = {p: swap(blocks[p], p) for p in (*near[along_col:], *far, *near[:along_col])} if last else {}
         if waiting is not None:
-            passed = [walker, before, log_steps]
-            new = taylor(*stage_along_col(waiting, first, along_wa, along_col, passed), before, k - 1, new, walkers)
-        before = walker
+            passed = [log_steps]
+            new = taylor(*stage_along_col(waiting, first, along_wa, along_col, passed), brought.pop(k - 1), k - 1, new, walkers)
         if last:
-            new = taylor(*ordered(got), walker, k, new, walkers)
+            new = taylor(*ordered(got), brought[k], k, new, walkers)
         else:
             waiting = blocks
             greens = (*stage_along_col(later, coming, along_wa, along_col, [log_steps]), True)

time: 145 us -> 145 us (level)
  Pallas kernels: 39.5 us -> 37.6 us
    pallas_call x2, Pallas kernels: 11.1 us -> 9.29 us  [taylor(): pl.pallas_call(functools.partial(taylor_kernel, k, where), in_specs=[IN_V...]
    ppermute x4, waiting for transfers between devices: 10.6 us -> 12.4 us  [reduced(): sums.append(lax.ppermute(sums[0], 'wa', pairs))]
  transfers between devices with their start and end apart: 28 -> 28, of which waited for: 13 -> 14; matrix products, arithmetic and copies ran while one was open for 0% -> 0% of each run, Pallas kernels for 22% -> 22%
where the time goes in v6:
time: 145 us; the launch traced here: 144 us
  waiting for transfers between devices  63.7 us (44%)
  starting transfers between devices  41.2 us (28%)
  Pallas kernels  37.6 us (26%)
    ppermute x24, waiting for transfers between devices, swap(): return lax.ppermute(block, PLANE, [(i, i ^ place) for i in range(planes)])  51.3 us
    ppermute x24, starting transfers between devices, swap(): return lax.ppermute(block, PLANE, [(i, i ^ place) for i in range(planes)])  37.1 us
    ppermute x4, waiting for transfers between devices, reduced(): sums.append(lax.ppermute(sums[0], 'wa', pairs))  12.4 us
    pallas_call x2, Pallas kernels, taylor(): pl.pallas_call(functools.partial(taylor_kernel, k, where), in_specs=[IN_V...  9.29 us
    pallas_call x3, Pallas kernels, load(): pl.pallas_call(functools.partial(load_kernel, start), in_specs=[IN_HBM, I...  8.21 us
    pallas_call x2, Pallas kernels, potential_rows(): pl.pallas_call(functools.partial(potential_kernel, groups, relative, len(...  6.69 us
    pallas_call x3, Pallas kernels, green_rows(): pl.pallas_call(functools.partial(green_kernel, k, groups, relative), in_s...  5.08 us
    ppermute x4, starting transfers between devices, reduced(): sums.append(lax.ppermute(sums[0], 'wa', pairs))  4.08 us
  transfers between devices with their start and end apart: 28, of which 14 were waited for; matrix products, arithmetic and copies ran while one was open for 0% of the time, Pallas kernels for 22%

profile of v6, /device:TPU:8, one launch (start us, length us, event | category | flops | bytes accessed | tf_op | source)
XLA Modules:
  0.0 144.1 jit_solution(6667091085313114572)
XLA Ops:
  0.6 1.6 %green_rows.3 = (bf16[2,128,384]{2,1,0:T(8,128)(2,1)S(1)}, bf16[2,128,384]{2,1,0:T(8,128)(2,1)S(1)}) custom-call(bf16[2,1024,384]{2,1,0:T(8,128)(2,1)} %refs_10_.1, bf16[2,384,384]{2,1,0:T(8,128)(2,1)} %inverse_ref.5, bf16[2,1024,384]{2,1,0:T(8,128)(2,1)} %refs_10_.1), custom_call_target="tpu_custom_call" | custom-call | tf_op jit(solution)/shard_map/green_rows/pallas_call | solution.py:95
  2.2 2.7 %collective-permute-start = (bf16[2,128,384]{2,1,0:T(8,128)(2,1)S(1)}, bf16[2,128,384]{2,1,0:T(8,128)(2,1)S(1)}, u32[]{:S(2)}, u32[]{:S(2)}) collective-permute-start(bf16[2,128,384]{2,1,0:T(8,128)(2,1)S(1)} %get-tuple-element.30), channel_id=1, source_target_pairs={{0,8},{2,10},{4,12},{6,14},{8,0},{10,2},{12,4},{14,6},{1,9},{3,11}... | collective-permute-start | bytes 589832 | tf_op jit(solution)/shard_map/ppermute | solution.py:323
  8.3 1.6 %collective-permute-start.4 = (bf16[1,128,384]{2,1,0:T(8,128)(2,1)S(1)}, bf16[1,128,384]{2,1,0:T(8,128)(2,1)S(1)}, u32[]{:S(2)}, u32[]{:S(2)}) collective-permute-start(bf16[1,128,384]{2,1,0:T(8,128)(2,1)S(1)} %get-tuple-element.29._), channel_id=1, source_target_pairs={{0,12},{2,14},{4,8},{6,10},{8,4},{10,6},{12,0},{14,2},{1,13},{3,15... | collective-permute-start | bytes 294920 | tf_op jit(solution)/shard_map/ppermute | solution.py:323
  9.9 3.6 %load_cholesky.3.refs_2_.chol_ref.refs_3_ = bf16[64,128,512]{2,1,0:T(8,128)(2,1)S(1)} custom-call(bf16[64,128,1024]{2,1,0:T(8,128)(2,1)} %chol_ref.5, bf16[1,128,384]{2,1,0:T(8,128)(2,1)S(1)} %get-tuple-element.29._), custom_call_target="tpu_custom_call" | custom-call | tf_op jit(solution)/shard_map/load_cholesky/pallas_call | solution.py:128
  15.6 1.6 %collective-permute-start.7 = (bf16[3,128,384]{2,1,0:T(8,128)(2,1)S(1)}, bf16[3,128,384]{2,1,0:T(8,128)(2,1)S(1)}, u32[]{:S(2)}, u32[]{:S(2)}) collective-permute-start(bf16[3,128,384]{2,1,0:T(8,128)(2,1)S(1)} %join.3), channel_id=1, source_target_pairs={{0,2},{2,0},{4,6},{6,4},{8,10},{10,8},{12,14},{14,12},{1,3},{3,1},... | collective-permute-start | bytes 884744 | tf_op jit(solution)/shard_map/ppermute | solution.py:323
  17.2 2.0 %green_rows.5 = (bf16[1,128,384]{2,1,0:T(8,128)(2,1)S(1)}, bf16[2,128,384]{2,1,0:T(8,128)(2,1)S(1)}, bf16[2,128,384]{2,1,0:T(8,128)(2,1)S(1)}, bf16[2,128,384]{2,1,0:T(8,128)(2,1)S(1)}, bf16[4,128,384]{2,1,0:T(8,128)(2,1)S(1)}) custom-call(bf16[2,1024,384]{2,1,0:T(8,128)(2,1)} %refs_10_.1, bf16[2,384,384]{2,1,0:T(8,128)(2,1)} %inverse_ref.5, ...), custom_call_target="tpu_custom_call" | custom-call | tf_op jit(solution)/shard_map/green_rows/pallas_call | solution.py:95
  23.9 2.0 %bias_rows.2._.a_ref = f32[16,64]{1,0:T(8,128)S(1)} custom-call(bf16[64,128,512]{2,1,0:T(8,128)(2,1)S(1)} %load_cholesky.3.refs_2_.chol_ref.refs_3_, f32[1,64]{1,0:T(1,128)S(1)} %get-tuple-element.54.noise_ref, bf16[1,128,384]{2,1,0:T(8,128)(2,1)S(1)} %collective-permute-done.4.refs_0_, bf16[1,128,384]{2,1,0:T(8,128)(2,1)S(1)} %collective-permute-done.5.refs_1_, ...), custom_call_target="tpu_custom_call" | custom-call | tf_op jit(solution)/shard_map/bias_rows/pallas_call | solution.py:191
  27.4 2.3 %load_cholesky.4.refs_0_.refs_4_ = bf16[64,128,256]{2,1,0:T(8,128)(2,1)S(1)} custom-call(bf16[64,128,1024]{2,1,0:T(8,128)(2,1)} %chol_ref.5, f32[16,64]{1,0:T(8,128)S(1)} %bias_rows.2._.a_ref), custom_call_target="tpu_custom_call" | custom-call | tf_op jit(solution)/shard_map/load_cholesky/pallas_call | solution.py:128
  31.2 2.3 %load_cholesky.5.refs_0_.refs_5_ = bf16[64,128,256]{2,1,0:T(8,128)(2,1)S(1)} custom-call(bf16[64,128,1024]{2,1,0:T(8,128)(2,1)} %chol_ref.5, f32[16,64]{1,0:T(8,128)S(1)} %plus.4._.a_ref), custom_call_target="tpu_custom_call" | custom-call | tf_op jit(solution)/shard_map/load_cholesky/pallas_call | solution.py:128
  35.5 7.3 %collective-permute-done.10.refs_1_ = f32[16,64]{1,0:T(8,128)S(1)} collective-permute-done((f32[16,64]{1,0:T(8,128)S(1)}, f32[16,64]{1,0:T(8,128)S(1)}, u32[]{:S(2)}, u32[]{:S(2)}) %collective-permute-start.10) | collective-permute-done | bytes 4128 | tf_op jit(solution)/shard_map/ppermute | solution.py:441
  42.8 3.0 %potential_rows.2 = (bf16[1,128,1024]{2,1,0:T(8,128)(2,1)S(1)}, bf16[2,128,1024]{2,1,0:T(8,128)(2,1)S(1)}, bf16[2,128,1024]{2,1,0:T(8,128)(2,1)S(1)}, bf16[2,128...) custom-call(f32[16,64]{1,0:T(8,128)S(1)} %plus.5.refs_0_, ...), custom_call_target="tpu_custom_call" | custom-call | tf_op jit(solution)/shard_map/potential_rows/pallas_call | solution.py:243
  46.1 3.0 %collective-permute-start.25 = (bf16[2,128,1024]{2,1,0:T(8,128)(2,1)S(1)}, bf16[2,128,1024]{2,1,0:T(8,128)(2,1)S(1)}, u32[]{:S(2)}, u32[]{:S(2)}) collective-permute-start(bf16[2,128,1024]{2,1,0:T(8,128)(2,1)S(1)} %get-tuple-element.50), channel_id=1, source_target_pairs={{0,8},{2,10},{4,12},{6,14},{8,0},{10,2},{12,4},{14,6},{1,9},{3,11}... | collective-permute-start | bytes 1572872 | tf_op jit(solution)/shard_map/ppermute | solution.py:323
  50.5 2.2 %collective-permute-start.12 = (bf16[4,128,384]{2,1,0:T(8,128)(2,1)S(1)}, bf16[4,128,384]{2,1,0:T(8,128)(2,1)S(1)}, u32[]{:S(2)}, u32[]{:S(2)}) collective-permute-start(bf16[4,128,384]{2,1,0:T(8,128)(2,1)S(1)} %join.4), channel_id=1, source_target_pairs={{0,2},{2,0},{4,6},{6,4},{8,10},{10,8},{12,14},{14,12},{1,3},{3,1},... | collective-permute-start | bytes 1179656 | tf_op jit(solution)/shard_map/ppermute | solution.py:323
  52.7 5.8 %collective-permute-done.12.refs_4_ = bf16[4,128,384]{2,1,0:T(8,128)(2,1)S(1)} collective-permute-done((bf16[4,128,384]{2,1,0:T(8,128)(2,1)S(1)}, bf16[4,128,384]{2,1,0:T(8,128)(2,1)S(1)}, u32[]{:S(2)}, u32[]{:S(2)}) %collective-permute-start.12) | collective-permute-done | bytes 393248 | tf_op jit(solution)/shard_map/ppermute | solution.py:323
  58.5 2.0 %bias_rows.3.a_ref.refs_7_ = f32[16,64]{1,0:T(8,128)S(1)} custom-call(bf16[64,128,512]{2,1,0:T(8,128)(2,1)S(1)} %load_cholesky.3.refs_2_.chol_ref.refs_3_, f32[1,64]{1,0:T(1,128)S(1)} %get-tuple-element.55.noise_ref, bf16[1,128,384]{2,1,0:T(8,128)(2,1)S(1)} %get-tuple-element.31.refs_0_, bf16[2,128,384]{2,1,0:T(8,128)(2,1)S(1)} %collective-permute-done.1.refs_2_.refs_1_, ...), custom_call_target="tpu_custom_call" | custom-call | tf_op jit(solution)/shard_map/bias_rows/pallas_call | solution.py:191
  60.5 2.1 %collective-permute-start.13 = (f32[16,64]{1,0:T(8,128)S(1)}, f32[16,64]{1,0:T(8,128)S(1)}, u32[]{:S(2)}, u32[]{:S(2)}) collective-permute-start(f32[16,64]{1,0:T(8,128)S(1)} %bias_rows.3.a_ref.refs_7_), channel_id=1, source_target_pairs={{0,2},{2,0},{4,6},{6,4},{8,10},{10,8},{12,14},{14,12},{1,3},{3,1},... | collective-permute-start | bytes 12296 | tf_op jit(solution)/shard_map/ppermute | solution.py:323
  62.6 1.6 %collective-permute-done.13.b_ref = f32[16,64]{1,0:T(8,128)S(1)} collective-permute-done((f32[16,64]{1,0:T(8,128)S(1)}, f32[16,64]{1,0:T(8,128)S(1)}, u32[]{:S(2)}, u32[]{:S(2)}) %collective-permute-start.13) | collective-permute-done | bytes 4128 | tf_op jit(solution)/shard_map/ppermute | solution.py:323
  68.5 10.1 %collective-permute-done.14.b_ref = f32[16,64]{1,0:T(8,128)S(1)} collective-permute-done((f32[16,64]{1,0:T(8,128)S(1)}, f32[16,64]{1,0:T(8,128)S(1)}, u32[]{:S(2)}, u32[]{:S(2)}) %collective-permute-start.14) | collective-permute-done | bytes 4128 | tf_op jit(solution)/shard_map/ppermute | solution.py:323
  80.7 5.1 %collective-permute-done.15.refs_1_ = f32[16,64]{1,0:T(8,128)S(1)} collective-permute-done((f32[16,64]{1,0:T(8,128)S(1)}, f32[16,64]{1,0:T(8,128)S(1)}, u32[]{:S(2)}, u32[]{:S(2)}) %collective-permute-start.15) | collective-permute-done | bytes 4128 | tf_op jit(solution)/shard_map/ppermute | solution.py:441
  85.8 3.7 %potential_rows.3 = (bf16[1,128,1024]{2,1,0:T(8,128)(2,1)S(1)}, bf16[1,128,1024]{2,1,0:T(8,128)(2,1)S(1)}, bf16[1,128,1024]{2,1,0:T(8,128)(2,1)S(1)}, bf16[1,128...) custom-call(f32[16,64]{1,0:T(8,128)S(1)} %plus.7.refs_0_, ...), custom_call_target="tpu_custom_call" | custom-call | tf_op jit(solution)/shard_map/potential_rows/pallas_call | solution.py:243
  89.5 1.7 %collective-permute-done.26.refs_0_.refs_3_ = bf16[2,128,1024]{2,1,0:T(8,128)(2,1)S(1)} collective-permute-done((bf16[2,128,1024]{2,1,0:T(8,128)(2,1)S(1)}, bf16[2,128,1024]{2,1,0:T(8,128)(2,1)S(1)}, u32[]{:S(2)}, u32[]{:S(2)}) %collective-permute-start.26) | collective-permute-done | bytes 524320 | tf_op jit(solution)/shard_map/ppermute | solution.py:323
  93.0 2.5 %collective-permute-start.18 = (bf16[1,128,1024]{2,1,0:T(8,128)(2,1)S(1)}, bf16[1,128,1024]{2,1,0:T(8,128)(2,1)S(1)}, u32[]{:S(2)}, u32[]{:S(2)}) collective-permute-start(bf16[1,128,1024]{2,1,0:T(8,128)(2,1)S(1)} %get-tuple-element.41), channel_id=1, source_target_pairs={{0,6},{2,4},{4,2},{6,0},{8,14},{10,12},{12,10},{14,8},{1,7},{3,5},... | collective-permute-start | bytes 786440 | tf_op jit(solution)/shard_map/ppermute | solution.py:323
  95.5 1.9 %collective-permute-start.19 = (bf16[1,128,1024]{2,1,0:T(8,128)(2,1)S(1)}, bf16[1,128,1024]{2,1,0:T(8,128)(2,1)S(1)}, u32[]{:S(2)}, u32[]{:S(2)}) collective-permute-start(bf16[1,128,1024]{2,1,0:T(8,128)(2,1)S(1)} %get-tuple-element.42), channel_id=1, source_target_pairs={{0,8},{2,10},{4,12},{6,14},{8,0},{10,2},{12,4},{14,6},{1,9},{3,11}... | collective-permute-start | bytes 786440 | tf_op jit(solution)/shard_map/ppermute | solution.py:323
  98.9 4.9 %collective-permute-done.17.refs_0_ = bf16[1,128,1024]{2,1,0:T(8,128)(2,1)S(1)} collective-permute-done((bf16[1,128,1024]{2,1,0:T(8,128)(2,1)S(1)}, bf16[1,128,1024]{2,1,0:T(8,128)(2,1)S(1)}, u32[]{:S(2)}, u32[]{:S(2)}) %collective-permute-start.17) | collective-permute-done | bytes 262176 | tf_op jit(solution)/shard_map/ppermute | solution.py:323
  103.8 2.5 %collective-permute-start.21 = (bf16[1,128,1024]{2,1,0:T(8,128)(2,1)S(1)}, bf16[1,128,1024]{2,1,0:T(8,128)(2,1)S(1)}, u32[]{:S(2)}, u32[]{:S(2)}) collective-permute-start(bf16[1,128,1024]{2,1,0:T(8,128)(2,1)S(1)} %get-tuple-element.44), channel_id=1, source_target_pairs={{0,12},{2,14},{4,8},{6,10},{8,4},{10,6},{12,0},{14,2},{1,13},{3,15... | collective-permute-start | bytes 786440 | tf_op jit(solution)/shard_map/ppermute | solution.py:323
  106.3 2.2 %collective-permute-done.18.refs_1_ = bf16[1,128,1024]{2,1,0:T(8,128)(2,1)S(1)} collective-permute-done((bf16[1,128,1024]{2,1,0:T(8,128)(2,1)S(1)}, bf16[1,128,1024]{2,1,0:T(8,128)(2,1)S(1)}, u32[]{:S(2)}, u32[]{:S(2)}) %collective-permute-start.18) | collective-permute-done | bytes 262176 | tf_op jit(solution)/shard_map/ppermute | solution.py:323
  108.5 3.9 %collective-permute-start.22 = (bf16[1,128,1024]{2,1,0:T(8,128)(2,1)S(1)}, bf16[1,128,1024]{2,1,0:T(8,128)(2,1)S(1)}, u32[]{:S(2)}, u32[]{:S(2)}) collective-permute-start(bf16[1,128,1024]{2,1,0:T(8,128)(2,1)S(1)} %get-tuple-element.45), channel_id=1, source_target_pairs={{0,14},{2,12},{4,10},{6,8},{8,6},{10,4},{12,2},{14,0},{1,15},{3,13... | collective-permute-start | bytes 786440 | tf_op jit(solution)/shard_map/ppermute | solution.py:323
  112.4 14.6 %collective-permute-done.27.refs_4_ = bf16[4,128,1024]{2,1,0:T(8,128)(2,1)S(1)} collective-permute-done((bf16[4,128,1024]{2,1,0:T(8,128)(2,1)S(1)}, bf16[4,128,1024]{2,1,0:T(8,128)(2,1)S(1)}, u32[]{:S(2)}, u32[]{:S(2)}) %collective-permute-start.27) | collective-permute-done | bytes 1048608 | tf_op jit(solution)/shard_map/ppermute | solution.py:323
  127.1 4.6 %taylor.2.refs_9_ = bf16[2,1024,384]{2,1,0:T(8,128)(2,1)} custom-call(bf16[1,128,1024]{2,1,0:T(8,128)(2,1)S(1)} %get-tuple-element.48.refs_0_, bf16[2,128,1024]{2,1,0:T(8,128)(2,1)S(1)} %collective-permute-done.24.refs_2_.refs_1_, bf16[2,128,1024]{2,1,0:T(8,128)(2,1)S(1)} %collective-permute-done.25.refs_1_.refs_2_, ...), custom_call_target="tpu_custom_call" | custom-call | tf_op jit(solution)/shard_map/taylor/pallas_call | solution.py:300
  131.7 4.4 %collective-permute-done.21.refs_4_ = bf16[1,128,1024]{2,1,0:T(8,128)(2,1)S(1)} collective-permute-done((bf16[1,128,1024]{2,1,0:T(8,128)(2,1)S(1)}, bf16[1,128,1024]{2,1,0:T(8,128)(2,1)S(1)}, u32[]{:S(2)}, u32[]{:S(2)}) %collective-permute-start.21) | collective-permute-done | bytes 262176 | tf_op jit(solution)/shard_map/ppermute | solution.py:323
  136.1 3.2 %collective-permute-done.22.refs_5_ = bf16[1,128,1024]{2,1,0:T(8,128)(2,1)S(1)} collective-permute-done((bf16[1,128,1024]{2,1,0:T(8,128)(2,1)S(1)}, bf16[1,128,1024]{2,1,0:T(8,128)(2,1)S(1)}, u32[]{:S(2)}, u32[]{:S(2)}) %collective-permute-start.22) | collective-permute-done | bytes 262176 | tf_op jit(solution)/shard_map/ppermute | solution.py:323
  139.3 4.7 %taylor.3 = bf16[2,1024,384]{2,1,0:T(8,128)(2,1)} custom-call(bf16[1,128,1024]{2,1,0:T(8,128)(2,1)S(1)} %collective-permute-done.17.refs_0_, bf16[1,128,1024]{2,1,0:T(8,128)(2,1)S(1)} %collective-permute-done.18.refs_1_, bf16[1,128,1024]{2,1,0:T(8,128)(2,1)S(1)} %collective-permute-done.19.refs_2_, ...), custom_call_target="tpu_custom_call", output_to_operand_aliasing={{}: (9, {})} | custom-call | tf_op jit(solution)/shard_map/taylor/pallas_call | solution.py:300
  (53 shorter events, 26.6 us)
Async XLA Ops:
  2.2 11.9 %collective-permute-start = (bf16[2,128,384]{2,1,0:T(8,128)(2,1)S(1)}, bf16[2,128,384]{2,1,0:T(8,128)(2,1)S(1)}, u32[]{:S(2)}, u32[]{:S(2)}) collective-permute-start(bf16[2,128,384]{2,1,0:T(8,128)(2,1)S(1)} %get-tuple-element.30), channel_id=1, source_target_pairs={{0,8},{2,10},{4,12},{6,14},{8,0},{10,2},{12,4},{14,6},{1,9},{3,11}... | collective-permute-start | bytes 589832 | tf_op jit(solution)/shard_map/ppermute | solution.py:323
  4.9 10.5 %collective-permute-start.6 = (bf16[2,128,384]{2,1,0:T(8,128)(2,1)S(1)}, bf16[2,128,384]{2,1,0:T(8,128)(2,1)S(1)}, u32[]{:S(2)}, u32[]{:S(2)}) collective-permute-start(bf16[2,128,384]{2,1,0:T(8,128)(2,1)S(1)} %get-tuple-element.28._), channel_id=1, source_target_pairs={{0,4},{2,6},{4,0},{6,2},{8,12},{10,14},{12,8},{14,10},{1,5},{3,7},... | collective-permute-start | bytes 589832 | tf_op jit(solution)/shard_map/ppermute | solution.py:323
  6.9 14.9 %collective-permute-start.5 = (bf16[1,128,384]{2,1,0:T(8,128)(2,1)S(1)}, bf16[1,128,384]{2,1,0:T(8,128)(2,1)S(1)}, u32[]{:S(2)}, u32[]{:S(2)}) collective-permute-start(bf16[1,128,384]{2,1,0:T(8,128)(2,1)S(1)} %get-tuple-element.35), channel_id=1, source_target_pairs={{0,14},{2,12},{4,10},{6,8},{8,6},{10,4},{12,2},{14,0},{1,15},{3,13... | collective-permute-start | bytes 294920 | tf_op jit(solution)/shard_map/ppermute | solution.py:323
  8.3 14.7 %collective-permute-start.4 = (bf16[1,128,384]{2,1,0:T(8,128)(2,1)S(1)}, bf16[1,128,384]{2,1,0:T(8,128)(2,1)S(1)}, u32[]{:S(2)}, u32[]{:S(2)}) collective-permute-start(bf16[1,128,384]{2,1,0:T(8,128)(2,1)S(1)} %get-tuple-element.29._), channel_id=1, source_target_pairs={{0,12},{2,14},{4,8},{6,10},{8,4},{10,6},{12,0},{14,2},{1,13},{3,15... | collective-permute-start | bytes 294920 | tf_op jit(solution)/shard_map/ppermute | solution.py:323
  15.3 1.8 %copy-start.2 = (s32[2,64]{1,0:T(2,128)S(1)}, s32[2,64]{1,0:T(2,128)}, u32[]{:S(2)}) copy-start(s32[2,64]{1,0:T(2,128)} %param.6) | copy-start | bytes 1540
  15.6 8.3 %collective-permute-start.7 = (bf16[3,128,384]{2,1,0:T(8,128)(2,1)S(1)}, bf16[3,128,384]{2,1,0:T(8,128)(2,1)S(1)}, u32[]{:S(2)}, u32[]{:S(2)}) collective-permute-start(bf16[3,128,384]{2,1,0:T(8,128)(2,1)S(1)} %join.3), channel_id=1, source_target_pairs={{0,2},{2,0},{4,6},{6,4},{8,10},{10,8},{12,14},{14,12},{1,3},{3,1},... | collective-permute-start | bytes 884744 | tf_op jit(solution)/shard_map/ppermute | solution.py:323
  19.2 30.3 %collective-permute-start.1 = (bf16[2,128,384]{2,1,0:T(8,128)(2,1)S(1)}, bf16[2,128,384]{2,1,0:T(8,128)(2,1)S(1)}, u32[]{:S(2)}, u32[]{:S(2)}) collective-permute-start(bf16[2,128,384]{2,1,0:T(8,128)(2,1)S(1)} %get-tuple-element.32), channel_id=1, source_target_pairs={{0,4},{2,6},{4,0},{6,2},{8,12},{10,14},{12,8},{14,10},{1,5},{3,7},... | collective-permute-start | bytes 589832 | tf_op jit(solution)/shard_map/ppermute | solution.py:323
  20.6 14.9 %collective-permute-start.2 = (bf16[2,128,384]{2,1,0:T(8,128)(2,1)S(1)}, bf16[2,128,384]{2,1,0:T(8,128)(2,1)S(1)}, u32[]{:S(2)}, u32[]{:S(2)}) collective-permute-start(bf16[2,128,384]{2,1,0:T(8,128)(2,1)S(1)} %get-tuple-element.33), channel_id=1, source_target_pairs={{0,8},{2,10},{4,12},{6,14},{8,0},{10,2},{12,4},{14,6},{1,9},{3,11}... | collective-permute-start | bytes 589832 | tf_op jit(solution)/shard_map/ppermute | solution.py:323
  21.7 27.7 %collective-permute-start.3 = (bf16[2,128,384]{2,1,0:T(8,128)(2,1)S(1)}, bf16[2,128,384]{2,1,0:T(8,128)(2,1)S(1)}, u32[]{:S(2)}, u32[]{:S(2)}) collective-permute-start(bf16[2,128,384]{2,1,0:T(8,128)(2,1)S(1)} %get-tuple-element.34), channel_id=1, source_target_pairs={{0,12},{2,14},{4,8},{6,10},{8,4},{10,6},{12,0},{14,2},{1,13},{3,15... | collective-permute-start | bytes 589832 | tf_op jit(solution)/shard_map/ppermute | solution.py:323
  26.0 3.7 %collective-permute-start.8 = (f32[16,64]{1,0:T(8,128)S(1)}, f32[16,64]{1,0:T(8,128)S(1)}, u32[]{:S(2)}, u32[]{:S(2)}) collective-permute-start(f32[16,64]{1,0:T(8,128)S(1)} %bias_rows.2._.a_ref), channel_id=1, source_target_pairs={{0,2},{2,0},{4,6},{6,4},{8,10},{10,8},{12,14},{14,12},{1,3},{3,1},... | collective-permute-start | bytes 12296 | tf_op jit(solution)/shard_map/ppermute | solution.py:323
  29.7 3.8 %collective-permute-start.9 = (f32[16,64]{1,0:T(8,128)S(1)}, f32[16,64]{1,0:T(8,128)S(1)}, u32[]{:S(2)}, u32[]{:S(2)}) collective-permute-start(f32[16,64]{1,0:T(8,128)S(1)} %plus.4._.a_ref), channel_id=1, source_target_pairs={{0,4},{2,6},{4,0},{6,2},{8,12},{10,14},{12,8},{14,10},{1,5},{3,7},... | collective-permute-start | bytes 12296 | tf_op jit(solution)/shard_map/ppermute | solution.py:323
  33.6 2.0 %collective-permute-start.11 = (f32[16,64]{1,0:T(8,128)S(1)}, f32[16,64]{1,0:T(8,128)S(1)}, u32[]{:S(2)}, u32[]{:S(2)}) collective-permute-start(f32[16,64]{1,0:T(8,128)S(1)} %plus.5.refs_0_), channel_id=1, source_target_pairs={{0,12},{12,0},{1,13},{13,1},{2,14},{14,2},{3,15},{15,3},{16,28},{2... | collective-permute-start | bytes 12296 | tf_op jit(solution)/shard_map/ppermute | solution.py:441
  34.2 8.6 %collective-permute-start.10 = (f32[16,64]{1,0:T(8,128)S(1)}, f32[16,64]{1,0:T(8,128)S(1)}, u32[]{:S(2)}, u32[]{:S(2)}) collective-permute-start(f32[16,64]{1,0:T(8,128)S(1)} %plus.5.refs_0_), channel_id=1, source_target_pairs={{0,8},{12,4},{1,9},{13,5},{2,10},{14,6},{3,11},{15,7},{16,24},{28,... | collective-permute-start | bytes 12296 | tf_op jit(solution)/shard_map/ppermute | solution.py:441
  45.9 43.6 %collective-permute-start.24 = (bf16[2,128,1024]{2,1,0:T(8,128)(2,1)S(1)}, bf16[2,128,1024]{2,1,0:T(8,128)(2,1)S(1)}, u32[]{:S(2)}, u32[]{:S(2)}) collective-permute-start(bf16[2,128,1024]{2,1,0:T(8,128)(2,1)S(1)} %get-tuple-element.49), channel_id=1, source_target_pairs={{0,4},{2,6},{4,0},{6,2},{8,12},{10,14},{12,8},{14,10},{1,5},{3,7},... | collective-permute-start | bytes 1572872 | tf_op jit(solution)/shard_map/ppermute | solution.py:323
  46.1 43.4 %collective-permute-start.25 = (bf16[2,128,1024]{2,1,0:T(8,128)(2,1)S(1)}, bf16[2,128,1024]{2,1,0:T(8,128)(2,1)S(1)}, u32[]{:S(2)}, u32[]{:S(2)}) collective-permute-start(bf16[2,128,1024]{2,1,0:T(8,128)(2,1)S(1)} %get-tuple-element.50), channel_id=1, source_target_pairs={{0,8},{2,10},{4,12},{6,14},{8,0},{10,2},{12,4},{14,6},{1,9},{3,11}... | collective-permute-start | bytes 1572872 | tf_op jit(solution)/shard_map/ppermute | solution.py:323
  49.1 42.1 %collective-permute-start.26 = (bf16[2,128,1024]{2,1,0:T(8,128)(2,1)S(1)}, bf16[2,128,1024]{2,1,0:T(8,128)(2,1)S(1)}, u32[]{:S(2)}, u32[]{:S(2)}) collective-permute-start(bf16[2,128,1024]{2,1,0:T(8,128)(2,1)S(1)} %get-tuple-element.51), channel_id=1, source_target_pairs={{0,12},{2,14},{4,8},{6,10},{8,4},{10,6},{12,0},{14,2},{1,13},{3,15... | collective-permute-start | bytes 1572872 | tf_op jit(solution)/shard_map/ppermute | solution.py:323
  50.5 8.0 %collective-permute-start.12 = (bf16[4,128,384]{2,1,0:T(8,128)(2,1)S(1)}, bf16[4,128,384]{2,1,0:T(8,128)(2,1)S(1)}, u32[]{:S(2)}, u32[]{:S(2)}) collective-permute-start(bf16[4,128,384]{2,1,0:T(8,128)(2,1)S(1)} %join.4), channel_id=1, source_target_pairs={{0,2},{2,0},{4,6},{6,4},{8,10},{10,8},{12,14},{14,12},{1,3},{3,1},... | collective-permute-start | bytes 1179656 | tf_op jit(solution)/shard_map/ppermute | solution.py:323
  60.5 3.7 %collective-permute-start.13 = (f32[16,64]{1,0:T(8,128)S(1)}, f32[16,64]{1,0:T(8,128)S(1)}, u32[]{:S(2)}, u32[]{:S(2)}) collective-permute-start(f32[16,64]{1,0:T(8,128)S(1)} %bias_rows.3.a_ref.refs_7_), channel_id=1, source_target_pairs={{0,2},{2,0},{4,6},{6,4},{8,10},{10,8},{12,14},{14,12},{1,3},{3,1},... | collective-permute-start | bytes 12296 | tf_op jit(solution)/shard_map/ppermute | solution.py:323
  64.2 14.3 %collective-permute-start.14 = (f32[16,64]{1,0:T(8,128)S(1)}, f32[16,64]{1,0:T(8,128)S(1)}, u32[]{:S(2)}, u32[]{:S(2)}) collective-permute-start(f32[16,64]{1,0:T(8,128)S(1)} %plus.6._.a_ref), channel_id=1, source_target_pairs={{0,4},{2,6},{4,0},{6,2},{8,12},{10,14},{12,8},{14,10},{1,5},{3,7},... | collective-permute-start | bytes 12296 | tf_op jit(solution)/shard_map/ppermute | solution.py:323
  78.6 2.1 %collective-permute-start.16 = (f32[16,64]{1,0:T(8,128)S(1)}, f32[16,64]{1,0:T(8,128)S(1)}, u32[]{:S(2)}, u32[]{:S(2)}) collective-permute-start(f32[16,64]{1,0:T(8,128)S(1)} %plus.7.refs_0_), channel_id=1, source_target_pairs={{0,12},{12,0},{1,13},{13,1},{2,14},{14,2},{3,15},{15,3},{16,28},{2... | collective-permute-start | bytes 12296 | tf_op jit(solution)/shard_map/ppermute | solution.py:441
  79.2 6.6 %collective-permute-start.15 = (f32[16,64]{1,0:T(8,128)S(1)}, f32[16,64]{1,0:T(8,128)S(1)}, u32[]{:S(2)}, u32[]{:S(2)}) collective-permute-start(f32[16,64]{1,0:T(8,128)S(1)} %plus.7.refs_0_), channel_id=1, source_target_pairs={{0,8},{12,4},{1,9},{13,5},{2,10},{14,6},{3,11},{15,7},{16,24},{28,... | collective-permute-start | bytes 12296 | tf_op jit(solution)/shard_map/ppermute | solution.py:441
  91.2 0.7 copy-start.1
  92.0 35.0 %collective-permute-start.27 = (bf16[4,128,1024]{2,1,0:T(8,128)(2,1)S(1)}, bf16[4,128,1024]{2,1,0:T(8,128)(2,1)S(1)}, u32[]{:S(2)}, u32[]{:S(2)}) collective-permute-start(bf16[4,128,1024]{2,1,0:T(8,128)(2,1)S(1)} %join.5), channel_id=1, source_target_pairs={{0,2},{2,0},{4,6},{6,4},{8,10},{10,8},{12,14},{14,12},{1,3},{3,1},... | collective-permute-start | bytes 3145736 | tf_op jit(solution)/shard_map/ppermute | solution.py:323
  93.0 10.8 %collective-permute-start.17 = (bf16[1,128,1024]{2,1,0:T(8,128)(2,1)S(1)}, bf16[1,128,1024]{2,1,0:T(8,128)(2,1)S(1)}, u32[]{:S(2)}, u32[]{:S(2)}) collective-permute-start(bf16[1,128,1024]{2,1,0:T(8,128)(2,1)S(1)} %get-tuple-element.40), channel_id=1, source_target_pairs={{0,4},{2,6},{4,0},{6,2},{8,12},{10,14},{12,8},{14,10},{1,5},{3,7},... | collective-permute-start | bytes 786440 | tf_op jit(solution)/shard_map/ppermute | solution.py:323
  93.0 15.4 %collective-permute-start.18 = (bf16[1,128,1024]{2,1,0:T(8,128)(2,1)S(1)}, bf16[1,128,1024]{2,1,0:T(8,128)(2,1)S(1)}, u32[]{:S(2)}, u32[]{:S(2)}) collective-permute-start(bf16[1,128,1024]{2,1,0:T(8,128)(2,1)S(1)} %get-tuple-element.41), channel_id=1, source_target_pairs={{0,6},{2,4},{4,2},{6,0},{8,14},{10,12},{12,10},{14,8},{1,7},{3,5},... | collective-permute-start | bytes 786440 | tf_op jit(solution)/shard_map/ppermute | solution.py:323
  95.5 36.2 %collective-permute-start.19 = (bf16[1,128,1024]{2,1,0:T(8,128)(2,1)S(1)}, bf16[1,128,1024]{2,1,0:T(8,128)(2,1)S(1)}, u32[]{:S(2)}, u32[]{:S(2)}) collective-permute-start(bf16[1,128,1024]{2,1,0:T(8,128)(2,1)S(1)} %get-tuple-element.42), channel_id=1, source_target_pairs={{0,8},{2,10},{4,12},{6,14},{8,0},{10,2},{12,4},{14,6},{1,9},{3,11}... | collective-permute-start | bytes 786440 | tf_op jit(solution)/shard_map/ppermute | solution.py:323
  97.4 34.3 %collective-permute-start.20 = (bf16[1,128,1024]{2,1,0:T(8,128)(2,1)S(1)}, bf16[1,128,1024]{2,1,0:T(8,128)(2,1)S(1)}, u32[]{:S(2)}, u32[]{:S(2)}) collective-permute-start(bf16[1,128,1024]{2,1,0:T(8,128)(2,1)S(1)} %get-tuple-element.43), channel_id=1, source_target_pairs={{0,10},{2,8},{4,14},{6,12},{8,2},{10,0},{12,6},{14,4},{1,11},{3,9}... | collective-permute-start | bytes 786440 | tf_op jit(solution)/shard_map/ppermute | solution.py:323
  103.8 32.3 %collective-permute-start.21 = (bf16[1,128,1024]{2,1,0:T(8,128)(2,1)S(1)}, bf16[1,128,1024]{2,1,0:T(8,128)(2,1)S(1)}, u32[]{:S(2)}, u32[]{:S(2)}) collective-permute-start(bf16[1,128,1024]{2,1,0:T(8,128)(2,1)S(1)} %get-tuple-element.44), channel_id=1, source_target_pairs={{0,12},{2,14},{4,8},{6,10},{8,4},{10,6},{12,0},{14,2},{1,13},{3,15... | collective-permute-start | bytes 786440 | tf_op jit(solution)/shard_map/ppermute | solution.py:323
  108.5 30.8 %collective-permute-start.22 = (bf16[1,128,1024]{2,1,0:T(8,128)(2,1)S(1)}, bf16[1,128,1024]{2,1,0:T(8,128)(2,1)S(1)}, u32[]{:S(2)}, u32[]{:S(2)}) collective-permute-start(bf16[1,128,1024]{2,1,0:T(8,128)(2,1)S(1)} %get-tuple-element.45), channel_id=1, source_target_pairs={{0,14},{2,12},{4,10},{6,8},{8,6},{10,4},{12,2},{14,0},{1,15},{3,13... | collective-permute-start | bytes 786440 | tf_op jit(solution)/shard_map/ppermute | solution.py:323
  127.0 12.3 %collective-permute-start.23 = (bf16[1,128,1024]{2,1,0:T(8,128)(2,1)S(1)}, bf16[1,128,1024]{2,1,0:T(8,128)(2,1)S(1)}, u32[]{:S(2)}, u32[]{:S(2)}) collective-permute-start(bf16[1,128,1024]{2,1,0:T(8,128)(2,1)S(1)} %get-tuple-element.47), channel_id=1, source_target_pairs={{0,2},{2,0},{4,6},{6,4},{8,10},{10,8},{12,14},{14,12},{1,3},{3,1},... | collective-permute-start | bytes 786440 | tf_op jit(solution)/shard_map/ppermute | solution.py:323
  127.1 12.2 %copy-start = (bf16[2,1024,384]{2,1,0:T(8,128)(2,1)S(1)}, bf16[2,1024,384]{2,1,0:T(8,128)(2,1)}, u32[]{:S(2)}) copy-start(bf16[2,1024,384]{2,1,0:T(8,128)(2,1)} %refs_10_.1) | copy-start | bytes 4718596

commit v7 on v6

--- a/solution.py
+++ b/solution.py
@@ -403,7 +403,7 @@
         return green_rows(walkers, intersection_inverse, k, tile_rows, groups, True, after)
 
     def ordered(received):
-        places = (*near[along_col:], *far, *near[:along_col])
+        places = (*far[:1], *near[along_col:], *far[1:], *near[:along_col])
         return [received[p] for p in places], tuple((places.index(p), 0) for p in range(planes))
 
     short = along_wa - 1
@@ -457,9 +457,9 @@
         groups = direct if last else staged
         after = sums if last else coming[half_wa - 1]
         blocks, log_steps = potential_rows(parts, held, groups, True, log_steps, after)
-        got = {p: swap(blocks[p], p) for p in (*near[along_col:], *far, *near[:along_col])} if last else {}
+        got = {p: swap(blocks[p], p) for p in (*far[:1], *near[along_col:], *far[1:], *near[:along_col])} if last else {}
         if waiting is not None:
-            passed = [log_steps]
+            passed = [blocks[0]]
             new = taylor(*stage_along_col(waiting, first, along_wa, along_col, passed), brought.pop(k - 1), k - 1, new, walkers)
         if last:
             new = taylor(*ordered(got), brought[k], k, new, walkers)

time: 145 us -> 143 us (0.986)
  starting transfers between devices: 41.2 us -> 37.3 us
  waiting for transfers between devices: 63.7 us -> 66.9 us
    ppermute x24, starting transfers between devices: 37.1 us -> 33.2 us  [swap(): return lax.ppermute(block, PLANE, [(i, i ^ place) for i in range(planes)])]
    ppermute x24, waiting for transfers between devices: 51.3 us -> 54.5 us  [swap(): return lax.ppermute(block, PLANE, [(i, i ^ place) for i in range(planes)])]
  transfers between devices with their start and end apart: 28 -> 28, of which waited for: 14 -> 13; matrix products, arithmetic and copies ran while one was open for 0% -> 0% of each run, Pallas kernels for 22% -> 22%
where the time goes in v7:
time: 143 us
  waiting for transfers between devices  66.9 us (47%)
  Pallas kernels  37.6 us (26%)
  starting transfers between devices  37.3 us (26%)
    ppermute x24, waiting for transfers between devices, swap(): return lax.ppermute(block, PLANE, [(i, i ^ place) for i in range(planes)])  54.5 us
    ppermute x24, starting transfers between devices, swap(): return lax.ppermute(block, PLANE, [(i, i ^ place) for i in range(planes)])  33.2 us
    ppermute x4, waiting for transfers between devices, reduced(): sums.append(lax.ppermute(sums[0], 'wa', pairs))  12.4 us
    pallas_call x2, Pallas kernels, taylor(): pl.pallas_call(functools.partial(taylor_kernel, k, where), in_specs=[IN_V...  9.3 us
    pallas_call x3, Pallas kernels, load(): pl.pallas_call(functools.partial(load_kernel, start), in_specs=[IN_HBM, I...  8.21 us
    pallas_call x2, Pallas kernels, potential_rows(): pl.pallas_call(functools.partial(potential_kernel, groups, relative, len(...  6.68 us
    pallas_call x3, Pallas kernels, green_rows(): pl.pallas_call(functools.partial(green_kernel, k, groups, relative), in_s...  5.08 us
    ppermute x4, starting transfers between devices, reduced(): sums.append(lax.ppermute(sums[0], 'wa', pairs))  4.08 us
  transfers between devices with their start and end apart: 28, of which 13 were waited for; matrix products, arithmetic and copies ran while one was open for 0% of the time, Pallas kernels for 22%

profile of v7, /device:TPU:8, one launch (start us, length us, event | category | flops | bytes accessed | tf_op | source)
XLA Modules:
  0.0 142.8 jit_solution(1762493706844682402)
XLA Ops:
  0.6 1.6 %green_rows.3 = (bf16[2,128,384]{2,1,0:T(8,128)(2,1)S(1)}, bf16[2,128,384]{2,1,0:T(8,128)(2,1)S(1)}) custom-call(bf16[2,1024,384]{2,1,0:T(8,128)(2,1)} %refs_10_.1, bf16[2,384,384]{2,1,0:T(8,128)(2,1)} %inverse_ref.5, bf16[2,1024,384]{2,1,0:T(8,128)(2,1)} %refs_10_.1), custom_call_target="tpu_custom_call" | custom-call | tf_op jit(solution)/shard_map/green_rows/pallas_call | solution.py:95
  2.2 2.7 %collective-permute-start = (bf16[2,128,384]{2,1,0:T(8,128)(2,1)S(1)}, bf16[2,128,384]{2,1,0:T(8,128)(2,1)S(1)}, u32[]{:S(2)}, u32[]{:S(2)}) collective-permute-start(bf16[2,128,384]{2,1,0:T(8,128)(2,1)S(1)} %get-tuple-element.30), channel_id=1, source_target_pairs={{0,8},{2,10},{4,12},{6,14},{8,0},{10,2},{12,4},{14,6},{1,9},{3,11}... | collective-permute-start | bytes 589832 | tf_op jit(solution)/shard_map/ppermute | solution.py:323
  5.3 1.6 %green_rows.4 = (bf16[1,128,384]{2,1,0:T(8,128)(2,1)S(1)}, bf16[1,128,384]{2,1,0:T(8,128)(2,1)S(1)}, bf16[1,128,384]{2,1,0:T(8,128)(2,1)S(1)}, bf16[3,128,384]{2,1,0:T(8,128)(2,1)S(1)}) custom-call(bf16[2,1024,384]{2,1,0:T(8,128)(2,1)} %refs_10_.1, bf16[2,384,384]{2,1,0:T(8,128)(2,1)} %inverse_ref.5, bf16[2,128,384]{2,1,0:T(8,128)(2,1)S(1)} %get-tuple-element.28._), custom_call_target="tpu_custom_call" | custom-call | tf_op jit(solution)/shard_map/green_rows/pallas_call | solution.py:95
  8.3 1.6 %collective-permute-start.4 = (bf16[1,128,384]{2,1,0:T(8,128)(2,1)S(1)}, bf16[1,128,384]{2,1,0:T(8,128)(2,1)S(1)}, u32[]{:S(2)}, u32[]{:S(2)}) collective-permute-start(bf16[1,128,384]{2,1,0:T(8,128)(2,1)S(1)} %get-tuple-element.29._), channel_id=1, source_target_pairs={{0,12},{2,14},{4,8},{6,10},{8,4},{10,6},{12,0},{14,2},{1,13},{3,15... | collective-permute-start | bytes 294920 | tf_op jit(solution)/shard_map/ppermute | solution.py:323
  9.9 3.6 %load_cholesky.3.refs_2_.chol_ref.refs_3_ = bf16[64,128,512]{2,1,0:T(8,128)(2,1)S(1)} custom-call(bf16[64,128,1024]{2,1,0:T(8,128)(2,1)} %chol_ref.5, bf16[1,128,384]{2,1,0:T(8,128)(2,1)S(1)} %get-tuple-element.29._), custom_call_target="tpu_custom_call" | custom-call | tf_op jit(solution)/shard_map/load_cholesky/pallas_call | solution.py:128
  15.6 1.6 %collective-permute-start.7 = (bf16[3,128,384]{2,1,0:T(8,128)(2,1)S(1)}, bf16[3,128,384]{2,1,0:T(8,128)(2,1)S(1)}, u32[]{:S(2)}, u32[]{:S(2)}) collective-permute-start(bf16[3,128,384]{2,1,0:T(8,128)(2,1)S(1)} %join.3), channel_id=1, source_target_pairs={{0,2},{2,0},{4,6},{6,4},{8,10},{10,8},{12,14},{14,12},{1,3},{3,1},... | collective-permute-start | bytes 884744 | tf_op jit(solution)/shard_map/ppermute | solution.py:323
  17.2 2.0 %green_rows.5 = (bf16[1,128,384]{2,1,0:T(8,128)(2,1)S(1)}, bf16[2,128,384]{2,1,0:T(8,128)(2,1)S(1)}, bf16[2,128,384]{2,1,0:T(8,128)(2,1)S(1)}, bf16[2,128,384]{2,1,0:T(8,128)(2,1)S(1)}, bf16[4,128,384]{2,1,0:T(8,128)(2,1)S(1)}) custom-call(bf16[2,1024,384]{2,1,0:T(8,128)(2,1)} %refs_10_.1, bf16[2,384,384]{2,1,0:T(8,128)(2,1)} %inverse_ref.5, ...), custom_call_target="tpu_custom_call" | custom-call | tf_op jit(solution)/shard_map/green_rows/pallas_call | solution.py:95
  19.2 1.5 %collective-permute-start.1 = (bf16[2,128,384]{2,1,0:T(8,128)(2,1)S(1)}, bf16[2,128,384]{2,1,0:T(8,128)(2,1)S(1)}, u32[]{:S(2)}, u32[]{:S(2)}) collective-permute-start(bf16[2,128,384]{2,1,0:T(8,128)(2,1)S(1)} %get-tuple-element.32), channel_id=1, source_target_pairs={{0,4},{2,6},{4,0},{6,2},{8,12},{10,14},{12,8},{14,10},{1,5},{3,7},... | collective-permute-start | bytes 589832 | tf_op jit(solution)/shard_map/ppermute | solution.py:323
  23.9 2.0 %bias_rows.2._.a_ref = f32[16,64]{1,0:T(8,128)S(1)} custom-call(bf16[64,128,512]{2,1,0:T(8,128)(2,1)S(1)} %load_cholesky.3.refs_2_.chol_ref.refs_3_, f32[1,64]{1,0:T(1,128)S(1)} %get-tuple-element.54.noise_ref, bf16[1,128,384]{2,1,0:T(8,128)(2,1)S(1)} %collective-permute-done.4.refs_0_, bf16[1,128,384]{2,1,0:T(8,128)(2,1)S(1)} %collective-permute-done.5.refs_1_, ...), custom_call_target="tpu_custom_call" | custom-call | tf_op jit(solution)/shard_map/bias_rows/pallas_call | solution.py:191
  27.4 2.3 %load_cholesky.4.refs_0_.refs_4_ = bf16[64,128,256]{2,1,0:T(8,128)(2,1)S(1)} custom-call(bf16[64,128,1024]{2,1,0:T(8,128)(2,1)} %chol_ref.5, f32[16,64]{1,0:T(8,128)S(1)} %bias_rows.2._.a_ref), custom_call_target="tpu_custom_call" | custom-call | tf_op jit(solution)/shard_map/load_cholesky/pallas_call | solution.py:128
  29.7 1.5 %collective-permute-start.9 = (f32[16,64]{1,0:T(8,128)S(1)}, f32[16,64]{1,0:T(8,128)S(1)}, u32[]{:S(2)}, u32[]{:S(2)}) collective-permute-start(f32[16,64]{1,0:T(8,128)S(1)} %plus.4._.a_ref), channel_id=1, source_target_pairs={{0,4},{2,6},{4,0},{6,2},{8,12},{10,14},{12,8},{14,10},{1,5},{3,7},... | collective-permute-start | bytes 12296 | tf_op jit(solution)/shard_map/ppermute | solution.py:323
  31.2 2.3 %load_cholesky.5.refs_0_.refs_5_ = bf16[64,128,256]{2,1,0:T(8,128)(2,1)S(1)} custom-call(bf16[64,128,1024]{2,1,0:T(8,128)(2,1)} %chol_ref.5, f32[16,64]{1,0:T(8,128)S(1)} %plus.4._.a_ref), custom_call_target="tpu_custom_call" | custom-call | tf_op jit(solution)/shard_map/load_cholesky/pallas_call | solution.py:128
  35.5 7.3 %collective-permute-done.10.refs_1_ = f32[16,64]{1,0:T(8,128)S(1)} collective-permute-done((f32[16,64]{1,0:T(8,128)S(1)}, f32[16,64]{1,0:T(8,128)S(1)}, u32[]{:S(2)}, u32[]{:S(2)}) %collective-permute-start.10) | collective-permute-done | bytes 4128 | tf_op jit(solution)/shard_map/ppermute | solution.py:441
  42.8 3.0 %potential_rows.2 = (bf16[1,128,1024]{2,1,0:T(8,128)(2,1)S(1)}, bf16[2,128,1024]{2,1,0:T(8,128)(2,1)S(1)}, bf16[2,128,1024]{2,1,0:T(8,128)(2,1)S(1)}, bf16[2,128...) custom-call(f32[16,64]{1,0:T(8,128)S(1)} %plus.5.refs_0_, ...), custom_call_target="tpu_custom_call" | custom-call | tf_op jit(solution)/shard_map/potential_rows/pallas_call | solution.py:243
  46.1 3.0 %collective-permute-start.25 = (bf16[2,128,1024]{2,1,0:T(8,128)(2,1)S(1)}, bf16[2,128,1024]{2,1,0:T(8,128)(2,1)S(1)}, u32[]{:S(2)}, u32[]{:S(2)}) collective-permute-start(bf16[2,128,1024]{2,1,0:T(8,128)(2,1)S(1)} %get-tuple-element.50), channel_id=1, source_target_pairs={{0,8},{2,10},{4,12},{6,14},{8,0},{10,2},{12,4},{14,6},{1,9},{3,11}... | collective-permute-start | bytes 1572872 | tf_op jit(solution)/shard_map/ppermute | solution.py:323
  50.5 2.2 %collective-permute-start.12 = (bf16[4,128,384]{2,1,0:T(8,128)(2,1)S(1)}, bf16[4,128,384]{2,1,0:T(8,128)(2,1)S(1)}, u32[]{:S(2)}, u32[]{:S(2)}) collective-permute-start(bf16[4,128,384]{2,1,0:T(8,128)(2,1)S(1)} %join.4), channel_id=1, source_target_pairs={{0,2},{2,0},{4,6},{6,4},{8,10},{10,8},{12,14},{14,12},{1,3},{3,1},... | collective-permute-start | bytes 1179656 | tf_op jit(solution)/shard_map/ppermute | solution.py:323
  52.7 5.8 %collective-permute-done.12.refs_4_ = bf16[4,128,384]{2,1,0:T(8,128)(2,1)S(1)} collective-permute-done((bf16[4,128,384]{2,1,0:T(8,128)(2,1)S(1)}, bf16[4,128,384]{2,1,0:T(8,128)(2,1)S(1)}, u32[]{:S(2)}, u32[]{:S(2)}) %collective-permute-start.12) | collective-permute-done | bytes 393248 | tf_op jit(solution)/shard_map/ppermute | solution.py:323
  58.5 2.0 %bias_rows.3.a_ref.refs_7_ = f32[16,64]{1,0:T(8,128)S(1)} custom-call(bf16[64,128,512]{2,1,0:T(8,128)(2,1)S(1)} %load_cholesky.3.refs_2_.chol_ref.refs_3_, f32[1,64]{1,0:T(1,128)S(1)} %get-tuple-element.55.noise_ref, bf16[1,128,384]{2,1,0:T(8,128)(2,1)S(1)} %get-tuple-element.31.refs_0_, bf16[2,128,384]{2,1,0:T(8,128)(2,1)S(1)} %collective-permute-done.1.refs_2_.refs_1_, ...), custom_call_target="tpu_custom_call" | custom-call | tf_op jit(solution)/shard_map/bias_rows/pallas_call | solution.py:191
  60.5 2.1 %collective-permute-start.13 = (f32[16,64]{1,0:T(8,128)S(1)}, f32[16,64]{1,0:T(8,128)S(1)}, u32[]{:S(2)}, u32[]{:S(2)}) collective-permute-start(f32[16,64]{1,0:T(8,128)S(1)} %bias_rows.3.a_ref.refs_7_), channel_id=1, source_target_pairs={{0,2},{2,0},{4,6},{6,4},{8,10},{10,8},{12,14},{14,12},{1,3},{3,1},... | collective-permute-start | bytes 12296 | tf_op jit(solution)/shard_map/ppermute | solution.py:323
  62.6 1.6 %collective-permute-done.13.b_ref = f32[16,64]{1,0:T(8,128)S(1)} collective-permute-done((f32[16,64]{1,0:T(8,128)S(1)}, f32[16,64]{1,0:T(8,128)S(1)}, u32[]{:S(2)}, u32[]{:S(2)}) %collective-permute-start.13) | collective-permute-done | bytes 4128 | tf_op jit(solution)/shard_map/ppermute | solution.py:323
  68.5 10.0 %collective-permute-done.14.b_ref = f32[16,64]{1,0:T(8,128)S(1)} collective-permute-done((f32[16,64]{1,0:T(8,128)S(1)}, f32[16,64]{1,0:T(8,128)S(1)}, u32[]{:S(2)}, u32[]{:S(2)}) %collective-permute-start.14) | collective-permute-done | bytes 4128 | tf_op jit(solution)/shard_map/ppermute | solution.py:323
  79.2 1.5 %collective-permute-start.15 = (f32[16,64]{1,0:T(8,128)S(1)}, f32[16,64]{1,0:T(8,128)S(1)}, u32[]{:S(2)}, u32[]{:S(2)}) collective-permute-start(f32[16,64]{1,0:T(8,128)S(1)} %plus.7.refs_0_), channel_id=1, source_target_pairs={{0,8},{12,4},{1,9},{13,5},{2,10},{14,6},{3,11},{15,7},{16,24},{28,... | collective-permute-start | bytes 12296 | tf_op jit(solution)/shard_map/ppermute | solution.py:441
  80.7 5.1 %collective-permute-done.15.refs_1_ = f32[16,64]{1,0:T(8,128)S(1)} collective-permute-done((f32[16,64]{1,0:T(8,128)S(1)}, f32[16,64]{1,0:T(8,128)S(1)}, u32[]{:S(2)}, u32[]{:S(2)}) %collective-permute-start.15) | collective-permute-done | bytes 4128 | tf_op jit(solution)/shard_map/ppermute | solution.py:441
  85.8 3.7 %potential_rows.3 = (bf16[1,128,1024]{2,1,0:T(8,128)(2,1)S(1)}, bf16[1,128,1024]{2,1,0:T(8,128)(2,1)S(1)}, bf16[1,128,1024]{2,1,0:T(8,128)(2,1)S(1)}, bf16[1,128...) custom-call(f32[16,64]{1,0:T(8,128)S(1)} %plus.7.refs_0_, ...), custom_call_target="tpu_custom_call" | custom-call | tf_op jit(solution)/shard_map/potential_rows/pallas_call | solution.py:243
  89.5 7.9 %collective-permute-done.26.refs_0_.refs_3_ = bf16[2,128,1024]{2,1,0:T(8,128)(2,1)S(1)} collective-permute-done((bf16[2,128,1024]{2,1,0:T(8,128)(2,1)S(1)}, bf16[2,128,1024]{2,1,0:T(8,128)(2,1)S(1)}, u32[]{:S(2)}, u32[]{:S(2)}) %collective-permute-start.26) | collective-permute-done | bytes 524320 | tf_op jit(solution)/shard_map/ppermute | solution.py:323
  97.9 3.9 %collective-permute-start.18 = (bf16[1,128,1024]{2,1,0:T(8,128)(2,1)S(1)}, bf16[1,128,1024]{2,1,0:T(8,128)(2,1)S(1)}, u32[]{:S(2)}, u32[]{:S(2)}) collective-permute-start(bf16[1,128,1024]{2,1,0:T(8,128)(2,1)S(1)} %get-tuple-element.41), channel_id=1, source_target_pairs={{0,4},{2,6},{4,0},{6,2},{8,12},{10,14},{12,8},{14,10},{1,5},{3,7},... | collective-permute-start | bytes 786440 | tf_op jit(solution)/shard_map/ppermute | solution.py:323
  103.7 12.2 %collective-permute-done.17.refs_0_ = bf16[1,128,1024]{2,1,0:T(8,128)(2,1)S(1)} collective-permute-done((bf16[1,128,1024]{2,1,0:T(8,128)(2,1)S(1)}, bf16[1,128,1024]{2,1,0:T(8,128)(2,1)S(1)}, u32[]{:S(2)}, u32[]{:S(2)}) %collective-permute-start.17) | collective-permute-done | bytes 262176 | tf_op jit(solution)/shard_map/ppermute | solution.py:323
  116.6 2.4 %collective-permute-start.22 = (bf16[1,128,1024]{2,1,0:T(8,128)(2,1)S(1)}, bf16[1,128,1024]{2,1,0:T(8,128)(2,1)S(1)}, u32[]{:S(2)}, u32[]{:S(2)}) collective-permute-start(bf16[1,128,1024]{2,1,0:T(8,128)(2,1)S(1)} %get-tuple-element.45), channel_id=1, source_target_pairs={{0,14},{2,12},{4,10},{6,8},{8,6},{10,4},{12,2},{14,0},{1,15},{3,13... | collective-permute-start | bytes 786440 | tf_op jit(solution)/shard_map/ppermute | solution.py:323
  119.1 9.1 %collective-permute-done.27.refs_4_ = bf16[4,128,1024]{2,1,0:T(8,128)(2,1)S(1)} collective-permute-done((bf16[4,128,1024]{2,1,0:T(8,128)(2,1)S(1)}, bf16[4,128,1024]{2,1,0:T(8,128)(2,1)S(1)}, u32[]{:S(2)}, u32[]{:S(2)}) %collective-permute-start.27) | collective-permute-done | bytes 1048608 | tf_op jit(solution)/shard_map/ppermute | solution.py:323
  128.4 4.6 %taylor.2.refs_9_ = bf16[2,1024,384]{2,1,0:T(8,128)(2,1)} custom-call(bf16[1,128,1024]{2,1,0:T(8,128)(2,1)S(1)} %get-tuple-element.48.refs_0_, bf16[2,128,1024]{2,1,0:T(8,128)(2,1)S(1)} %collective-permute-done.24.refs_2_.refs_1_, bf16[2,128,1024]{2,1,0:T(8,128)(2,1)S(1)} %collective-permute-done.25.refs_1_.refs_2_, ...), custom_call_target="tpu_custom_call" | custom-call | tf_op jit(solution)/shard_map/taylor/pallas_call | solution.py:300
  134.3 3.7 %collective-permute-done.22.refs_5_ = bf16[1,128,1024]{2,1,0:T(8,128)(2,1)S(1)} collective-permute-done((bf16[1,128,1024]{2,1,0:T(8,128)(2,1)S(1)}, bf16[1,128,1024]{2,1,0:T(8,128)(2,1)S(1)}, u32[]{:S(2)}, u32[]{:S(2)}) %collective-permute-start.22) | collective-permute-done | bytes 262176 | tf_op jit(solution)/shard_map/ppermute | solution.py:323
  138.0 4.7 %taylor.3 = bf16[2,1024,384]{2,1,0:T(8,128)(2,1)} custom-call(bf16[1,128,1024]{2,1,0:T(8,128)(2,1)S(1)} %collective-permute-done.17.refs_0_, bf16[1,128,1024]{2,1,0:T(8,128)(2,1)S(1)} %collective-permute-done.18.refs_1_, bf16[1,128,1024]{2,1,0:T(8,128)(2,1)S(1)} %collective-permute-done.19.refs_2_, ...), custom_call_target="tpu_custom_call", output_to_operand_aliasing={{}: (9, {})} | custom-call | tf_op jit(solution)/shard_map/taylor/pallas_call | solution.py:300
  (51 shorter events, 21.7 us)
Async XLA Ops:
  2.2 11.9 %collective-permute-start = (bf16[2,128,384]{2,1,0:T(8,128)(2,1)S(1)}, bf16[2,128,384]{2,1,0:T(8,128)(2,1)S(1)}, u32[]{:S(2)}, u32[]{:S(2)}) collective-permute-start(bf16[2,128,384]{2,1,0:T(8,128)(2,1)S(1)} %get-tuple-element.30), channel_id=1, source_target_pairs={{0,8},{2,10},{4,12},{6,14},{8,0},{10,2},{12,4},{14,6},{1,9},{3,11}... | collective-permute-start | bytes 589832 | tf_op jit(solution)/shard_map/ppermute | solution.py:323
  4.9 10.5 %collective-permute-start.6 = (bf16[2,128,384]{2,1,0:T(8,128)(2,1)S(1)}, bf16[2,128,384]{2,1,0:T(8,128)(2,1)S(1)}, u32[]{:S(2)}, u32[]{:S(2)}) collective-permute-start(bf16[2,128,384]{2,1,0:T(8,128)(2,1)S(1)} %get-tuple-element.28._), channel_id=1, source_target_pairs={{0,4},{2,6},{4,0},{6,2},{8,12},{10,14},{12,8},{14,10},{1,5},{3,7},... | collective-permute-start | bytes 589832 | tf_op jit(solution)/shard_map/ppermute | solution.py:323
  6.9 14.9 %collective-permute-start.5 = (bf16[1,128,384]{2,1,0:T(8,128)(2,1)S(1)}, bf16[1,128,384]{2,1,0:T(8,128)(2,1)S(1)}, u32[]{:S(2)}, u32[]{:S(2)}) collective-permute-start(bf16[1,128,384]{2,1,0:T(8,128)(2,1)S(1)} %get-tuple-element.35), channel_id=1, source_target_pairs={{0,14},{2,12},{4,10},{6,8},{8,6},{10,4},{12,2},{14,0},{1,15},{3,13... | collective-permute-start | bytes 294920 | tf_op jit(solution)/shard_map/ppermute | solution.py:323
  8.3 14.7 %collective-permute-start.4 = (bf16[1,128,384]{2,1,0:T(8,128)(2,1)S(1)}, bf16[1,128,384]{2,1,0:T(8,128)(2,1)S(1)}, u32[]{:S(2)}, u32[]{:S(2)}) collective-permute-start(bf16[1,128,384]{2,1,0:T(8,128)(2,1)S(1)} %get-tuple-element.29._), channel_id=1, source_target_pairs={{0,12},{2,14},{4,8},{6,10},{8,4},{10,6},{12,0},{14,2},{1,13},{3,15... | collective-permute-start | bytes 294920 | tf_op jit(solution)/shard_map/ppermute | solution.py:323
  15.3 1.8 %copy-start.1 = (s32[2,64]{1,0:T(2,128)S(1)}, s32[2,64]{1,0:T(2,128)}, u32[]{:S(2)}) copy-start(s32[2,64]{1,0:T(2,128)} %param.6) | copy-start | bytes 1540
  15.6 8.3 %collective-permute-start.7 = (bf16[3,128,384]{2,1,0:T(8,128)(2,1)S(1)}, bf16[3,128,384]{2,1,0:T(8,128)(2,1)S(1)}, u32[]{:S(2)}, u32[]{:S(2)}) collective-permute-start(bf16[3,128,384]{2,1,0:T(8,128)(2,1)S(1)} %join.3), channel_id=1, source_target_pairs={{0,2},{2,0},{4,6},{6,4},{8,10},{10,8},{12,14},{14,12},{1,3},{3,1},... | collective-permute-start | bytes 884744 | tf_op jit(solution)/shard_map/ppermute | solution.py:323
  19.2 30.3 %collective-permute-start.1 = (bf16[2,128,384]{2,1,0:T(8,128)(2,1)S(1)}, bf16[2,128,384]{2,1,0:T(8,128)(2,1)S(1)}, u32[]{:S(2)}, u32[]{:S(2)}) collective-permute-start(bf16[2,128,384]{2,1,0:T(8,128)(2,1)S(1)} %get-tuple-element.32), channel_id=1, source_target_pairs={{0,4},{2,6},{4,0},{6,2},{8,12},{10,14},{12,8},{14,10},{1,5},{3,7},... | collective-permute-start | bytes 589832 | tf_op jit(solution)/shard_map/ppermute | solution.py:323
  20.6 14.9 %collective-permute-start.2 = (bf16[2,128,384]{2,1,0:T(8,128)(2,1)S(1)}, bf16[2,128,384]{2,1,0:T(8,128)(2,1)S(1)}, u32[]{:S(2)}, u32[]{:S(2)}) collective-permute-start(bf16[2,128,384]{2,1,0:T(8,128)(2,1)S(1)} %get-tuple-element.33), channel_id=1, source_target_pairs={{0,8},{2,10},{4,12},{6,14},{8,0},{10,2},{12,4},{14,6},{1,9},{3,11}... | collective-permute-start | bytes 589832 | tf_op jit(solution)/shard_map/ppermute | solution.py:323
  21.7 27.7 %collective-permute-start.3 = (bf16[2,128,384]{2,1,0:T(8,128)(2,1)S(1)}, bf16[2,128,384]{2,1,0:T(8,128)(2,1)S(1)}, u32[]{:S(2)}, u32[]{:S(2)}) collective-permute-start(bf16[2,128,384]{2,1,0:T(8,128)(2,1)S(1)} %get-tuple-element.34), channel_id=1, source_target_pairs={{0,12},{2,14},{4,8},{6,10},{8,4},{10,6},{12,0},{14,2},{1,13},{3,15... | collective-permute-start | bytes 589832 | tf_op jit(solution)/shard_map/ppermute | solution.py:323
  26.0 3.7 %collective-permute-start.8 = (f32[16,64]{1,0:T(8,128)S(1)}, f32[16,64]{1,0:T(8,128)S(1)}, u32[]{:S(2)}, u32[]{:S(2)}) collective-permute-start(f32[16,64]{1,0:T(8,128)S(1)} %bias_rows.2._.a_ref), channel_id=1, source_target_pairs={{0,2},{2,0},{4,6},{6,4},{8,10},{10,8},{12,14},{14,12},{1,3},{3,1},... | collective-permute-start | bytes 12296 | tf_op jit(solution)/shard_map/ppermute | solution.py:323
  29.7 3.8 %collective-permute-start.9 = (f32[16,64]{1,0:T(8,128)S(1)}, f32[16,64]{1,0:T(8,128)S(1)}, u32[]{:S(2)}, u32[]{:S(2)}) collective-permute-start(f32[16,64]{1,0:T(8,128)S(1)} %plus.4._.a_ref), channel_id=1, source_target_pairs={{0,4},{2,6},{4,0},{6,2},{8,12},{10,14},{12,8},{14,10},{1,5},{3,7},... | collective-permute-start | bytes 12296 | tf_op jit(solution)/shard_map/ppermute | solution.py:323
  33.5 2.0 %collective-permute-start.11 = (f32[16,64]{1,0:T(8,128)S(1)}, f32[16,64]{1,0:T(8,128)S(1)}, u32[]{:S(2)}, u32[]{:S(2)}) collective-permute-start(f32[16,64]{1,0:T(8,128)S(1)} %plus.5.refs_0_), channel_id=1, source_target_pairs={{0,12},{12,0},{1,13},{13,1},{2,14},{14,2},{3,15},{15,3},{16,28},{2... | collective-permute-start | bytes 12296 | tf_op jit(solution)/shard_map/ppermute | solution.py:441
  34.2 8.6 %collective-permute-start.10 = (f32[16,64]{1,0:T(8,128)S(1)}, f32[16,64]{1,0:T(8,128)S(1)}, u32[]{:S(2)}, u32[]{:S(2)}) collective-permute-start(f32[16,64]{1,0:T(8,128)S(1)} %plus.5.refs_0_), channel_id=1, source_target_pairs={{0,8},{12,4},{1,9},{13,5},{2,10},{14,6},{3,11},{15,7},{16,24},{28,... | collective-permute-start | bytes 12296 | tf_op jit(solution)/shard_map/ppermute | solution.py:441
  45.9 43.6 %collective-permute-start.24 = (bf16[2,128,1024]{2,1,0:T(8,128)(2,1)S(1)}, bf16[2,128,1024]{2,1,0:T(8,128)(2,1)S(1)}, u32[]{:S(2)}, u32[]{:S(2)}) collective-permute-start(bf16[2,128,1024]{2,1,0:T(8,128)(2,1)S(1)} %get-tuple-element.49), channel_id=1, source_target_pairs={{0,4},{2,6},{4,0},{6,2},{8,12},{10,14},{12,8},{14,10},{1,5},{3,7},... | collective-permute-start | bytes 1572872 | tf_op jit(solution)/shard_map/ppermute | solution.py:323
  46.1 43.4 %collective-permute-start.25 = (bf16[2,128,1024]{2,1,0:T(8,128)(2,1)S(1)}, bf16[2,128,1024]{2,1,0:T(8,128)(2,1)S(1)}, u32[]{:S(2)}, u32[]{:S(2)}) collective-permute-start(bf16[2,128,1024]{2,1,0:T(8,128)(2,1)S(1)} %get-tuple-element.50), channel_id=1, source_target_pairs={{0,8},{2,10},{4,12},{6,14},{8,0},{10,2},{12,4},{14,6},{1,9},{3,11}... | collective-permute-start | bytes 1572872 | tf_op jit(solution)/shard_map/ppermute | solution.py:323
  49.1 48.3 %collective-permute-start.26 = (bf16[2,128,1024]{2,1,0:T(8,128)(2,1)S(1)}, bf16[2,128,1024]{2,1,0:T(8,128)(2,1)S(1)}, u32[]{:S(2)}, u32[]{:S(2)}) collective-permute-start(bf16[2,128,1024]{2,1,0:T(8,128)(2,1)S(1)} %get-tuple-element.51), channel_id=1, source_target_pairs={{0,12},{2,14},{4,8},{6,10},{8,4},{10,6},{12,0},{14,2},{1,13},{3,15... | collective-permute-start | bytes 1572872 | tf_op jit(solution)/shard_map/ppermute | solution.py:323
  50.5 8.0 %collective-permute-start.12 = (bf16[4,128,384]{2,1,0:T(8,128)(2,1)S(1)}, bf16[4,128,384]{2,1,0:T(8,128)(2,1)S(1)}, u32[]{:S(2)}, u32[]{:S(2)}) collective-permute-start(bf16[4,128,384]{2,1,0:T(8,128)(2,1)S(1)} %join.4), channel_id=1, source_target_pairs={{0,2},{2,0},{4,6},{6,4},{8,10},{10,8},{12,14},{14,12},{1,3},{3,1},... | collective-permute-start | bytes 1179656 | tf_op jit(solution)/shard_map/ppermute | solution.py:323
  60.5 3.7 %collective-permute-start.13 = (f32[16,64]{1,0:T(8,128)S(1)}, f32[16,64]{1,0:T(8,128)S(1)}, u32[]{:S(2)}, u32[]{:S(2)}) collective-permute-start(f32[16,64]{1,0:T(8,128)S(1)} %bias_rows.3.a_ref.refs_7_), channel_id=1, source_target_pairs={{0,2},{2,0},{4,6},{6,4},{8,10},{10,8},{12,14},{14,12},{1,3},{3,1},... | collective-permute-start | bytes 12296 | tf_op jit(solution)/shard_map/ppermute | solution.py:323
  64.2 14.3 %collective-permute-start.14 = (f32[16,64]{1,0:T(8,128)S(1)}, f32[16,64]{1,0:T(8,128)S(1)}, u32[]{:S(2)}, u32[]{:S(2)}) collective-permute-start(f32[16,64]{1,0:T(8,128)S(1)} %plus.6._.a_ref), channel_id=1, source_target_pairs={{0,4},{2,6},{4,0},{6,2},{8,12},{10,14},{12,8},{14,10},{1,5},{3,7},... | collective-permute-start | bytes 12296 | tf_op jit(solution)/shard_map/ppermute | solution.py:323
  78.6 2.1 %collective-permute-start.16 = (f32[16,64]{1,0:T(8,128)S(1)}, f32[16,64]{1,0:T(8,128)S(1)}, u32[]{:S(2)}, u32[]{:S(2)}) collective-permute-start(f32[16,64]{1,0:T(8,128)S(1)} %plus.7.refs_0_), channel_id=1, source_target_pairs={{0,12},{12,0},{1,13},{13,1},{2,14},{14,2},{3,15},{15,3},{16,28},{2... | collective-permute-start | bytes 12296 | tf_op jit(solution)/shard_map/ppermute | solution.py:441
  79.2 6.6 %collective-permute-start.15 = (f32[16,64]{1,0:T(8,128)S(1)}, f32[16,64]{1,0:T(8,128)S(1)}, u32[]{:S(2)}, u32[]{:S(2)}) collective-permute-start(f32[16,64]{1,0:T(8,128)S(1)} %plus.7.refs_0_), channel_id=1, source_target_pairs={{0,8},{12,4},{1,9},{13,5},{2,10},{14,6},{3,11},{15,7},{16,24},{28,... | collective-permute-start | bytes 12296 | tf_op jit(solution)/shard_map/ppermute | solution.py:441
  97.5 30.7 %collective-permute-start.27 = (bf16[4,128,1024]{2,1,0:T(8,128)(2,1)S(1)}, bf16[4,128,1024]{2,1,0:T(8,128)(2,1)S(1)}, u32[]{:S(2)}, u32[]{:S(2)}) collective-permute-start(bf16[4,128,1024]{2,1,0:T(8,128)(2,1)S(1)} %join.5), channel_id=1, source_target_pairs={{0,2},{2,0},{4,6},{6,4},{8,10},{10,8},{12,14},{14,12},{1,3},{3,1},... | collective-permute-start | bytes 3145736 | tf_op jit(solution)/shard_map/ppermute | solution.py:323
  97.9 18.0 %collective-permute-start.17 = (bf16[1,128,1024]{2,1,0:T(8,128)(2,1)S(1)}, bf16[1,128,1024]{2,1,0:T(8,128)(2,1)S(1)}, u32[]{:S(2)}, u32[]{:S(2)}) collective-permute-start(bf16[1,128,1024]{2,1,0:T(8,128)(2,1)S(1)} %get-tuple-element.40), channel_id=1, source_target_pairs={{0,8},{2,10},{4,12},{6,14},{8,0},{10,2},{12,4},{14,6},{1,9},{3,11}... | collective-permute-start | bytes 786440 | tf_op jit(solution)/shard_map/ppermute | solution.py:323
  97.9 18.8 %collective-permute-start.18 = (bf16[1,128,1024]{2,1,0:T(8,128)(2,1)S(1)}, bf16[1,128,1024]{2,1,0:T(8,128)(2,1)S(1)}, u32[]{:S(2)}, u32[]{:S(2)}) collective-permute-start(bf16[1,128,1024]{2,1,0:T(8,128)(2,1)S(1)} %get-tuple-element.41), channel_id=1, source_target_pairs={{0,4},{2,6},{4,0},{6,2},{8,12},{10,14},{12,8},{14,10},{1,5},{3,7},... | collective-permute-start | bytes 786440 | tf_op jit(solution)/shard_map/ppermute | solution.py:323
  101.8 31.2 %collective-permute-start.19 = (bf16[1,128,1024]{2,1,0:T(8,128)(2,1)S(1)}, bf16[1,128,1024]{2,1,0:T(8,128)(2,1)S(1)}, u32[]{:S(2)}, u32[]{:S(2)}) collective-permute-start(bf16[1,128,1024]{2,1,0:T(8,128)(2,1)S(1)} %get-tuple-element.42), channel_id=1, source_target_pairs={{0,6},{2,4},{4,2},{6,0},{8,14},{10,12},{12,10},{14,8},{1,7},{3,5},... | collective-permute-start | bytes 786440 | tf_op jit(solution)/shard_map/ppermute | solution.py:323
  103.0 30.0 %collective-permute-start.20 = (bf16[1,128,1024]{2,1,0:T(8,128)(2,1)S(1)}, bf16[1,128,1024]{2,1,0:T(8,128)(2,1)S(1)}, u32[]{:S(2)}, u32[]{:S(2)}) collective-permute-start(bf16[1,128,1024]{2,1,0:T(8,128)(2,1)S(1)} %get-tuple-element.43), channel_id=1, source_target_pairs={{0,10},{2,8},{4,14},{6,12},{8,2},{10,0},{12,6},{14,4},{1,11},{3,9}... | collective-permute-start | bytes 786440 | tf_op jit(solution)/shard_map/ppermute | solution.py:323
  115.9 18.3 %collective-permute-start.21 = (bf16[1,128,1024]{2,1,0:T(8,128)(2,1)S(1)}, bf16[1,128,1024]{2,1,0:T(8,128)(2,1)S(1)}, u32[]{:S(2)}, u32[]{:S(2)}) collective-permute-start(bf16[1,128,1024]{2,1,0:T(8,128)(2,1)S(1)} %get-tuple-element.44), channel_id=1, source_target_pairs={{0,12},{2,14},{4,8},{6,10},{8,4},{10,6},{12,0},{14,2},{1,13},{3,15... | collective-permute-start | bytes 786440 | tf_op jit(solution)/shard_map/ppermute | solution.py:323
  116.6 21.4 %collective-permute-start.22 = (bf16[1,128,1024]{2,1,0:T(8,128)(2,1)S(1)}, bf16[1,128,1024]{2,1,0:T(8,128)(2,1)S(1)}, u32[]{:S(2)}, u32[]{:S(2)}) collective-permute-start(bf16[1,128,1024]{2,1,0:T(8,128)(2,1)S(1)} %get-tuple-element.45), channel_id=1, source_target_pairs={{0,14},{2,12},{4,10},{6,8},{8,6},{10,4},{12,2},{14,0},{1,15},{3,13... | collective-permute-start | bytes 786440 | tf_op jit(solution)/shard_map/ppermute | solution.py:323
  128.2 9.8 %collective-permute-start.23 = (bf16[1,128,1024]{2,1,0:T(8,128)(2,1)S(1)}, bf16[1,128,1024]{2,1,0:T(8,128)(2,1)S(1)}, u32[]{:S(2)}, u32[]{:S(2)}) collective-permute-start(bf16[1,128,1024]{2,1,0:T(8,128)(2,1)S(1)} %get-tuple-element.47), channel_id=1, source_target_pairs={{0,2},{2,0},{4,6},{6,4},{8,10},{10,8},{12,14},{14,12},{1,3},{3,1},... | collective-permute-start | bytes 786440 | tf_op jit(solution)/shard_map/ppermute | solution.py:323
  128.4 9.6 %copy-start = (bf16[2,1024,384]{2,1,0:T(8,128)(2,1)S(1)}, bf16[2,1024,384]{2,1,0:T(8,128)(2,1)}, u32[]{:S(2)}) copy-start(bf16[2,1024,384]{2,1,0:T(8,128)(2,1)} %refs_10_.1) | copy-start | bytes 4718596
